TPU v7x, 32 devices: a whole 2x2x4 slice. The times are simulated.
32 devices in a mesh: row: 4 (over z), col: 8 (over y, x, core).
Axes of the slice: x: 2, y: 2, z: 4, core: 2. Of those that a mesh axis runs over, the one named last changes fastest.
Arguments:
- h_values: float32 [4, 64, 4096], P('row', 'col'), as said below
- h_places: int32 [4, 64], P('row', 'col'), may hold values from 0 to 7, as said below
- h_counts: int32 [4, 8], P('row', 'col'), may hold values from 0 to 8, as said below
- p_values: float32 [4, 64, 4096], P('row', 'col'), as said below
- p_places: int32 [4, 64], P('row', 'col'), may hold values from 0 to 7, as said below
- p_counts: int32 [4, 8], P('row', 'col'), may hold values from 0 to 8, as said below
- s_values: float32 [4, 64, 4096], P('row', 'col'), as said below
- s_places: int32 [4, 64], P('row', 'col'), may hold values from 0 to 7, as said below
- s_counts: int32 [4, 8], P('row', 'col'), may hold values from 0 to 8, as said below
- x_places: int32 [4, 64], P('row', 'col'), may hold values from 0 to 7, as said below
- x_counts: int32 [4, 8], P('row', 'col'), may hold values from 0 to 8, as said below
Outputs:
- gradient: float32 [4, 64, 4096], P('row', 'col')
Inputs may be any that keep to these rules, and one draw needn't show every extreme that they name: `h_places`: in each tile the 8 entries are a permutation of the tile's positions; the first count entries are the present blocks. Every pattern is symmetric, holds every block whose block row and block column lie in the same row panel, and every block (i, j) whose cyclic block distance min(|i - j|, 16 - |i - j|) is 2 or less or exactly 8. `p_places`: as for h_places. `s_places`: as for h_places. `x_places`: as for h_places. `h_counts`: every tile whose block columns lie in its own row panel is full. `p_counts`: as for h_counts. `s_counts`: as for h_counts. `x_counts`: as for h_counts. `h_values`: the assembled H is symmetric. `p_values`: the assembled P is symmetric. `s_values`: the assembled S is symmetric.
All inputs are finite; a program needn't handle non-finite values.
Results may differ from a plain program's by a relative error of at most 0.000088.
Values sent between devices are 32-bit elements; how exact they have to be, the bound alone decides.
No kernel may reach another device: no remote copies, remote signals or barrier semaphores. Data moves between devices by JAX's collectives and lax.ppermute only.
A program may use at most 64 MiB of HBM per device.

v0:
```python
import jax
import jax.numpy as jnp
from jax import lax
from jax.sharding import PartitionSpec as P

BS = 64
TC = 2


def from_root(value, axis, source):
    kept = jnp.where(lax.axis_index(axis) == source, value, 0).astype(value.dtype)
    return lax.psum(kept, axis)


def assemble(values, places, counts):
    blocks_in = values[0]
    capacity = blocks_in.shape[0]
    slot_ids = lax.iota(jnp.int32, capacity)
    matches = (places[0][:, None] == slot_ids[None, :]) & (slot_ids[:, None] < counts[0, 0])
    spread = jnp.dot(matches.astype(jnp.float32).T, blocks_in, precision=lax.Precision.HIGHEST)
    row_count = capacity // TC
    return (
        spread.reshape(row_count, TC, BS, BS).transpose(0, 2, 1, 3).reshape(row_count * BS, TC * BS)
    )


def expand_mask(present, row_count, col_count):
    flags = present.reshape(row_count, col_count)
    return jnp.broadcast_to(flags[:, None, :, None], (row_count, BS, col_count, BS)).reshape(
        row_count * BS, col_count * BS
    )


def tile_mask(places, counts):
    capacity = places.shape[1]
    slot_ids = lax.iota(jnp.int32, capacity)
    matches = (places[0][:, None] == slot_ids[None, :]) & (slot_ids[:, None] < counts[0, 0])
    present = jnp.sum(matches.astype(jnp.float32), axis=0)
    return expand_mask(present, capacity // TC, TC)


def tile_to_slots(tile, places, counts):
    row_count = tile.shape[0] // BS
    blocks = (
        tile.reshape(row_count, BS, TC, BS).transpose(0, 2, 1, 3).reshape(row_count * TC, BS * BS)
    )
    picked = jnp.take(blocks, places[0], axis=0)
    slot_ids = lax.iota(jnp.int32, places.shape[1])
    used = (slot_ids < counts[0, 0]).astype(jnp.float32)
    return (picked * used[:, None])[None]


def shards(
    h_values,
    h_places,
    h_counts,
    p_values,
    p_places,
    p_counts,
    s_values,
    s_places,
    s_counts,
    x_places,
    x_counts,
):
    col_index = lax.axis_index("col")
    h_tile = assemble(h_values, h_places, h_counts)
    p_tile = assemble(p_values, p_places, p_counts)
    s_tile = assemble(s_values, s_places, s_counts)
    mask_tile = tile_mask(x_places, x_counts)
    row_width = h_tile.shape[0]
    col_width = h_tile.shape[1]
    p_columns, s_columns = (
        lax.all_gather(p_tile, "row", axis=0, tiled=True),
        lax.all_gather(s_tile, "row", axis=0, tiled=True),
    )
    product = jnp.dot(
        lax.all_gather(h_tile, "col", axis=1, tiled=True),
        p_columns,
        precision=lax.Precision.HIGHEST,
    )
    y_tile = mask_tile * product
    y_panel = lax.all_gather(y_tile, "col", axis=1, tiled=True)
    x_tile = mask_tile * jnp.dot(y_panel, s_columns, precision=lax.Precision.HIGHEST)
    per_panel = row_width // col_width
    source_row = col_index // per_panel
    offset = col_index % per_panel * col_width
    x_panel = lax.all_gather(x_tile, "col", axis=1, tiled=True)
    x_part = lax.dynamic_slice_in_dim(x_panel, offset, col_width, 0)
    x_mirror = from_root(x_part, "row", source_row)
    row_anchor = lax.axis_index("row") * row_width
    mirrored = lax.dynamic_slice_in_dim(x_mirror, row_anchor, row_width, 1).T
    return tile_to_slots(x_tile + mirrored, x_places, x_counts)


def solution(mesh):
    in_specs = (
        P("row", "col", None),
        P("row", "col"),
        P("row", "col"),
        P("row", "col", None),
        P("row", "col"),
        P("row", "col"),
        P("row", "col", None),
        P("row", "col"),
        P("row", "col"),
        P("row", "col"),
        P("row", "col"),
    )
    out_specs = P("row", "col", None)
    return jax.shard_map(shards, mesh=mesh, in_specs=in_specs, out_specs=out_specs, check_vma=False)
```

profile of v0, /device:TPU:2, one launch (start us, length us, event | category | flops | bytes accessed | tf_op | source)
XLA Modules:
  0.0 138.3 jit_solution(12831709009330923796)
XLA Ops:
  6.5 1.0 dot_general.28
  8.2 0.6 copy-done.2
  8.9 0.4 convolution_bitcast_fusion.2
  9.5 0.8 reshape.189
  11.1 0.6 copy-done.5
  12.3 0.7 copy-done
  13.8 0.6 copy-done.3
  14.4 0.4 convolution_bitcast_fusion.1
  15.2 15.9 %all_gather.16 = f32[1024,128]{1,0:T(8,128)S(1)} all-gather(f32[256,128]{1,0:T(8,128)S(1)} %reshape.190), channel_id=1, replica_groups=mesh['row'=4,'col'=8] {'row'}, dimensions={0}, use_global_device_ids=true | all-gather | bytes 655360 | tf_op jit(solution)/shard_map/all_gather | solution.py:74
  31.1 4.2 %all-gather.4.cloned.1.call-done = f32[256,1024]{1,0:T(8,128)} async-done(((f32[256,128]{1,0:T(8,128)}), f32[256,1024]{1,0:T(8,128)}) %all-gather.4.cloned.1.call-update) | async-done | bytes 1048592 | tf_op jit(solution)/shard_map/all_gather | solution.py:78
  35.4 2.9 %convolution_multiply_fusion.1 = f32[256,128]{1,0:T(8,128)} fusion(f32[256,128]{1,0:T(8,128)S(1)} %reshape.188, f32[256,1024]{1,0:T(8,128)} %all-gather.4.cloned.1.call-done, f32[1024,128]{1,0:T(8,128)S(1)} %all_gather.16), kind=kOutput, calls=%fused_computation.5 | convolution fusion | flops 402685952 | bytes 1835008 | tf_op jit(solution)/shard_map/dot_general | solution.py:77
  38.3 0.8 copy-done.1
  39.9 0.6 copy-done.4
  40.6 0.4 convolution_bitcast_fusion
  41.4 16.0 %all_gather.18 = f32[1024,128]{1,0:T(8,128)S(1)} all-gather(f32[256,128]{1,0:T(8,128)S(1)} %reshape.191), channel_id=1, replica_groups=mesh['row'=4,'col'=8] {'row'}, dimensions={0}, use_global_device_ids=true | all-gather | bytes 655360 | tf_op jit(solution)/shard_map/all_gather | solution.py:75
  57.4 4.6 %all-gather.6.cloned.1.call-done = f32[256,1024]{1,0:T(8,128)} async-done(((f32[256,128]{1,0:T(8,128)}), f32[256,1024]{1,0:T(8,128)}) %all-gather.6.cloned.1.call-update) | async-done | bytes 1048592 | tf_op jit(solution)/shard_map/all_gather | solution.py:83
  62.0 2.2 %convolution_multiply_fusion = f32[256,128]{1,0:T(8,128)S(1)} fusion(f32[256,128]{1,0:T(8,128)S(1)} %reshape.188, f32[256,1024]{1,0:T(8,128)} %all-gather.6.cloned.1.call-done, f32[1024,128]{1,0:T(8,128)S(1)} %all_gather.18), kind=kOutput, calls=%fused_computation.4 | convolution fusion | flops 402685952 | bytes 1835008 | tf_op jit(solution)/shard_map/dot_general | solution.py:84
  64.2 0.8 copy.31
  65.1 23.6 %all-gather.8.cloned.1.call-done = f32[256,1024]{0,1:T(8,128)} async-done(((f32[256,128]{0,1:T(8,128)}), f32[256,1024]{0,1:T(8,128)}) %all-gather.8.cloned.1.call-update) | async-done | bytes 1048592 | tf_op jit(solution)/shard_map/all_gather | solution.py:88
  88.6 1.9 %dynamic-slice_select_fusion = f32[128,1024]{0,1:T(8,128)} fusion(f32[256,1024]{0,1:T(8,128)} %all-gather.8.cloned.1.call-done, s32[]{:T(128)S(6)} %select_n.56, pred[]{:T(512)S(6)} %eq.125), kind=kLoop, calls=%fused_computation.6 | loop fusion | flops 131072 | bytes 1048581 | tf_op jit(solution)/shard_map/jit(_where)/select_n | solution.py:11
  90.6 38.6 %all-reduce.2.cloned.1.call-done = f32[128,1024]{0,1:T(8,128)} async-done(((f32[128,1024]{0,1:T(8,128)}), f32[128,1024]{0,1:T(8,128)}) %all-reduce.2.cloned.1.call-update) | async-done | bytes 524304 | tf_op jit(solution)/shard_map/psum | solution.py:12
  129.1 0.9 bitcast_add_fusion
  130.4 0.6 gather_fusion
  131.0 0.7 fusion.6
  (36 shorter events, 2.3 us)
Async XLA Ops:
  6.5 28.8 %all-gather.4.cloned.1.call-start = ((), (), s32[]{:S(2)}) async-start(), calls=%async_computation | async-start | bytes 1179648 | tf_op jit(solution)/shard_map/all_gather | solution.py:78
  8.2 0.7 copy-start.2
  10.4 51.6 %all-gather.6.cloned.1.call-start = ((), (), s32[]{:S(2)}) async-start(), calls=%async_computation.1 | async-start | bytes 1179648 | tf_op jit(solution)/shard_map/all_gather | solution.py:83
  11.1 0.7 copy-start.5
  12.1 0.9 copy-start
  13.7 0.7 copy-start.3
  38.2 0.9 copy-start.1
  38.3 50.4 %all-gather.8.cloned.1.call-start = ((), (), s32[]{:S(2)}) async-start(), calls=%async_computation.2 | async-start | bytes 1179648 | tf_op jit(solution)/shard_map/all_gather | solution.py:88
  39.9 0.7 copy-start.4
  65.0 64.2 %all-reduce.2.cloned.1.call-start = ((), (), s32[]{:S(2)}) async-start(), calls=%async_computation.3 | async-start | bytes 1048576 | tf_op jit(solution)/shard_map/psum | solution.py:12
Sparse Core Ops, SparseCore 0:
  10.5 24.8 all-gather.3
  38.4 23.5 all-gather.5
  65.1 23.4 all-gather.7
  90.8 38.2 all-reduce.1
where the time goes:
time: 140 us; the launch traced here: 138 us
  waiting for transfers between devices  71 us (51%)
  blocking collectives  31.9 us (23%)
  between operations  15.9 us (11%)
  local copies, waits for them, and re-layouts  9.26 us (7%)
  matrix products  6.34 us (5%)
  other arithmetic  3.7 us (3%)
    psum x1, waiting for transfers between devices, from_root(): return lax.psum(kept, axis)  38.6 us
    all_gather x1, waiting for transfers between devices, shards(): x_panel = lax.all_gather(x_tile, 'col', axis=1, tiled=True)  23.6 us
    all_gather x1, blocking collectives, shards(): lax.all_gather(s_tile, 'row', axis=0, tiled=True)  16 us
    all_gather x1, blocking collectives, shards(): lax.all_gather(p_tile, 'row', axis=0, tiled=True)  15.9 us
    all_gather x1, waiting for transfers between devices, shards(): y_panel = lax.all_gather(y_tile, 'col', axis=1, tiled=True)  4.55 us
    all_gather x1, waiting for transfers between devices, shards(): lax.all_gather(h_tile, 'col', axis=1, tiled=True)  4.24 us
    unnamed x12, local copies, waits for them, and re-layouts  4.14 us
    dot_general x1, matrix products, shards(): jnp.dot(lax.all_gather(h_tile, 'col', axis=1, tiled=True), p_columns, pre...  2.87 us
  transfers between devices with their start and end apart: 4, of which 4 were waited for; matrix products, arithmetic and copies ran while one was open for 2% of the time, Pallas kernels for 0%

commit v1 on v0

v1 whole, which is shorter than its diff:
```python
import functools

import jax
import jax.numpy as jnp
from jax import lax
from jax.experimental import pallas as pl
from jax.experimental.pallas import tpu as pltpu
from jax.sharding import PartitionSpec as P

BS = 64
LANES = 128
PAIR = 2 * LANES
LINES = BS * BS // LANES
VMEM = pl.BlockSpec(memory_space=pltpu.VMEM)
SMEM = pl.BlockSpec(memory_space=pltpu.SMEM)
AXES = ("row", "col")


def position():
    col = lax.axis_index("col")
    return lax.axis_index("row"), col // 2, col % 2


def left_lanes(rows):
    return lax.broadcasted_iota(jnp.int32, (rows, LANES), 1) < BS


def invert(places, inverse, base):
    cap = places.shape[1]
    for slot in range(cap):
        inverse[base + places[0, slot]] = slot


def assemble_kernel(*refs):
    values, places, counts = refs[0:3], refs[3:7], refs[7:11]
    out, lines, inverse = refs[11:]
    cap = values[0].shape[1]
    rows = cap * LINES
    left = left_lanes(LINES)
    for which in range(4):
        invert(places[which], inverse, which * cap)
    for which in range(3):
        for line in range(LINES):
            lines[which, pl.ds(line, cap, stride=LINES), :] = values[which][
                0, :, line * LANES : (line + 1) * LANES
            ]
        count = counts[which][0, 0]

        def block(place):
            slot = inverse[which * cap + place]
            kept = (slot < count).astype(jnp.float32)
            start = pl.multiple_of(slot * LINES, LINES)
            return lines[which, pl.ds(start, LINES), :] * kept

        for pair in range(cap // 2):
            first, second = block(2 * pair), block(2 * pair + 1)
            even = jnp.where(left, first, pltpu.roll(second, BS, 1))
            odd = jnp.where(left, pltpu.roll(first, BS, 1), second)
            start = which * rows + pair * BS
            out[pl.ds(start, LINES, stride=2), :] = even
            out[pl.ds(start + 1, LINES, stride=2), :] = odd
    count = counts[3][0, 0]
    for pair in range(cap // 2):
        flags = [
            (inverse[3 * cap + 2 * pair + side] < count).astype(jnp.float32) for side in range(2)
        ]
        out[3 * rows + pair : 3 * rows + pair + 1, :] = jnp.where(
            left_lanes(1), flags[0], flags[1]
        )


def pack_kernel(rows, combos, own, other, *outs):
    _, _, core = position()
    for k in range(2):

        @pl.when(core == k)
        def _():
            halves = (own, other) if k == 0 else (other, own)
            for combo, out in zip(combos, outs):
                start = "HPS".index(combo[k]) * rows
                for side in range(2):
                    out[:, side * LANES : (side + 1) * LANES] = halves[side][
                        start : start + rows, :
                    ]


def split(x):
    high = x.astype(jnp.bfloat16)
    return high, (x - high.astype(jnp.float32)).astype(jnp.bfloat16)


def dot3(a, b_high, b_low):
    a_high, a_low = split(a)
    dot = functools.partial(jnp.dot, preferred_element_type=jnp.float32)
    return dot(a_high, b_high) + (dot(a_high, b_low) + dot(a_low, b_high))


def store_split(high, low, start, rows, x, columns=slice(None)):
    h, l = split(x)
    high[pl.ds(start, rows), columns] = h
    low[pl.ds(start, rows), columns] = l


def masked(acc, halves, rows, k):
    count = acc.shape[0] // BS
    lines = []
    for line in range(count):
        at = 3 * rows + k * count + line
        row = jnp.concatenate([half[at : at + 1, :] for half in halves], axis=1)
        lines.append(acc[line * BS : (line + 1) * BS, :] * row)
    return jnp.concatenate(lines, axis=0)


def y_kernel(rows, ops, own, other, *refs):
    count = len(ops)
    got, shared = refs[:count], refs[count : 2 * count]
    out, high, low = refs[2 * count :]
    row, chip, core = position()
    half = rows // 2
    for k in range(2):

        @pl.when(core == k)
        def _():
            halves = (own, other) if k == 0 else (other, own)
            start = pl.multiple_of(row * rows, rows)
            for side in range(2):
                store_split(
                    high,
                    low,
                    start,
                    rows,
                    halves[side][rows : 2 * rows, :],
                    slice(side * LANES, (side + 1) * LANES),
                )
            pieces = []
            for i, op in enumerate(ops):
                for holder in range(2):
                    item = op[holder]
                    ref = got[i] if holder == k else shared[i]
                    if item is None or item[0] == "S":
                        continue
                    if item[0] == "P":
                        start = pl.multiple_of((row ^ item[1]) * rows, rows)
                        store_split(high, low, start, rows, ref[...])
                    else:
                        pieces.append((item[1], ref))
            mine = slice(k * half, (k + 1) * half)
            a = jnp.concatenate([ref[mine, :] for ref in halves], axis=1)
            at = pl.ds(pl.multiple_of(chip * PAIR, PAIR), PAIR)
            acc = dot3(a, high[at, :], low[at, :])
            for offset, ref in pieces:
                at = pl.ds(pl.multiple_of((chip ^ offset) * PAIR, PAIR), PAIR)
                acc += dot3(ref[mine, :], high[at, :], low[at, :])
            out[...] = masked(acc, halves, rows, k)


def x_kernel(rows, ops, offsets, parts, own, other, *refs):
    count = len(ops)
    got, shared = refs[:count], refs[count : 2 * count]
    y_refs = refs[2 * count : 2 * count + len(offsets)]
    out, swap = refs[2 * count + len(offsets) :][:2]
    sent = refs[2 * count + len(offsets) + 2 : -2]
    high, low = refs[-2:]
    row, chip, core = position()
    half = rows // 2
    for k in range(2):

        @pl.when(core == k)
        def _():
            halves = (own, other) if k == 0 else (other, own)
            start = pl.multiple_of(row * rows, rows)
            for side in range(2):
                store_split(
                    high,
                    low,
                    start,
                    rows,
                    halves[side][2 * rows : 3 * rows, :],
                    slice(side * LANES, (side + 1) * LANES),
                )
            for i, op in enumerate(ops):
                for holder in range(2):
                    item = op[holder]
                    ref = got[i] if holder == k else shared[i]
                    if item is not None and item[0] == "S":
                        start = pl.multiple_of((row ^ item[1]) * rows, rows)
                        store_split(high, low, start, rows, ref[...])
            acc = jnp.zeros((half, PAIR), jnp.float32)
            for offset, ref in zip(offsets, y_refs):
                at = pl.ds(pl.multiple_of((chip ^ offset) * PAIR, PAIR), PAIR)
                acc += dot3(ref[...], high[at, :], low[at, :])
            x = masked(acc, halves, rows, k)
            out[...] = x
            swap[...] = x[:, (1 - k) * LANES : (2 - k) * LANES]
    for turn, ref in enumerate(sent):
        part = (chip % parts + turn) % parts
        ref[...] = out[pl.ds(pl.multiple_of(part * LANES, LANES), LANES), :]


def slots_kernel(parts, places, counts, x, swapped, *refs):
    mirrors = refs[:parts]
    out, tile, lines, inverse = refs[parts:]
    _, _, core = position()
    cap = places.shape[1]
    half = x.shape[0]
    invert(places, inverse, 0)
    for k in range(2):

        @pl.when(core == k)
        def _():
            tile[k * half : (k + 1) * half, :] = x[:, k * LANES : (k + 1) * LANES]
            tile[(1 - k) * half : (2 - k) * half, :] = swapped[...]

    for turn in range(parts):
        col = lax.axis_index("col")
        at = ((col % parts) - turn + parts) % parts
        at = pl.ds(pl.multiple_of(at * PAIR, PAIR), PAIR)
        tile[at, :] += mirrors[turn][...].T
    count = counts[0, 0]
    left = left_lanes(LINES)
    for pair in range(cap // 2):
        even = tile[pl.ds(pair * BS, LINES, stride=2), :]
        odd = tile[pl.ds(pair * BS + 1, LINES, stride=2), :]
        blocks = (
            jnp.where(left, even, pltpu.roll(odd, BS, 1)),
            jnp.where(left, pltpu.roll(even, BS, 1), odd),
        )
        for side in range(2):
            slot = inverse[2 * pair + side]
            used = (slot < count).astype(jnp.float32)
            start = pl.multiple_of(slot * LINES, LINES)
            lines[pl.ds(start, LINES), :] = blocks[side] * used
    for line in range(LINES):
        out[0, :, line * LANES : (line + 1) * LANES] = lines[
            pl.ds(line, cap, stride=LINES), :
        ]


def call(kernel, out_shapes, in_specs, scratch, cost, *args):
    single = not isinstance(out_shapes, list)
    return pl.pallas_call(
        kernel,
        out_shape=out_shapes,
        in_specs=in_specs,
        out_specs=VMEM if single else [VMEM] * len(out_shapes),
        scratch_shapes=scratch,
        compiler_params=pltpu.CompilerParams(vmem_limit_bytes=32 * 1024 * 1024),
        cost_estimate=pl.CostEstimate(flops=cost, bytes_accessed=1 << 20, transcendentals=0),
    )(*args)


def queues(row_count, chip_count):
    along = sorted(range(1, row_count), key=lambda s: (s != 2, -s))
    across = list(range(chip_count - 1, 0, -1))
    first = [("H", o) for o in across]
    second = [("P", s) for s in along]
    for s in along:
        (first if len(first) < len(second) else second).append(("S", s))
    steps = max(len(first), len(second))
    first += [None] * (steps - len(first))
    second += [None] * (steps - len(second))
    return list(zip(first, second))


def shards(row_count, chip_count, hv, hp, hc, pv, pp, pc, sv, sp, sc, xp, xc):
    cap = hp.shape[1]
    rows = cap * LINES
    half = rows // 2
    order = row_count * rows
    parts = chip_count // row_count
    mask_rows = max(8, cap // 2)
    f32 = jnp.float32

    def device(r, m, k):
        return (r * chip_count + m) * 2 + k

    places = [
        (r, m, k) for r in range(row_count) for m in range(chip_count) for k in range(2)
    ]

    def send(value, target):
        pairs = []
        for r, m, k in places:
            to = target(r, m, k)
            if to is not None:
                pairs.append((device(r, m, k), device(*to)))
        return lax.ppermute(value, AXES, pairs)

    def to_other(value):
        return send(value, lambda r, m, k: (r, m, 1 - k))

    tiles = call(
        assemble_kernel,
        jax.ShapeDtypeStruct((3 * rows + mask_rows, LANES), f32),
        [VMEM] * 3 + [SMEM] * 8,
        [pltpu.VMEM((3, rows, LANES), f32), pltpu.SMEM((4 * cap,), jnp.int32)],
        1 << 20,
        hv, pv, sv, hp, pp, sp, xp, hc, pc, sc, xc,
    )
    other = to_other(tiles)
    ops = queues(row_count, chip_count)
    kinds = [tuple((item or op[1 - k])[0] for k, item in enumerate(op)) for op in ops]
    combos = sorted(set(kinds))
    packed = call(
        functools.partial(pack_kernel, rows, combos),
        [jax.ShapeDtypeStruct((rows, PAIR), f32) for _ in combos],
        [VMEM] * 2,
        [],
        1 << 20,
        tiles, other,
    )
    got, shared = [], []
    for op, kind in zip(ops, kinds):

        def target(r, m, k):
            if op[k] is None:
                return None
            matrix, offset = op[k]
            return (r, m ^ offset, k) if matrix == "H" else (r ^ offset, m, k)

        got.append(send(packed[combos.index(kind)], target))
        shared.append(to_other(got[-1]))

    def holding(matrices):
        return [i for i, op in enumerate(ops) if any(x and x[0] in matrices for x in op)]

    flops = 2 * 3 * half * order * PAIR
    splits = [pltpu.VMEM((order, PAIR), jnp.bfloat16)] * 2
    used = holding("HP")
    y = call(
        functools.partial(y_kernel, rows, [ops[i] for i in used]),
        jax.ShapeDtypeStruct((half, PAIR), f32),
        [VMEM] * (2 + 2 * len(used)),
        splits,
        flops,
        tiles, other, *[got[i] for i in used], *[shared[i] for i in used],
    )
    offsets = list(range(chip_count - 1, -1, -1))
    ys = [
        send(y, lambda r, m, k, o=o: (r, m ^ o, k)) if o else y
        for o in offsets
    ]
    used = holding("S")
    sent_shapes = [jax.ShapeDtypeStruct((LANES, PAIR), f32)] * (parts if parts > 1 else 0)
    x, swap, *sent = call(
        functools.partial(x_kernel, rows, [ops[i] for i in used], offsets, parts),
        [jax.ShapeDtypeStruct((half, PAIR), f32), jax.ShapeDtypeStruct((half, LANES), f32)]
        + sent_shapes,
        [VMEM] * (2 + 2 * len(used) + len(offsets)),
        splits,
        flops,
        tiles, other, *[got[i] for i in used], *[shared[i] for i in used], *ys,
    )
    sent = sent or [x]

    def mirror(turn):
        def target(r, m, k):
            part = (m % parts + turn) % parts
            column = (r * 2 * parts) + k * parts + part
            return m // parts, column // 2, column % 2

        return target

    mirrors = [send(value, mirror(turn)) for turn, value in enumerate(sent)]
    swapped = to_other(swap)
    return call(
        functools.partial(slots_kernel, parts),
        jax.ShapeDtypeStruct((1, cap, BS * BS), f32),
        [SMEM] * 2 + [VMEM] * (2 + parts),
        [
            pltpu.VMEM((rows, LANES), f32),
            pltpu.VMEM((rows, LANES), f32),
            pltpu.SMEM((cap,), jnp.int32),
        ],
        1 << 20,
        xp, xc, x, swapped, *mirrors,
    )


def solution(mesh):
    values, ints = P("row", "col", None), P("row", "col")
    row_count, col_count = mesh.shape["row"], mesh.shape["col"]
    return jax.shard_map(
        functools.partial(shards, row_count, col_count // 2),
        mesh=mesh,
        in_specs=(values, ints, ints) * 3 + (ints, ints),
        out_specs=values,
        check_vma=False,
    )
```

time: 140 us -> 62.1 us (0.44); the launches traced: 138 us -> 61.8 us
  waiting for transfers between devices: 71 us -> 20.7 us
  blocking collectives: 31.9 us -> 0 us
  starting transfers between devices: 0.13 us -> 32 us
  between operations: 15.9 us -> 2.81 us
  local copies, waits for them, and re-layouts: 9.26 us -> 2.72 us
  matrix products: 6.34 us -> 0 us
  other arithmetic: 3.7 us -> 0 us
  Pallas kernels: 0 us -> 3.68 us
    psum x1 -> x0, waiting for transfers between devices: 38.6 us -> none  [from_root(): return lax.psum(kept, axis)]
    all_gather x3 -> x0, waiting for transfers between devices: 32.3 us -> none  [the longest x1 23.6 us: shards(): x_panel = lax.all_gather(x_tile, 'col', axis=1, tiled=True)]
    ppermute x0 -> x16, starting transfers between devices: none -> 32 us  [send(): return lax.ppermute(value, AXES, pairs)]
    all_gather x2 -> x0, blocking collectives: 31.9 us -> none  [the longest x1 16 us: shards(): lax.all_gather(s_tile, 'row', axis=0, tiled=True)]
    ppermute x0 -> x16, waiting for transfers between devices: none -> 20.7 us  [send(): return lax.ppermute(value, AXES, pairs)]
    dot_general x5 -> x0, matrix products: 6.34 us -> none  [the longest x1 2.87 us: shards(): jnp.dot(lax.all_gather(h_tile, 'col', axis=1, tiled=True), p_columns, pre...]
    pallas_call x0 -> x5, Pallas kernels: none -> 3.68 us  [call(): pl.pallas_call(kernel, out_shape=out_shapes, in_specs=in_specs, out_specs...]
    select_n x2 -> x0, other arithmetic: 1.91 us -> none  [the longest x1 1.91 us: from_root(): jnp.where(lax.axis_index(axis) == source, value, 0).astype(value.dtype)]
  transfers between devices with their start and end apart: 4 -> 16, of which waited for: 4 -> 7; matrix products, arithmetic and copies ran while one was open for 2% -> 0% of each run, Pallas kernels for 0% -> 1%
where the time goes in v1:
time: 62.1 us; the launch traced here: 61.8 us
  starting transfers between devices  32 us (52%)
  waiting for transfers between devices  20.7 us (33%)
  Pallas kernels  3.68 us (6%)
  between operations  2.81 us (5%)
  local copies, waits for them, and re-layouts  2.72 us (4%)
    ppermute x16, starting transfers between devices, send(): return lax.ppermute(value, AXES, pairs)  32 us
    ppermute x16, waiting for transfers between devices, send(): return lax.ppermute(value, AXES, pairs)  20.7 us
    pallas_call x5, Pallas kernels, call(): pl.pallas_call(kernel, out_shape=out_shapes, in_specs=in_specs, out_specs...  3.68 us
    unnamed x14, local copies, waits for them, and re-layouts  2.72 us
  transfers between devices with their start and end apart: 16, of which 7 were waited for; matrix products, arithmetic and copies ran while one was open for 0% of the time, Pallas kernels for 1%

profile of v1, /device:TPU:2, one launch (start us, length us, event | category | flops | bytes accessed | tf_op | source)
XLA Modules:
  0.0 61.8 jit_solution(12146059517373090583)
XLA Ops:
  2.7 0.9 %copy-done = f32[1,8,4096]{2,1,0:T(8,128)S(1)} copy-done((f32[1,8,4096]{2,1,0:T(8,128)S(1)}, f32[1,8,4096]{2,1,0:T(8,128)}, u32[]{:S(2)}) %copy-start) | copy-done | bytes 131096
  3.6 0.9 %copy-done.1 = f32[1,8,4096]{2,1,0:T(8,128)S(1)} copy-done((f32[1,8,4096]{2,1,0:T(8,128)S(1)}, f32[1,8,4096]{2,1,0:T(8,128)}, u32[]{:S(2)}) %copy-start.1) | copy-done | bytes 131096
  4.5 0.9 %copy-done.2 = f32[1,8,4096]{2,1,0:T(8,128)S(1)} copy-done((f32[1,8,4096]{2,1,0:T(8,128)S(1)}, f32[1,8,4096]{2,1,0:T(8,128)}, u32[]{:S(2)}) %copy-start.2) | copy-done | bytes 131096
  5.4 1.0 %shard_map.109.own = f32[776,128]{1,0:T(8,128)S(1)} custom-call(f32[1,8,4096]{2,1,0:T(8,128)S(1)} %copy-done, f32[1,8,4096]{2,1,0:T(8,128)S(1)} %copy-done.1, f32[1,8,4096]{2,1,0:T(8,128)S(1)} %copy-done.2, s32[1,8]{1,0:T(1,128)S(1)} %copy-done.4, s32[1,8]{1,0:T(1,128)S(1)} %copy-done.5, s32[1,8]{1,0:T(1,128)S(1)} %copy-done.6, s32[1,8]{1,0:T(1,128)S(1)} %copy-done.3, ...), custom_call_target="tpu_custom_call" | custom-call | flops 1048576 | bytes 1048576 | tf_op jit(solution)/shard_map/pallas_call | solution.py:241
  6.5 1.7 %collective-permute-done.other = f32[776,128]{1,0:T(8,128)S(1)} collective-permute-done((f32[776,128]{1,0:T(8,128)S(1)}, f32[776,128]{1,0:T(8,128)S(1)}, u32[]{:S(2)}, u32[]{:S(2)}) %collective-permute-start) | collective-permute-done | bytes 397344 | tf_op jit(solution)/shard_map/ppermute | solution.py:287
  8.3 3.0 %collective-permute-start.5 = (f32[256,256]{1,0:T(8,128)S(1)}, f32[256,256]{1,0:T(8,128)S(1)}, u32[]{:S(2)}, u32[]{:S(2)}) collective-permute-start(f32[256,256]{1,0:T(8,128)S(1)} %get-tuple-element.10), channel_id=1, source_target_pairs={{0,6},{1,17},{2,4},{3,19},{4,2},{5,21},{6,0},{7,23},{8,14},{9,25},... | collective-permute-start | bytes 786440 | tf_op jit(solution)/shard_map/ppermute | solution.py:287
  11.3 0.5 collective-permute-start.6
  11.8 3.6 %collective-permute-start.1 = (f32[256,256]{1,0:T(8,128)S(1)}, f32[256,256]{1,0:T(8,128)S(1)}, u32[]{:S(2)}, u32[]{:S(2)}) collective-permute-start(f32[256,256]{1,0:T(8,128)S(1)} %get-tuple-element.9), channel_id=1, source_target_pairs={{0,24},{1,17},{2,26},{3,19},{4,28},{5,21},{6,30},{7,23},{8,16},{9,... | collective-permute-start | bytes 786440 | tf_op jit(solution)/shard_map/ppermute | solution.py:287
  15.4 0.7 %collective-permute-start.2 = (f32[256,256]{1,0:T(8,128)S(1)}, f32[256,256]{1,0:T(8,128)S(1)}, u32[]{:S(2)}, u32[]{:S(2)}) collective-permute-start(f32[256,256]{1,0:T(8,128)S(1)} %get-tuple-element.9), channel_id=1, source_target_pairs={{1,9},{3,11},{5,13},{7,15},{9,1},{11,3},{13,5},{15,7},{17,25},{19,... | collective-permute-start | bytes 786440 | tf_op jit(solution)/shard_map/ppermute | solution.py:287
  16.1 1.5 %collective-permute-start.10 = (f32[256,256]{1,0:T(8,128)S(1)}, f32[256,256]{1,0:T(8,128)S(1)}, u32[]{:S(2)}, u32[]{:S(2)}) collective-permute-start(f32[256,256]{1,0:T(8,128)S(1)} %collective-permute-done.7.refs_2_), channel_id=1, source_target_pairs={{0,1},{1,0},{2,3},{3,2},{4,5},{5,4},{6,7},{7,6},{8,9},{9,8},{10,11... | collective-permute-start | bytes 786440 | tf_op jit(solution)/shard_map/ppermute | solution.py:287
  17.6 1.0 %collective-permute-done.5.refs_0_ = f32[256,256]{1,0:T(8,128)S(1)} collective-permute-done((f32[256,256]{1,0:T(8,128)S(1)}, f32[256,256]{1,0:T(8,128)S(1)}, u32[]{:S(2)}, u32[]{:S(2)}) %collective-permute-start.5) | collective-permute-done | bytes 262176 | tf_op jit(solution)/shard_map/ppermute | solution.py:287
  18.5 8.7 %collective-permute-start.8 = (f32[256,256]{1,0:T(8,128)S(1)}, f32[256,256]{1,0:T(8,128)S(1)}, u32[]{:S(2)}, u32[]{:S(2)}) collective-permute-start(f32[256,256]{1,0:T(8,128)S(1)} %collective-permute-done.5.refs_0_), channel_id=1, source_target_pairs={{0,1},{1,0},{2,3},{3,2},{4,5},{5,4},{6,7},{7,6},{8,9},{9,8},{10,11... | collective-permute-start | bytes 786440 | tf_op jit(solution)/shard_map/ppermute | solution.py:287
  27.2 8.4 %collective-permute-start.3 = (f32[256,256]{1,0:T(8,128)S(1)}, f32[256,256]{1,0:T(8,128)S(1)}, u32[]{:S(2)}, u32[]{:S(2)}) collective-permute-start(f32[256,256]{1,0:T(8,128)S(1)} %collective-permute-done.1.refs_0_), channel_id=1, source_target_pairs={{0,1},{1,0},{2,3},{3,2},{4,5},{5,4},{6,7},{7,6},{8,9},{9,8},{10,11... | collective-permute-start | bytes 786440 | tf_op jit(solution)/shard_map/ppermute | solution.py:287
  35.6 0.6 shard_map.111.refs_7_
  36.2 1.6 %collective-permute-start.11 = (f32[128,256]{1,0:T(8,128)S(1)}, f32[128,256]{1,0:T(8,128)S(1)}, u32[]{:S(2)}, u32[]{:S(2)}) collective-permute-start(f32[128,256]{1,0:T(8,128)S(1)} %shard_map.111.refs_7_), channel_id=1, source_target_pairs={{0,6},{1,7},{2,4},{3,5},{4,2},{5,3},{6,0},{7,1},{8,14},{9,15},{10,... | collective-permute-start | bytes 393224 | tf_op jit(solution)/shard_map/ppermute | solution.py:287
  37.8 0.5 collective-permute-start.12
  38.3 1.5 %collective-permute-start.13 = (f32[128,256]{1,0:T(8,128)S(1)}, f32[128,256]{1,0:T(8,128)S(1)}, u32[]{:S(2)}, u32[]{:S(2)}) collective-permute-start(f32[128,256]{1,0:T(8,128)S(1)} %shard_map.111.refs_7_), channel_id=1, source_target_pairs={{0,2},{1,3},{2,0},{3,1},{4,6},{5,7},{6,4},{7,5},{8,10},{9,11},{10,... | collective-permute-start | bytes 393224 | tf_op jit(solution)/shard_map/ppermute | solution.py:287
  39.8 3.7 %collective-permute-done.11.refs_4_ = f32[128,256]{1,0:T(8,128)S(1)} collective-permute-done((f32[128,256]{1,0:T(8,128)S(1)}, f32[128,256]{1,0:T(8,128)S(1)}, u32[]{:S(2)}, u32[]{:S(2)}) %collective-permute-start.11) | collective-permute-done | bytes 131104 | tf_op jit(solution)/shard_map/ppermute | solution.py:287
  43.5 2.4 %collective-permute-done.12.refs_5_ = f32[128,256]{1,0:T(8,128)S(1)} collective-permute-done((f32[128,256]{1,0:T(8,128)S(1)}, f32[128,256]{1,0:T(8,128)S(1)}, u32[]{:S(2)}, u32[]{:S(2)}) %collective-permute-start.12) | collective-permute-done | bytes 131104 | tf_op jit(solution)/shard_map/ppermute | solution.py:287
  46.0 0.6 shard_map.112
  46.6 1.9 %collective-permute-start.15 = (f32[128,256]{1,0:T(8,128)S(1)}, f32[128,256]{1,0:T(8,128)S(1)}, u32[]{:S(2)}, u32[]{:S(2)}) collective-permute-start(f32[128,256]{1,0:T(8,128)S(1)} %get-tuple-element.11.x), channel_id=1, source_target_pairs={{0,0},{1,1},{2,8},{3,9},{4,16},{5,17},{6,24},{7,25},{8,2},{9,3},{1... | collective-permute-start | bytes 393224 | tf_op jit(solution)/shard_map/ppermute | solution.py:287
  48.6 1.2 %collective-permute-done.14.swapped = f32[128,128]{1,0:T(8,128)S(1)} collective-permute-done((f32[128,128]{1,0:T(8,128)S(1)}, f32[128,128]{1,0:T(8,128)S(1)}, u32[]{:S(2)}, u32[]{:S(2)}) %collective-permute-start.14) | collective-permute-done | bytes 65568 | tf_op jit(solution)/shard_map/ppermute | solution.py:287
  49.8 10.5 %collective-permute-done.15.refs_0_ = f32[128,256]{1,0:T(8,128)S(1)} collective-permute-done((f32[128,256]{1,0:T(8,128)S(1)}, f32[128,256]{1,0:T(8,128)S(1)}, u32[]{:S(2)}, u32[]{:S(2)}) %collective-permute-start.15) | collective-permute-done | bytes 131104 | tf_op jit(solution)/shard_map/ppermute | solution.py:287
  60.3 1.5 %shard_map.113 = f32[1,8,4096]{2,1,0:T(8,128)} custom-call(s32[1,8]{1,0:T(1,128)S(1)} %copy-done.3, s32[1,1]{1,0:T(1,128)S(6)} %copy.15.refs_10_.counts, f32[128,256]{1,0:T(8,128)S(1)} %get-tuple-element.11.x, f32[128,128]{1,0:T(8,128)S(1)} %collective-permute-done.14.swapped, f32[128,256]{1,0:T(8,128)S(1)} %collective-permute-done.15.refs_0_), custom_call_target="tpu_custom_call" | custom-call | flops 1048576 | bytes 1048576 | tf_op jit(solution)/shard_map/pallas_call | solution.py:241
  (27 shorter events, 0.4 us)
Async XLA Ops:
  1.3 1.4 %copy-start.6 = (s32[1,8]{1,0:T(1,128)S(1)}, s32[1,8]{1,0:T(1,128)}, u32[]{:S(2)}) copy-start(s32[1,8]{1,0:T(1,128)} %refs_5_.1) | copy-start | bytes 100
  2.0 0.7 %copy-start.3 = (s32[1,8]{1,0:T(1,128)S(1)}, s32[1,8]{1,0:T(1,128)}, u32[]{:S(2)}) copy-start(s32[1,8]{1,0:T(1,128)} %places.1) | copy-start | bytes 100
  2.0 0.7 %copy-start.4 = (s32[1,8]{1,0:T(1,128)S(1)}, s32[1,8]{1,0:T(1,128)}, u32[]{:S(2)}) copy-start(s32[1,8]{1,0:T(1,128)} %refs_3_.1) | copy-start | bytes 100
  2.0 0.7 %copy-start.5 = (s32[1,8]{1,0:T(1,128)S(1)}, s32[1,8]{1,0:T(1,128)}, u32[]{:S(2)}) copy-start(s32[1,8]{1,0:T(1,128)} %refs_4_.1) | copy-start | bytes 100
  2.7 0.9 %copy-start = (f32[1,8,4096]{2,1,0:T(8,128)S(1)}, f32[1,8,4096]{2,1,0:T(8,128)}, u32[]{:S(2)}) copy-start(f32[1,8,4096]{2,1,0:T(8,128)} %refs_0_.1) | copy-start | bytes 393220
  3.6 0.9 %copy-start.1 = (f32[1,8,4096]{2,1,0:T(8,128)S(1)}, f32[1,8,4096]{2,1,0:T(8,128)}, u32[]{:S(2)}) copy-start(f32[1,8,4096]{2,1,0:T(8,128)} %refs_1_.1) | copy-start | bytes 393220
  4.5 0.9 %copy-start.2 = (f32[1,8,4096]{2,1,0:T(8,128)S(1)}, f32[1,8,4096]{2,1,0:T(8,128)}, u32[]{:S(2)}) copy-start(f32[1,8,4096]{2,1,0:T(8,128)} %refs_2_.1) | copy-start | bytes 393220
  6.4 1.8 %collective-permute-start = (f32[776,128]{1,0:T(8,128)S(1)}, f32[776,128]{1,0:T(8,128)S(1)}, u32[]{:S(2)}, u32[]{:S(2)}) collective-permute-start(f32[776,128]{1,0:T(8,128)S(1)} %shard_map.109.own), channel_id=1, source_target_pairs={{0,1},{1,0},{2,3},{3,2},{4,5},{5,4},{6,7},{7,6},{8,9},{9,8},{10,11... | collective-permute-start | bytes 1191944 | tf_op jit(solution)/shard_map/ppermute | solution.py:287
  8.2 7.8 %collective-permute-start.7 = (f32[256,256]{1,0:T(8,128)S(1)}, f32[256,256]{1,0:T(8,128)S(1)}, u32[]{:S(2)}, u32[]{:S(2)}) collective-permute-start(f32[256,256]{1,0:T(8,128)S(1)} %get-tuple-element.10), channel_id=1, source_target_pairs={{0,2},{1,9},{2,0},{3,11},{4,6},{5,13},{6,4},{7,15},{8,10},{9,1},{1... | collective-permute-start | bytes 786440 | tf_op jit(solution)/shard_map/ppermute | solution.py:287
  8.3 10.2 %collective-permute-start.5 = (f32[256,256]{1,0:T(8,128)S(1)}, f32[256,256]{1,0:T(8,128)S(1)}, u32[]{:S(2)}, u32[]{:S(2)}) collective-permute-start(f32[256,256]{1,0:T(8,128)S(1)} %get-tuple-element.10), channel_id=1, source_target_pairs={{0,6},{1,17},{2,4},{3,19},{4,2},{5,21},{6,0},{7,23},{8,14},{9,25},... | collective-permute-start | bytes 786440 | tf_op jit(solution)/shard_map/ppermute | solution.py:287
  11.3 15.9 %collective-permute-start.6 = (f32[256,256]{1,0:T(8,128)S(1)}, f32[256,256]{1,0:T(8,128)S(1)}, u32[]{:S(2)}, u32[]{:S(2)}) collective-permute-start(f32[256,256]{1,0:T(8,128)S(1)} %get-tuple-element.10), channel_id=1, source_target_pairs={{0,4},{1,25},{2,6},{3,27},{4,0},{5,29},{6,2},{7,31},{8,12},{9,17},... | collective-permute-start | bytes 786440 | tf_op jit(solution)/shard_map/ppermute | solution.py:287
  11.8 15.4 %collective-permute-start.1 = (f32[256,256]{1,0:T(8,128)S(1)}, f32[256,256]{1,0:T(8,128)S(1)}, u32[]{:S(2)}, u32[]{:S(2)}) collective-permute-start(f32[256,256]{1,0:T(8,128)S(1)} %get-tuple-element.9), channel_id=1, source_target_pairs={{0,24},{1,17},{2,26},{3,19},{4,28},{5,21},{6,30},{7,23},{8,16},{9,... | collective-permute-start | bytes 786440 | tf_op jit(solution)/shard_map/ppermute | solution.py:287
  15.4 20.2 %collective-permute-start.2 = (f32[256,256]{1,0:T(8,128)S(1)}, f32[256,256]{1,0:T(8,128)S(1)}, u32[]{:S(2)}, u32[]{:S(2)}) collective-permute-start(f32[256,256]{1,0:T(8,128)S(1)} %get-tuple-element.9), channel_id=1, source_target_pairs={{1,9},{3,11},{5,13},{7,15},{9,1},{11,3},{13,5},{15,7},{17,25},{19,... | collective-permute-start | bytes 786440 | tf_op jit(solution)/shard_map/ppermute | solution.py:287
  16.1 19.5 %collective-permute-start.10 = (f32[256,256]{1,0:T(8,128)S(1)}, f32[256,256]{1,0:T(8,128)S(1)}, u32[]{:S(2)}, u32[]{:S(2)}) collective-permute-start(f32[256,256]{1,0:T(8,128)S(1)} %collective-permute-done.7.refs_2_), channel_id=1, source_target_pairs={{0,1},{1,0},{2,3},{3,2},{4,5},{5,4},{6,7},{7,6},{8,9},{9,8},{10,11... | collective-permute-start | bytes 786440 | tf_op jit(solution)/shard_map/ppermute | solution.py:287
  18.5 17.1 %collective-permute-start.8 = (f32[256,256]{1,0:T(8,128)S(1)}, f32[256,256]{1,0:T(8,128)S(1)}, u32[]{:S(2)}, u32[]{:S(2)}) collective-permute-start(f32[256,256]{1,0:T(8,128)S(1)} %collective-permute-done.5.refs_0_), channel_id=1, source_target_pairs={{0,1},{1,0},{2,3},{3,2},{4,5},{5,4},{6,7},{7,6},{8,9},{9,8},{10,11... | collective-permute-start | bytes 786440 | tf_op jit(solution)/shard_map/ppermute | solution.py:287
  27.2 8.4 %collective-permute-start.9 = (f32[256,256]{1,0:T(8,128)S(1)}, f32[256,256]{1,0:T(8,128)S(1)}, u32[]{:S(2)}, u32[]{:S(2)}) collective-permute-start(f32[256,256]{1,0:T(8,128)S(1)} %collective-permute-done.6.refs_1_), channel_id=1, source_target_pairs={{0,1},{1,0},{2,3},{3,2},{4,5},{5,4},{6,7},{7,6},{8,9},{9,8},{10,11... | collective-permute-start | bytes 786440 | tf_op jit(solution)/shard_map/ppermute | solution.py:287
  27.2 12.6 %collective-permute-start.3 = (f32[256,256]{1,0:T(8,128)S(1)}, f32[256,256]{1,0:T(8,128)S(1)}, u32[]{:S(2)}, u32[]{:S(2)}) collective-permute-start(f32[256,256]{1,0:T(8,128)S(1)} %collective-permute-done.1.refs_0_), channel_id=1, source_target_pairs={{0,1},{1,0},{2,3},{3,2},{4,5},{5,4},{6,7},{7,6},{8,9},{9,8},{10,11... | collective-permute-start | bytes 786440 | tf_op jit(solution)/shard_map/ppermute | solution.py:287
  35.6 4.2 %collective-permute-start.4 = (f32[256,256]{1,0:T(8,128)S(1)}, f32[256,256]{1,0:T(8,128)S(1)}, u32[]{:S(2)}, u32[]{:S(2)}) collective-permute-start(f32[256,256]{1,0:T(8,128)S(1)} %collective-permute-done.2.refs_1_), channel_id=1, source_target_pairs={{0,1},{1,0},{2,3},{3,2},{4,5},{5,4},{6,7},{7,6},{8,9},{9,8},{10,11... | collective-permute-start | bytes 786440 | tf_op jit(solution)/shard_map/ppermute | solution.py:287
  36.2 7.3 %collective-permute-start.11 = (f32[128,256]{1,0:T(8,128)S(1)}, f32[128,256]{1,0:T(8,128)S(1)}, u32[]{:S(2)}, u32[]{:S(2)}) collective-permute-start(f32[128,256]{1,0:T(8,128)S(1)} %shard_map.111.refs_7_), channel_id=1, source_target_pairs={{0,6},{1,7},{2,4},{3,5},{4,2},{5,3},{6,0},{7,1},{8,14},{9,15},{10,... | collective-permute-start | bytes 393224 | tf_op jit(solution)/shard_map/ppermute | solution.py:287
  37.8 8.1 %collective-permute-start.12 = (f32[128,256]{1,0:T(8,128)S(1)}, f32[128,256]{1,0:T(8,128)S(1)}, u32[]{:S(2)}, u32[]{:S(2)}) collective-permute-start(f32[128,256]{1,0:T(8,128)S(1)} %shard_map.111.refs_7_), channel_id=1, source_target_pairs={{0,4},{1,5},{2,6},{3,7},{4,0},{5,1},{6,2},{7,3},{8,12},{9,13},{10,... | collective-permute-start | bytes 393224 | tf_op jit(solution)/shard_map/ppermute | solution.py:287
  38.3 7.7 %collective-permute-start.13 = (f32[128,256]{1,0:T(8,128)S(1)}, f32[128,256]{1,0:T(8,128)S(1)}, u32[]{:S(2)}, u32[]{:S(2)}) collective-permute-start(f32[128,256]{1,0:T(8,128)S(1)} %shard_map.111.refs_7_), channel_id=1, source_target_pairs={{0,2},{1,3},{2,0},{3,1},{4,6},{5,7},{6,4},{7,5},{8,10},{9,11},{10,... | collective-permute-start | bytes 393224 | tf_op jit(solution)/shard_map/ppermute | solution.py:287
  46.6 13.8 %collective-permute-start.15 = (f32[128,256]{1,0:T(8,128)S(1)}, f32[128,256]{1,0:T(8,128)S(1)}, u32[]{:S(2)}, u32[]{:S(2)}) collective-permute-start(f32[128,256]{1,0:T(8,128)S(1)} %get-tuple-element.11.x), channel_id=1, source_target_pairs={{0,0},{1,1},{2,8},{3,9},{4,16},{5,17},{6,24},{7,25},{8,2},{9,3},{1... | collective-permute-start | bytes 393224 | tf_op jit(solution)/shard_map/ppermute | solution.py:287
  48.5 1.3 %collective-permute-start.14 = (f32[128,128]{1,0:T(8,128)S(1)}, f32[128,128]{1,0:T(8,128)S(1)}, u32[]{:S(2)}, u32[]{:S(2)}) collective-permute-start(f32[128,128]{1,0:T(8,128)S(1)} %get-tuple-element.12), channel_id=1, source_target_pairs={{0,1},{1,0},{2,3},{3,2},{4,5},{5,4},{6,7},{7,6},{8,9},{9,8},{10,11... | collective-permute-start | bytes 196616 | tf_op jit(solution)/shard_map/ppermute | solution.py:287

commit v2 on v0

v2 whole, which is shorter than its diff:
```python
import functools

import jax
import jax.numpy as jnp
from jax import lax
from jax.experimental import pallas as pl
from jax.experimental.pallas import tpu as pltpu
from jax.sharding import PartitionSpec as P

BS = 64
LANES = 128
COST = 1 << 10
LINES = BS * BS // LANES
VMEM = pl.BlockSpec(memory_space=pltpu.VMEM)
SMEM = pl.BlockSpec(memory_space=pltpu.SMEM)
AXES = ("row", "col")


def position():
    col = lax.axis_index("col")
    return lax.axis_index("row"), col // 2, col % 2


def left_lanes(rows):
    return lax.broadcasted_iota(jnp.int32, (rows, LANES), 1) < BS


def invert(places, inverse, base):
    cap = places.shape[1]
    for slot in range(cap):
        inverse[base + places[0, slot]] = slot


def fill(ref, rows):
    if ref.shape[0] > rows:
        ref[rows:, :] = jnp.zeros((ref.shape[0] - rows, LANES), jnp.float32)


def assemble(values, places, counts, lines, inverse, ready, tiles):
    left = left_lanes(LINES)
    for which, value in enumerate(values):
        cap = value.shape[1]
        ready(which)
        invert(places[which], inverse, which * cap)
        count = counts[which][0, 0]
        for line in range(LINES):
            lines[which, pl.ds(line, cap, stride=LINES), :] = value[
                0, :, line * LANES : (line + 1) * LANES
            ]

        def block(place):
            slot = inverse[which * cap + place]
            kept = (slot < count).astype(jnp.float32)
            start = pl.multiple_of(slot * LINES, LINES)
            return lines[which, pl.ds(start, LINES), :] * kept

        for pair in range(cap // 2):
            first, second = block(2 * pair), block(2 * pair + 1)
            even = jnp.where(left, first, pltpu.roll(second, BS, 1))
            odd = jnp.where(left, pltpu.roll(first, BS, 1), second)
            for tile in tiles[which]:
                tile[pl.ds(pair * BS, LINES, stride=2), :] = even
                tile[pl.ds(pair * BS + 1, LINES, stride=2), :] = odd
        for tile in tiles[which]:
            fill(tile, cap * LINES)


def first_kernel(value, places, count, near, far, value_in, places_in, lines, inverse, sems):
    copies = [
        pltpu.make_async_copy(places, places_in, sems.at[0]),
        pltpu.make_async_copy(value, value_in, sems.at[1]),
    ]
    for copy in copies:
        copy.start()

    def ready(_):
        for copy in copies:
            copy.wait()

    assemble([value_in], [places_in], [count], lines, inverse, ready, [(near, far)])


def rest_kernel(*refs):
    sources, counts, (h_tile, s_near, s_far, mask, order) = refs[:5], refs[5:8], refs[9:14]
    values, places = refs[14:16], refs[16:19]
    lines, inverse, sems = refs[19:]
    copies = [
        pltpu.make_async_copy(source, ref, sems.at[i])
        for i, (source, ref) in enumerate(zip(sources, refs[14:19]))
    ]
    for copy in copies:
        copy.start()
    cap = values[0].shape[1]

    def ready(which):
        copies[which].wait()
        copies[2 + which].wait()

    assemble(values, places, counts, lines, inverse, ready, [(h_tile,), (s_near, s_far)])
    copies[4].wait()
    invert(places[2], inverse, 2 * cap)
    count = counts[2][0, 0]
    slots = [inverse[2 * cap + place] for place in range(cap)]
    lanes = lax.broadcasted_iota(jnp.int32, (1, LANES), 1)
    row = jnp.where(lanes == cap, count, 0)
    for place in range(cap):
        row = jnp.where(lanes == place, slots[place], row)
    order[...] = row
    for pair in range(cap // 2):
        flags = [(slots[2 * pair + side] < count).astype(jnp.float32) for side in range(2)]
        mask[pair : pair + 1, :] = jnp.where(left_lanes(1), flags[0], flags[1])


def stack_kernel(others, count, rows, *refs):
    for i, ref in enumerate(refs[others : others + count]):
        refs[-1][i * rows : (i + 1) * rows, :] = ref[:rows, :]


def split(x):
    high = x.astype(jnp.bfloat16)
    return high, (x - high.astype(jnp.float32)).astype(jnp.bfloat16)


def dot3(a, b_high, b_low):
    a_high, a_low = split(a)
    dot = functools.partial(jnp.dot, preferred_element_type=jnp.float32)
    return dot(a_high, b_high) + (dot(a_high, b_low) + dot(a_low, b_high))


def product_kernel(along, across, sends, *refs):
    got, shared, b_own = refs[:3]
    b_got = refs[3 : 3 + len(along)]
    mask, out = refs[3 + len(along) :][:2]
    sent = refs[5 + len(along) : -2]
    high, low = refs[-2:]
    row, chip, core = position()
    rows = b_own.shape[0]
    for offset, ref in zip([0] + along, (b_own,) + b_got):
        at = pl.ds(pl.multiple_of((row ^ offset) * rows, rows), rows)
        high[at, :], low[at, :] = split(ref[:rows, :])
    acc = None
    for i, offset in enumerate([0] + across):
        for side in range(2):
            ref = (got, shared)[side]
            start = i * rows
            column = 2 * (chip ^ offset) + (core ^ side)
            at = pl.ds(pl.multiple_of(column * LANES, LANES), LANES)
            term = dot3(ref[start : start + rows, :], high[at, :], low[at, :])
            acc = term if acc is None else acc + term
    for pair in range(rows // BS):
        at = slice(pair * BS, (pair + 1) * BS)
        out[at, :] = acc[at, :] * mask[pair : pair + 1, :]
    fill(out, rows)
    for turn, ref in enumerate(sent):
        part = lax.rem(2 * chip + core + turn, sends)
        ref[...] = out[pl.ds(pl.multiple_of(part * LANES, LANES), LANES), :]


def slots_kernel(cap, order, x, *refs):
    mirrors, (out, tile, lines) = refs[:-3], refs[-3:]
    sends = len(mirrors)
    tile[...] = x[: tile.shape[0], :]
    for turn in range(sends):
        part = lax.rem(lax.axis_index("col") + (sends - turn), sends)
        at = pl.ds(pl.multiple_of(part * LANES, LANES), LANES)
        tile[at, :] += mirrors[turn][...].T
    count = order[0, cap]
    left = left_lanes(LINES)
    for pair in range(cap // 2):
        even = tile[pl.ds(pair * BS, LINES, stride=2), :]
        odd = tile[pl.ds(pair * BS + 1, LINES, stride=2), :]
        blocks = (
            jnp.where(left, even, pltpu.roll(odd, BS, 1)),
            jnp.where(left, pltpu.roll(even, BS, 1), odd),
        )
        for side in range(2):
            slot = order[0, 2 * pair + side]
            used = (slot < count).astype(jnp.float32)
            start = pl.multiple_of(slot * LINES, LINES)
            lines[pl.ds(start, LINES), :] = blocks[side] * used
    for line in range(LINES):
        out[0, :, line * LANES : (line + 1) * LANES] = lines[
            pl.ds(line, cap, stride=LINES), :
        ]


def call(kernel, out_shapes, in_specs, scratch, cost, *args):
    single = not isinstance(out_shapes, list)
    return pl.pallas_call(
        kernel,
        out_shape=out_shapes,
        in_specs=in_specs,
        out_specs=VMEM if single else [VMEM] * len(out_shapes),
        scratch_shapes=scratch,
        compiler_params=pltpu.CompilerParams(vmem_limit_bytes=32 * 1024 * 1024),
        cost_estimate=pl.CostEstimate(flops=COST, bytes_accessed=COST, transcendentals=0),
    )(*args)


def shards(row_count, chip_count, hv, hp, hc, pv, pp, pc, sv, sp, sc, xp, xc):
    cap = hp.shape[1]
    rows = cap * LINES
    order = row_count * rows
    sends = rows // LANES
    f32 = jnp.float32

    def device(r, m, k):
        return (r * chip_count + m) * 2 + k

    def send(value, target):
        pairs = [
            (device(r, m, k), device(*target(r, m, k)))
            for r in range(row_count)
            for m in range(chip_count)
            for k in range(2)
        ]
        return lax.ppermute(value, AXES, pairs)

    def to_other(value):
        return send(value, lambda r, m, k: (r, m, 1 - k))

    def stack(arrays, *others):
        return call(
            functools.partial(stack_kernel, len(others), len(arrays), rows),
            jax.ShapeDtypeStruct((len(arrays) * rows, LANES), f32),
            [pl.BlockSpec(memory_space=pl.ANY)] * len(others) + [VMEM] * len(arrays),
            [],
            1 << 10,
            *others, *arrays,
        )

    hv, hp, pv, pp, sv, sp, xp = (
        pltpu.with_memory_space_constraint(x, pltpu.HBM) for x in (hv, hp, pv, pp, sv, sp, xp)
    )
    hbm = pl.BlockSpec(memory_space=pltpu.HBM)
    value_in, places_in = pltpu.VMEM(hv.shape, f32), pltpu.SMEM(hp.shape, jnp.int32)
    tile, longer, longest = (
        jax.ShapeDtypeStruct((rows + 8 * extra, LANES), f32) for extra in range(3)
    )
    p_near, p_far = call(
        first_kernel,
        [tile, longest],
        [hbm, hbm, SMEM],
        [
            value_in,
            places_in,
            pltpu.VMEM((1, rows, LANES), f32),
            pltpu.SMEM((cap,), jnp.int32),
            pltpu.SemaphoreType.DMA((2,)),
        ],
        1 << 10,
        pv, pp, pc,
    )
    h_tile, s_near, s_far, mask, slot_order = call(
        rest_kernel,
        [
            longer,
            tile,
            longest,
            jax.ShapeDtypeStruct((max(8, cap // 2), LANES), f32),
            jax.ShapeDtypeStruct((1, LANES), jnp.int32),
        ],
        [hbm] * 5 + [SMEM] * 3 + [pl.BlockSpec(memory_space=pl.ANY)],
        [value_in] * 2
        + [places_in] * 3
        + [
            pltpu.VMEM((2, rows, LANES), f32),
            pltpu.SMEM((3 * cap,), jnp.int32),
            pltpu.SemaphoreType.DMA((5,)),
        ],
        1 << 10,
        hv, sv, hp, sp, xp, hc, sc, xc, p_near,
    )
    along = sorted(range(1, row_count), key=lambda s: (s != 1, s))
    across = list(range(chip_count - 1, 0, -1))

    def along_z(near, far):
        return [
            send(near if s == 1 else far, lambda r, m, k, s=s: (r ^ s, m, k)) for s in along
        ]

    def in_plane(x):
        return [send(x, lambda r, m, k, o=o: (r, m ^ o, k)) for o in across]

    def product(a_got, b, b_got, parts):
        part = jax.ShapeDtypeStruct((LANES, LANES), f32)
        return call(
            functools.partial(product_kernel, along, across, sends),
            [longer] + [part] * parts,
            [VMEM] * (4 + len(b_got)),
            [pltpu.VMEM((order, LANES), jnp.bfloat16)] * 2,
            2 * 3 * rows * order * LANES,
            a_got, to_other(a_got), b, *b_got, mask,
        )

    p_got = along_z(p_near, p_far)
    h_got = stack([h_tile] + in_plane(h_tile), *p_got)
    (y,) = product(h_got, p_near, p_got, 0)
    s_got = along_z(s_near, s_far)
    y_got = stack([y] + in_plane(y), *s_got)
    x, *sent = product(y_got, s_near, s_got, sends)

    def mirror(turn):
        def target(r, m, k):
            column = 2 * m + k
            part = (column + turn) % sends
            to = r * sends + part
            return column // sends, to // 2, to % 2

        return target

    mirrors = [send(value, mirror(turn)) for turn, value in enumerate(sent)]
    return call(
        functools.partial(slots_kernel, cap),
        jax.ShapeDtypeStruct((1, cap, BS * BS), f32),
        [SMEM] + [VMEM] * (1 + sends),
        [pltpu.VMEM((rows, LANES), f32)] * 2,
        1 << 20,
        slot_order, x, *mirrors,
    )


def solution(mesh):
    values, ints = P("row", "col", None), P("row", "col")
    row_count, col_count = mesh.shape["row"], mesh.shape["col"]
    return jax.shard_map(
        functools.partial(shards, row_count, col_count // 2),
        mesh=mesh,
        in_specs=(values, ints, ints) * 3 + (ints, ints),
        out_specs=values,
        check_vma=False,
    )
```

time: 140 us -> 51.6 us (0.37)
  waiting for transfers between devices: 71 us -> 22.8 us
  blocking collectives: 31.9 us -> 0 us
  starting transfers between devices: 0.13 us -> 20.1 us
  between operations: 15.9 us -> 2.69 us
  local copies, waits for them, and re-layouts: 9.26 us -> 0 us
  matrix products: 6.34 us -> 0 us
  Pallas kernels: 0 us -> 5.4 us
  other arithmetic: 3.7 us -> 0 us
    psum x1 -> x0, waiting for transfers between devices: 38.6 us -> none  [from_root(): return lax.psum(kept, axis)]
    all_gather x3 -> x0, waiting for transfers between devices: 32.3 us -> none  [the longest x1 23.6 us: shards(): x_panel = lax.all_gather(x_tile, 'col', axis=1, tiled=True)]
    all_gather x2 -> x0, blocking collectives: 31.9 us -> none  [the longest x1 16 us: shards(): lax.all_gather(s_tile, 'row', axis=0, tiled=True)]
    ppermute x0 -> x16, waiting for transfers between devices: none -> 22.8 us  [send(): return lax.ppermute(value, AXES, pairs)]
    ppermute x0 -> x16, starting transfers between devices: none -> 20.1 us  [send(): return lax.ppermute(value, AXES, pairs)]
    dot_general x5 -> x0, matrix products: 6.34 us -> none  [the longest x1 2.87 us: shards(): jnp.dot(lax.all_gather(h_tile, 'col', axis=1, tiled=True), p_columns, pre...]
    pallas_call x0 -> x7, Pallas kernels: none -> 5.4 us  [call(): pl.pallas_call(kernel, out_shape=out_shapes, in_specs=in_specs, out_specs...]
    unnamed x12 -> x0, local copies, waits for them, and re-layouts: 4.14 us -> none
  transfers between devices with their start and end apart: 4 -> 16, of which waited for: 4 -> 8; matrix products, arithmetic and copies ran while one was open for 2% -> 0% of each run, Pallas kernels for 0% -> 4%
where the time goes in v2:
time: 51.6 us; the launch traced here: 51 us
  waiting for transfers between devices  22.8 us (44%)
  starting transfers between devices  20.1 us (39%)
  Pallas kernels  5.4 us (10%)
  between operations  2.69 us (5%)
    ppermute x16, waiting for transfers between devices, send(): return lax.ppermute(value, AXES, pairs)  22.8 us
    ppermute x16, starting transfers between devices, send(): return lax.ppermute(value, AXES, pairs)  20.1 us
    pallas_call x7, Pallas kernels, call(): pl.pallas_call(kernel, out_shape=out_shapes, in_specs=in_specs, out_specs...  5.4 us
  transfers between devices with their start and end apart: 16, of which 8 were waited for; matrix products, arithmetic and copies ran while one was open for 0% of the time, Pallas kernels for 4%

profile of v2, /device:TPU:2, one launch (start us, length us, event | category | flops | bytes accessed | tf_op | source)
XLA Modules:
  0.0 51.0 jit_solution(7674423216600162020)
XLA Ops:
  0.7 1.1 %shard_map.109 = (f32[256,128]{1,0:T(8,128)S(1)}, f32[272,128]{1,0:T(8,128)S(1)}) custom-call(f32[1,8,4096]{2,1,0:T(8,128)} %value.1, s32[1,8]{1,0:T(1,128)} %places.1, s32[1,1]{1,0:T(1,128)S(6)} %copy.13.count), custom_call_target="tpu_custom_call" | custom-call | flops 1024 | bytes 1024 | tf_op jit(solution)/shard_map/pallas_call | solution.py:189
  1.8 1.6 %collective-permute-start.3 = (f32[256,128]{1,0:T(8,128)S(1)}, f32[256,128]{1,0:T(8,128)S(1)}, u32[]{:S(2)}, u32[]{:S(2)}) collective-permute-start(f32[256,128]{1,0:T(8,128)S(1)} %get-tuple-element.15.refs_8_.refs_2_), channel_id=1, source_target_pairs={{0,8},{1,9},{2,10},{3,11},{4,12},{5,13},{6,14},{7,15},{8,0},{9,1},... | collective-permute-start | bytes 393224 | tf_op jit(solution)/shard_map/ppermute | solution.py:217
  3.4 2.6 %collective-permute-start.4 = (f32[272,128]{1,0:T(8,128)S(1)}, f32[272,128]{1,0:T(8,128)S(1)}, u32[]{:S(2)}, u32[]{:S(2)}) collective-permute-start(f32[272,128]{1,0:T(8,128)S(1)} %get-tuple-element.19), channel_id=1, source_target_pairs={{0,16},{1,17},{2,18},{3,19},{4,20},{5,21},{6,22},{7,23},{8,24},{9,... | collective-permute-start | bytes 417800 | tf_op jit(solution)/shard_map/ppermute | solution.py:217
  8.2 1.4 %shard_map.110 = (f32[264,128]{1,0:T(8,128)S(1)}, f32[256,128]{1,0:T(8,128)S(1)}, f32[272,128]{1,0:T(8,128)S(1)}, f32[8,128]{1,0:T(8,128)S(1)}, s32[1,128]{1,0:T(1,128)S(1)}) custom-call(f32[1,8,4096]{2,1,0:T(8,128)} %refs_0_.1, f32[1,8,4096]{2,1,0:T(8,128)} %refs_1_.1, s32[1,8]{1,0:T(1,128)} %refs_2_.1, s32[1,8]{1,0:T(1,128)} %refs_3_.1, s32[1,8]{1,0:T(1,128)} %refs_4_.1, ...), custom_call_target="tpu_custom_call" | custom-call | flops 1024 | bytes 1024 | tf_op jit(solution)/shard_map/pallas_call | solution.py:189
  9.6 1.6 %collective-permute-start.6 = (f32[264,128]{1,0:T(8,128)S(1)}, f32[264,128]{1,0:T(8,128)S(1)}, u32[]{:S(2)}, u32[]{:S(2)}) collective-permute-start(f32[264,128]{1,0:T(8,128)S(1)} %get-tuple-element.20.refs_3_), channel_id=1, source_target_pairs={{0,6},{1,7},{2,4},{3,5},{4,2},{5,3},{6,0},{7,1},{8,14},{9,15},{10,... | collective-permute-start | bytes 405512 | tf_op jit(solution)/shard_map/ppermute | solution.py:217
  11.1 0.3 collective-permute-start.7
  11.4 1.7 %collective-permute-start.8 = (f32[264,128]{1,0:T(8,128)S(1)}, f32[264,128]{1,0:T(8,128)S(1)}, u32[]{:S(2)}, u32[]{:S(2)}) collective-permute-start(f32[264,128]{1,0:T(8,128)S(1)} %get-tuple-element.20.refs_3_), channel_id=1, source_target_pairs={{0,2},{1,3},{2,0},{3,1},{4,6},{5,7},{6,4},{7,5},{8,10},{9,11},{10,... | collective-permute-start | bytes 405512 | tf_op jit(solution)/shard_map/ppermute | solution.py:217
  13.1 3.5 %collective-permute-done.6.refs_4_ = f32[264,128]{1,0:T(8,128)S(1)} collective-permute-done((f32[264,128]{1,0:T(8,128)S(1)}, f32[264,128]{1,0:T(8,128)S(1)}, u32[]{:S(2)}, u32[]{:S(2)}) %collective-permute-start.6) | collective-permute-done | bytes 135200 | tf_op jit(solution)/shard_map/ppermute | solution.py:217
  16.6 1.4 %collective-permute-done.7.refs_5_ = f32[264,128]{1,0:T(8,128)S(1)} collective-permute-done((f32[264,128]{1,0:T(8,128)S(1)}, f32[264,128]{1,0:T(8,128)S(1)}, u32[]{:S(2)}, u32[]{:S(2)}) %collective-permute-start.7) | collective-permute-done | bytes 135200 | tf_op jit(solution)/shard_map/ppermute | solution.py:217
  18.2 1.0 %collective-permute-start = (f32[256,128]{1,0:T(8,128)S(1)}, f32[256,128]{1,0:T(8,128)S(1)}, u32[]{:S(2)}, u32[]{:S(2)}) collective-permute-start(f32[256,128]{1,0:T(8,128)S(1)} %get-tuple-element.17.refs_2_), channel_id=1, source_target_pairs={{0,8},{1,9},{2,10},{3,11},{4,12},{5,13},{6,14},{7,15},{8,0},{9,1},... | collective-permute-start | bytes 393224 | tf_op jit(solution)/shard_map/ppermute | solution.py:217
  19.2 3.2 %collective-permute-start.1 = (f32[272,128]{1,0:T(8,128)S(1)}, f32[272,128]{1,0:T(8,128)S(1)}, u32[]{:S(2)}, u32[]{:S(2)}) collective-permute-start(f32[272,128]{1,0:T(8,128)S(1)} %get-tuple-element.18), channel_id=1, source_target_pairs={{0,16},{1,17},{2,18},{3,19},{4,20},{5,21},{6,22},{7,23},{8,24},{9,... | collective-permute-start | bytes 417800 | tf_op jit(solution)/shard_map/ppermute | solution.py:217
  22.4 0.3 collective-permute-start.2
  22.6 0.7 %shard_map.112.refs_3_ = f32[264,128]{1,0:T(8,128)S(1)} custom-call(f32[1024,128]{1,0:T(8,128)S(1)} %shard_map.111.refs_0_, f32[1024,128]{1,0:T(8,128)S(1)} %collective-permute-done.9.refs_1_, f32[256,128]{1,0:T(8,128)S(1)} %get-tuple-element.15.refs_8_.refs_2_, f32[256,128]{1,0:T(8,128)S(1)} %collective-permute-done.3.refs_0_.refs_3_, ...), custom_call_target="tpu_custom_call" | custom-call | flops 1024 | bytes 1024 | tf_op jit(solution)/shard_map/pallas_call | solution.py:189
  23.3 1.5 %collective-permute-start.10 = (f32[264,128]{1,0:T(8,128)S(1)}, f32[264,128]{1,0:T(8,128)S(1)}, u32[]{:S(2)}, u32[]{:S(2)}) collective-permute-start(f32[264,128]{1,0:T(8,128)S(1)} %shard_map.112.refs_3_), channel_id=1, source_target_pairs={{0,6},{1,7},{2,4},{3,5},{4,2},{5,3},{6,0},{7,1},{8,14},{9,15},{10,... | collective-permute-start | bytes 405512 | tf_op jit(solution)/shard_map/ppermute | solution.py:217
  24.8 0.6 %collective-permute-start.11 = (f32[264,128]{1,0:T(8,128)S(1)}, f32[264,128]{1,0:T(8,128)S(1)}, u32[]{:S(2)}, u32[]{:S(2)}) collective-permute-start(f32[264,128]{1,0:T(8,128)S(1)} %shard_map.112.refs_3_), channel_id=1, source_target_pairs={{0,4},{1,5},{2,6},{3,7},{4,0},{5,1},{6,2},{7,3},{8,12},{9,13},{10,... | collective-permute-start | bytes 405512 | tf_op jit(solution)/shard_map/ppermute | solution.py:217
  25.3 1.3 %collective-permute-done.refs_0_.refs_3_ = f32[256,128]{1,0:T(8,128)S(1)} collective-permute-done((f32[256,128]{1,0:T(8,128)S(1)}, f32[256,128]{1,0:T(8,128)S(1)}, u32[]{:S(2)}, u32[]{:S(2)}) %collective-permute-start) | collective-permute-done | bytes 131104 | tf_op jit(solution)/shard_map/ppermute | solution.py:217
  26.7 0.5 collective-permute-start.12
  27.1 5.7 %collective-permute-done.1.refs_1_.refs_4_ = f32[272,128]{1,0:T(8,128)S(1)} collective-permute-done((f32[272,128]{1,0:T(8,128)S(1)}, f32[272,128]{1,0:T(8,128)S(1)}, u32[]{:S(2)}, u32[]{:S(2)}) %collective-permute-start.1) | collective-permute-done | bytes 139296 | tf_op jit(solution)/shard_map/ppermute | solution.py:217
  33.0 1.9 %collective-permute-done.13.refs_1_ = f32[1024,128]{1,0:T(8,128)S(1)} collective-permute-done((f32[1024,128]{1,0:T(8,128)S(1)}, f32[1024,128]{1,0:T(8,128)S(1)}, u32[]{:S(2)}, u32[]{:S(2)}) %collective-permute-start.13) | collective-permute-done | bytes 524320 | tf_op jit(solution)/shard_map/ppermute | solution.py:217
  34.9 0.7 %shard_map.114 = (f32[264,128]{1,0:T(8,128)S(1)}, f32[128,128]{1,0:T(8,128)S(1)}, f32[128,128]{1,0:T(8,128)S(1)}) custom-call(f32[1024,128]{1,0:T(8,128)S(1)} %shard_map.113.refs_0_, f32[1024,128]{1,0:T(8,128)S(1)} %collective-permute-done.13.refs_1_, f32[256,128]{1,0:T(8,128)S(1)} %get-tuple-element.17.refs_2_, ...), custom_call_target="tpu_custom_call" | custom-call | flops 1024 | bytes 1024 | tf_op jit(solution)/shard_map/pallas_call | solution.py:189
  35.6 4.9 %collective-permute-start.14 = (f32[128,128]{1,0:T(8,128)S(1)}, f32[128,128]{1,0:T(8,128)S(1)}, u32[]{:S(2)}, u32[]{:S(2)}) collective-permute-start(f32[128,128]{1,0:T(8,128)S(1)} %get-tuple-element.23), channel_id=1, source_target_pairs={{0,0},{1,1},{2,8},{3,9},{4,16},{5,17},{6,24},{7,25},{8,2},{9,3},{1... | collective-permute-start | bytes 196616 | tf_op jit(solution)/shard_map/ppermute | solution.py:217
  40.6 5.5 %collective-permute-done.14.refs_0_ = f32[128,128]{1,0:T(8,128)S(1)} collective-permute-done((f32[128,128]{1,0:T(8,128)S(1)}, f32[128,128]{1,0:T(8,128)S(1)}, u32[]{:S(2)}, u32[]{:S(2)}) %collective-permute-start.14) | collective-permute-done | bytes 65568 | tf_op jit(solution)/shard_map/ppermute | solution.py:217
  46.1 3.4 %collective-permute-done.15.refs_1_ = f32[128,128]{1,0:T(8,128)S(1)} collective-permute-done((f32[128,128]{1,0:T(8,128)S(1)}, f32[128,128]{1,0:T(8,128)S(1)}, u32[]{:S(2)}, u32[]{:S(2)}) %collective-permute-start.15) | collective-permute-done | bytes 65568 | tf_op jit(solution)/shard_map/ppermute | solution.py:217
  49.5 1.5 %shard_map.115 = f32[1,8,4096]{2,1,0:T(8,128)} custom-call(s32[1,128]{1,0:T(1,128)S(1)} %get-tuple-element.16.order, f32[264,128]{1,0:T(8,128)S(1)} %get-tuple-element.22.x, f32[128,128]{1,0:T(8,128)S(1)} %collective-permute-done.14.refs_0_, f32[128,128]{1,0:T(8,128)S(1)} %collective-permute-done.15.refs_1_), custom_call_target="tpu_custom_call" | custom-call | flops 1024 | bytes 1024 | tf_op jit(solution)/shard_map/pallas_call | solution.py:189
  (15 shorter events, 0.6 us)
Async XLA Ops:
  1.8 9.6 %collective-permute-start.3 = (f32[256,128]{1,0:T(8,128)S(1)}, f32[256,128]{1,0:T(8,128)S(1)}, u32[]{:S(2)}, u32[]{:S(2)}) collective-permute-start(f32[256,128]{1,0:T(8,128)S(1)} %get-tuple-element.15.refs_8_.refs_2_), channel_id=1, source_target_pairs={{0,8},{1,9},{2,10},{3,11},{4,12},{5,13},{6,14},{7,15},{8,0},{9,1},... | collective-permute-start | bytes 393224 | tf_op jit(solution)/shard_map/ppermute | solution.py:217
  3.4 14.7 %collective-permute-start.4 = (f32[272,128]{1,0:T(8,128)S(1)}, f32[272,128]{1,0:T(8,128)S(1)}, u32[]{:S(2)}, u32[]{:S(2)}) collective-permute-start(f32[272,128]{1,0:T(8,128)S(1)} %get-tuple-element.19), channel_id=1, source_target_pairs={{0,16},{1,17},{2,18},{3,19},{4,20},{5,21},{6,22},{7,23},{8,24},{9,... | collective-permute-start | bytes 417800 | tf_op jit(solution)/shard_map/ppermute | solution.py:217
  6.0 12.1 %collective-permute-start.5 = (f32[272,128]{1,0:T(8,128)S(1)}, f32[272,128]{1,0:T(8,128)S(1)}, u32[]{:S(2)}, u32[]{:S(2)}) collective-permute-start(f32[272,128]{1,0:T(8,128)S(1)} %get-tuple-element.19), channel_id=1, source_target_pairs={{0,24},{1,25},{2,26},{3,27},{4,28},{5,29},{6,30},{7,31},{8,16},{9,... | collective-permute-start | bytes 417800 | tf_op jit(solution)/shard_map/ppermute | solution.py:217
  9.6 7.0 %collective-permute-start.6 = (f32[264,128]{1,0:T(8,128)S(1)}, f32[264,128]{1,0:T(8,128)S(1)}, u32[]{:S(2)}, u32[]{:S(2)}) collective-permute-start(f32[264,128]{1,0:T(8,128)S(1)} %get-tuple-element.20.refs_3_), channel_id=1, source_target_pairs={{0,6},{1,7},{2,4},{3,5},{4,2},{5,3},{6,0},{7,1},{8,14},{9,15},{10,... | collective-permute-start | bytes 405512 | tf_op jit(solution)/shard_map/ppermute | solution.py:217
  11.1 6.9 %collective-permute-start.7 = (f32[264,128]{1,0:T(8,128)S(1)}, f32[264,128]{1,0:T(8,128)S(1)}, u32[]{:S(2)}, u32[]{:S(2)}) collective-permute-start(f32[264,128]{1,0:T(8,128)S(1)} %get-tuple-element.20.refs_3_), channel_id=1, source_target_pairs={{0,4},{1,5},{2,6},{3,7},{4,0},{5,1},{6,2},{7,3},{8,12},{9,13},{10,... | collective-permute-start | bytes 405512 | tf_op jit(solution)/shard_map/ppermute | solution.py:217
  11.4 6.7 %collective-permute-start.8 = (f32[264,128]{1,0:T(8,128)S(1)}, f32[264,128]{1,0:T(8,128)S(1)}, u32[]{:S(2)}, u32[]{:S(2)}) collective-permute-start(f32[264,128]{1,0:T(8,128)S(1)} %get-tuple-element.20.refs_3_), channel_id=1, source_target_pairs={{0,2},{1,3},{2,0},{3,1},{4,6},{5,7},{6,4},{7,5},{8,10},{9,11},{10,... | collective-permute-start | bytes 405512 | tf_op jit(solution)/shard_map/ppermute | solution.py:217
  18.1 4.5 %collective-permute-start.9 = (f32[1024,128]{1,0:T(8,128)S(1)}, f32[1024,128]{1,0:T(8,128)S(1)}, u32[]{:S(2)}, u32[]{:S(2)}) collective-permute-start(f32[1024,128]{1,0:T(8,128)S(1)} %shard_map.111.refs_0_), channel_id=1, source_target_pairs={{0,1},{1,0},{2,3},{3,2},{4,5},{5,4},{6,7},{7,6},{8,9},{9,8},{10,11... | collective-permute-start | bytes 1572872 | tf_op jit(solution)/shard_map/ppermute | solution.py:217
  18.2 8.5 %collective-permute-start = (f32[256,128]{1,0:T(8,128)S(1)}, f32[256,128]{1,0:T(8,128)S(1)}, u32[]{:S(2)}, u32[]{:S(2)}) collective-permute-start(f32[256,128]{1,0:T(8,128)S(1)} %get-tuple-element.17.refs_2_), channel_id=1, source_target_pairs={{0,8},{1,9},{2,10},{3,11},{4,12},{5,13},{6,14},{7,15},{8,0},{9,1},... | collective-permute-start | bytes 393224 | tf_op jit(solution)/shard_map/ppermute | solution.py:217
  19.2 13.6 %collective-permute-start.1 = (f32[272,128]{1,0:T(8,128)S(1)}, f32[272,128]{1,0:T(8,128)S(1)}, u32[]{:S(2)}, u32[]{:S(2)}) collective-permute-start(f32[272,128]{1,0:T(8,128)S(1)} %get-tuple-element.18), channel_id=1, source_target_pairs={{0,16},{1,17},{2,18},{3,19},{4,20},{5,21},{6,22},{7,23},{8,24},{9,... | collective-permute-start | bytes 417800 | tf_op jit(solution)/shard_map/ppermute | solution.py:217
  22.4 10.5 %collective-permute-start.2 = (f32[272,128]{1,0:T(8,128)S(1)}, f32[272,128]{1,0:T(8,128)S(1)}, u32[]{:S(2)}, u32[]{:S(2)}) collective-permute-start(f32[272,128]{1,0:T(8,128)S(1)} %get-tuple-element.18), channel_id=1, source_target_pairs={{0,24},{1,25},{2,26},{3,27},{4,28},{5,29},{6,30},{7,31},{8,16},{9,... | collective-permute-start | bytes 417800 | tf_op jit(solution)/shard_map/ppermute | solution.py:217
  23.3 9.5 %collective-permute-start.10 = (f32[264,128]{1,0:T(8,128)S(1)}, f32[264,128]{1,0:T(8,128)S(1)}, u32[]{:S(2)}, u32[]{:S(2)}) collective-permute-start(f32[264,128]{1,0:T(8,128)S(1)} %shard_map.112.refs_3_), channel_id=1, source_target_pairs={{0,6},{1,7},{2,4},{3,5},{4,2},{5,3},{6,0},{7,1},{8,14},{9,15},{10,... | collective-permute-start | bytes 405512 | tf_op jit(solution)/shard_map/ppermute | solution.py:217
  24.8 8.1 %collective-permute-start.11 = (f32[264,128]{1,0:T(8,128)S(1)}, f32[264,128]{1,0:T(8,128)S(1)}, u32[]{:S(2)}, u32[]{:S(2)}) collective-permute-start(f32[264,128]{1,0:T(8,128)S(1)} %shard_map.112.refs_3_), channel_id=1, source_target_pairs={{0,4},{1,5},{2,6},{3,7},{4,0},{5,1},{6,2},{7,3},{8,12},{9,13},{10,... | collective-permute-start | bytes 405512 | tf_op jit(solution)/shard_map/ppermute | solution.py:217
  26.7 6.2 %collective-permute-start.12 = (f32[264,128]{1,0:T(8,128)S(1)}, f32[264,128]{1,0:T(8,128)S(1)}, u32[]{:S(2)}, u32[]{:S(2)}) collective-permute-start(f32[264,128]{1,0:T(8,128)S(1)} %shard_map.112.refs_3_), channel_id=1, source_target_pairs={{0,2},{1,3},{2,0},{3,1},{4,6},{5,7},{6,4},{7,5},{8,10},{9,11},{10,... | collective-permute-start | bytes 405512 | tf_op jit(solution)/shard_map/ppermute | solution.py:217
  32.9 2.0 %collective-permute-start.13 = (f32[1024,128]{1,0:T(8,128)S(1)}, f32[1024,128]{1,0:T(8,128)S(1)}, u32[]{:S(2)}, u32[]{:S(2)}) collective-permute-start(f32[1024,128]{1,0:T(8,128)S(1)} %shard_map.113.refs_0_), channel_id=1, source_target_pairs={{0,1},{1,0},{2,3},{3,2},{4,5},{5,4},{6,7},{7,6},{8,9},{9,8},{10,11... | collective-permute-start | bytes 1572872 | tf_op jit(solution)/shard_map/ppermute | solution.py:217
  35.6 10.5 %collective-permute-start.14 = (f32[128,128]{1,0:T(8,128)S(1)}, f32[128,128]{1,0:T(8,128)S(1)}, u32[]{:S(2)}, u32[]{:S(2)}) collective-permute-start(f32[128,128]{1,0:T(8,128)S(1)} %get-tuple-element.23), channel_id=1, source_target_pairs={{0,0},{1,1},{2,8},{3,9},{4,16},{5,17},{6,24},{7,25},{8,2},{9,3},{1... | collective-permute-start | bytes 196616 | tf_op jit(solution)/shard_map/ppermute | solution.py:217
  40.5 9.0 %collective-permute-start.15 = (f32[128,128]{1,0:T(8,128)S(1)}, f32[128,128]{1,0:T(8,128)S(1)}, u32[]{:S(2)}, u32[]{:S(2)}) collective-permute-start(f32[128,128]{1,0:T(8,128)S(1)} %get-tuple-element.24), channel_id=1, source_target_pairs={{0,1},{1,0},{2,9},{3,8},{4,17},{5,16},{6,25},{7,24},{8,3},{9,2},{1... | collective-permute-start | bytes 196616 | tf_op jit(solution)/shard_map/ppermute | solution.py:217

commit v3 on v2

--- a/solution.py
+++ b/solution.py
@@ -156,14 +156,28 @@
         ref[...] = out[pl.ds(pl.multiple_of(part * LANES, LANES), LANES), :]
 
 
-def slots_kernel(cap, order, x, *refs):
+def slots_kernel(cap, sends, order, x, *refs):
     mirrors, (out, tile, lines) = refs[:-3], refs[-3:]
-    sends = len(mirrors)
+    row, chip, _ = position()
     tile[...] = x[: tile.shape[0], :]
-    for turn in range(sends):
-        part = lax.rem(lax.axis_index("col") + (sends - turn), sends)
-        at = pl.ds(pl.multiple_of(part * LANES, LANES), LANES)
-        tile[at, :] += mirrors[turn][...].T
+
+    def add(parts):
+        for turn, value in enumerate(parts):
+            part = lax.rem(lax.axis_index("col") + (sends - turn), sends)
+            at = pl.ds(pl.multiple_of(part * LANES, LANES), LANES)
+            tile[at, :] += value.T
+
+    def straight():
+        add([ref[...] for ref in mirrors[:sends]])
+
+    if len(mirrors) == sends:
+        straight()
+    else:
+        kept, other = mirrors[2 * sends :]
+        far = row ^ chip
+        pl.when(far == 0)(lambda: add([kept[...], other[...]]))
+        pl.when(far == 1)(lambda: add([ref[...] for ref in mirrors[sends : 2 * sends]]))
+        pl.when(far > 1)(straight)
     count = order[0, cap]
     left = left_lanes(LINES)
     for pair in range(cap // 2):
@@ -213,6 +227,7 @@
             for r in range(row_count)
             for m in range(chip_count)
             for k in range(2)
+            if target(r, m, k)
         ]
         return lax.ppermute(value, AXES, pairs)
 
@@ -271,13 +286,19 @@
         1 << 10,
         hv, sv, hp, sp, xp, hc, sc, xc, p_near,
     )
-    along = sorted(range(1, row_count), key=lambda s: (s != 1, s))
+    along = list(range(row_count - 1, 0, -1))
     across = list(range(chip_count - 1, 0, -1))
 
     def along_z(near, far):
-        return [
-            send(near if s == 1 else far, lambda r, m, k, s=s: (r ^ s, m, k)) for s in along
-        ]
+        got = {}
+        for offset in sorted(along, key=lambda s: s.bit_count()):
+            low = offset & -offset
+            if offset != low:
+                value = stack([got[offset ^ low]])
+            else:
+                value = near if low == 1 else far
+            got[offset] = send(value, lambda r, m, k: (r ^ low, m, k))
+        return [got[offset] for offset in along]
 
     def in_plane(x):
         return [send(x, lambda r, m, k, o=o: (r, m ^ o, k)) for o in across]
@@ -293,27 +314,40 @@
             a_got, to_other(a_got), b, *b_got, mask,
         )
 
-    p_got = along_z(p_near, p_far)
+    p_got = along_z(p_far, p_far)
     h_got = stack([h_tile] + in_plane(h_tile), *p_got)
     (y,) = product(h_got, p_near, p_got, 0)
     s_got = along_z(s_near, s_far)
     y_got = stack([y] + in_plane(y), *s_got)
     x, *sent = product(y_got, s_near, s_got, sends)
 
+    relay = row_count == chip_count == 4
+
     def mirror(turn):
         def target(r, m, k):
             column = 2 * m + k
             part = (column + turn) % sends
+            if relay and r ^ m < 2:
+                return r, m ^ 1, part
             to = r * sends + part
             return column // sends, to // 2, to % 2
 
         return target
 
     mirrors = [send(value, mirror(turn)) for turn, value in enumerate(sent)]
+    if relay:
+        mirrors += [
+            *(
+                send(part, lambda r, m, k: (r ^ 1, m, k) if r == m else None)
+                for part in mirrors
+            ),
+            sent[0],
+            to_other(sent[1]),
+        ]
     return call(
-        functools.partial(slots_kernel, cap),
+        functools.partial(slots_kernel, cap, sends),
         jax.ShapeDtypeStruct((1, cap, BS * BS), f32),
-        [SMEM] + [VMEM] * (1 + sends),
+        [SMEM] + [VMEM] * (1 + len(mirrors)),
         [pltpu.VMEM((rows, LANES), f32)] * 2,
         1 << 20,
         slot_order, x, *mirrors,

time: 51.6 us -> 50.5 us (0.979)
  starting transfers between devices: 20.1 us -> 18.6 us
  waiting for transfers between devices: 22.8 us -> 23.6 us
    ppermute x16 -> x19, starting transfers between devices: 20.1 us -> 18.6 us  [send(): return lax.ppermute(value, AXES, pairs)]
    ppermute x16 -> x19, waiting for transfers between devices: 22.8 us -> 23.6 us  [send(): return lax.ppermute(value, AXES, pairs)]
    pallas_call x7 -> x9, Pallas kernels: 5.4 us -> 5.43 us  [call(): pl.pallas_call(kernel, out_shape=out_shapes, in_specs=in_specs, out_specs...]
  transfers between devices with their start and end apart: 16 -> 19, of which waited for: 8 -> 11; matrix products, arithmetic and copies ran while one was open for 0% -> 0% of each run, Pallas kernels for 4% -> 4%
where the time goes in v3:
time: 50.5 us; the launch traced here: 50.3 us
  waiting for transfers between devices  23.6 us (47%)
  starting transfers between devices  18.6 us (37%)
  Pallas kernels  5.43 us (11%)
  between operations  2.72 us (5%)
    ppermute x19, waiting for transfers between devices, send(): return lax.ppermute(value, AXES, pairs)  23.6 us
    ppermute x19, starting transfers between devices, send(): return lax.ppermute(value, AXES, pairs)  18.6 us
    pallas_call x9, Pallas kernels, call(): pl.pallas_call(kernel, out_shape=out_shapes, in_specs=in_specs, out_specs...  5.43 us
  transfers between devices with their start and end apart: 19, of which 11 were waited for; matrix products, arithmetic and copies ran while one was open for 0% of the time, Pallas kernels for 4%

profile of v3, /device:TPU:2, one launch (start us, length us, event | category | flops | bytes accessed | tf_op | source)
XLA Modules:
  0.0 50.3 jit_solution(2574339975744375910)
XLA Ops:
  0.7 1.1 %shard_map.109 = (f32[256,128]{1,0:T(8,128)S(1)}, f32[272,128]{1,0:T(8,128)S(1)}) custom-call(f32[1,8,4096]{2,1,0:T(8,128)} %value.1, s32[1,8]{1,0:T(1,128)} %places.1, s32[1,1]{1,0:T(1,128)S(6)} %copy.13.count), custom_call_target="tpu_custom_call" | custom-call | flops 1024 | bytes 1024 | tf_op jit(solution)/shard_map/pallas_call | solution.py:203
  1.8 2.7 %collective-permute-start.3 = (f32[272,128]{1,0:T(8,128)S(1)}, f32[272,128]{1,0:T(8,128)S(1)}, u32[]{:S(2)}, u32[]{:S(2)}) collective-permute-start(f32[272,128]{1,0:T(8,128)S(1)} %get-tuple-element.19), channel_id=1, source_target_pairs={{0,16},{1,17},{2,18},{3,19},{4,20},{5,21},{6,22},{7,23},{8,24},{9,... | collective-permute-start | bytes 417800 | tf_op jit(solution)/shard_map/ppermute | solution.py:232
  4.4 1.6 %collective-permute-start.5 = (f32[272,128]{1,0:T(8,128)S(1)}, f32[272,128]{1,0:T(8,128)S(1)}, u32[]{:S(2)}, u32[]{:S(2)}) collective-permute-start(f32[272,128]{1,0:T(8,128)S(1)} %get-tuple-element.19), channel_id=1, source_target_pairs={{0,8},{1,9},{2,10},{3,11},{4,12},{5,13},{6,14},{7,15},{8,0},{9,1},... | collective-permute-start | bytes 417800 | tf_op jit(solution)/shard_map/ppermute | solution.py:232
  7.9 1.4 %shard_map.110 = (f32[264,128]{1,0:T(8,128)S(1)}, f32[256,128]{1,0:T(8,128)S(1)}, f32[272,128]{1,0:T(8,128)S(1)}, f32[8,128]{1,0:T(8,128)S(1)}, s32[1,128]{1,0:T(1,128)S(1)}) custom-call(f32[1,8,4096]{2,1,0:T(8,128)} %refs_0_.1, f32[1,8,4096]{2,1,0:T(8,128)} %refs_1_.1, s32[1,8]{1,0:T(1,128)} %refs_2_.1, s32[1,8]{1,0:T(1,128)} %refs_3_.1, s32[1,8]{1,0:T(1,128)} %refs_4_.1, ...), custom_call_target="tpu_custom_call" | custom-call | flops 1024 | bytes 1024 | tf_op jit(solution)/shard_map/pallas_call | solution.py:203
  9.3 1.6 %collective-permute-start.6 = (f32[264,128]{1,0:T(8,128)S(1)}, f32[264,128]{1,0:T(8,128)S(1)}, u32[]{:S(2)}, u32[]{:S(2)}) collective-permute-start(f32[264,128]{1,0:T(8,128)S(1)} %get-tuple-element.20.refs_3_), channel_id=1, source_target_pairs={{0,6},{1,7},{2,4},{3,5},{4,2},{5,3},{6,0},{7,1},{8,14},{9,15},{10,... | collective-permute-start | bytes 405512 | tf_op jit(solution)/shard_map/ppermute | solution.py:232
  11.4 1.5 %collective-permute-start.8 = (f32[264,128]{1,0:T(8,128)S(1)}, f32[264,128]{1,0:T(8,128)S(1)}, u32[]{:S(2)}, u32[]{:S(2)}) collective-permute-start(f32[264,128]{1,0:T(8,128)S(1)} %get-tuple-element.20.refs_3_), channel_id=1, source_target_pairs={{0,2},{1,3},{2,0},{3,1},{4,6},{5,7},{6,4},{7,5},{8,10},{9,11},{10,... | collective-permute-start | bytes 405512 | tf_op jit(solution)/shard_map/ppermute | solution.py:232
  13.4 3.2 %collective-permute-done.6.refs_4_ = f32[264,128]{1,0:T(8,128)S(1)} collective-permute-done((f32[264,128]{1,0:T(8,128)S(1)}, f32[264,128]{1,0:T(8,128)S(1)}, u32[]{:S(2)}, u32[]{:S(2)}) %collective-permute-start.6) | collective-permute-done | bytes 135200 | tf_op jit(solution)/shard_map/ppermute | solution.py:232
  16.6 1.4 %collective-permute-done.7.refs_5_ = f32[264,128]{1,0:T(8,128)S(1)} collective-permute-done((f32[264,128]{1,0:T(8,128)S(1)}, f32[264,128]{1,0:T(8,128)S(1)}, u32[]{:S(2)}, u32[]{:S(2)}) %collective-permute-start.7) | collective-permute-done | bytes 135200 | tf_op jit(solution)/shard_map/ppermute | solution.py:232
  18.2 0.9 %collective-permute-start = (f32[272,128]{1,0:T(8,128)S(1)}, f32[272,128]{1,0:T(8,128)S(1)}, u32[]{:S(2)}, u32[]{:S(2)}) collective-permute-start(f32[272,128]{1,0:T(8,128)S(1)} %get-tuple-element.17), channel_id=1, source_target_pairs={{0,16},{1,17},{2,18},{3,19},{4,20},{5,21},{6,22},{7,23},{8,24},{9,... | collective-permute-start | bytes 417800 | tf_op jit(solution)/shard_map/ppermute | solution.py:232
  19.1 1.0 %collective-permute-done.9.refs_1_ = f32[1024,128]{1,0:T(8,128)S(1)} collective-permute-done((f32[1024,128]{1,0:T(8,128)S(1)}, f32[1024,128]{1,0:T(8,128)S(1)}, u32[]{:S(2)}, u32[]{:S(2)}) %collective-permute-start.9) | collective-permute-done | bytes 524320 | tf_op jit(solution)/shard_map/ppermute | solution.py:232
  20.7 1.5 %collective-permute-start.10 = (f32[264,128]{1,0:T(8,128)S(1)}, f32[264,128]{1,0:T(8,128)S(1)}, u32[]{:S(2)}, u32[]{:S(2)}) collective-permute-start(f32[264,128]{1,0:T(8,128)S(1)} %shard_map.114.refs_3_), channel_id=1, source_target_pairs={{0,6},{1,7},{2,4},{3,5},{4,2},{5,3},{6,0},{7,1},{8,14},{9,15},{10,... | collective-permute-start | bytes 405512 | tf_op jit(solution)/shard_map/ppermute | solution.py:232
  22.8 1.5 %collective-permute-start.12 = (f32[264,128]{1,0:T(8,128)S(1)}, f32[264,128]{1,0:T(8,128)S(1)}, u32[]{:S(2)}, u32[]{:S(2)}) collective-permute-start(f32[264,128]{1,0:T(8,128)S(1)} %shard_map.114.refs_3_), channel_id=1, source_target_pairs={{0,2},{1,3},{2,0},{3,1},{4,6},{5,7},{6,4},{7,5},{8,10},{9,11},{10,... | collective-permute-start | bytes 405512 | tf_op jit(solution)/shard_map/ppermute | solution.py:232
  24.3 0.8 %collective-permute-start.2 = (f32[256,128]{1,0:T(8,128)S(1)}, f32[256,128]{1,0:T(8,128)S(1)}, u32[]{:S(2)}, u32[]{:S(2)}) collective-permute-start(f32[256,128]{1,0:T(8,128)S(1)} %get-tuple-element.18.refs_2_), channel_id=1, source_target_pairs={{0,8},{1,9},{2,10},{3,11},{4,12},{5,13},{6,14},{7,15},{8,0},{9,1},... | collective-permute-start | bytes 393224 | tf_op jit(solution)/shard_map/ppermute | solution.py:232
  25.1 3.1 %collective-permute-done.refs_0_.refs_1_.refs_4_ = f32[272,128]{1,0:T(8,128)S(1)} collective-permute-done((f32[272,128]{1,0:T(8,128)S(1)}, f32[272,128]{1,0:T(8,128)S(1)}, u32[]{:S(2)}, u32[]{:S(2)}) %collective-permute-start) | collective-permute-done | bytes 139296 | tf_op jit(solution)/shard_map/ppermute | solution.py:232
  28.2 2.6 %collective-permute-done.2.refs_2_.refs_5_ = f32[256,128]{1,0:T(8,128)S(1)} collective-permute-done((f32[256,128]{1,0:T(8,128)S(1)}, f32[256,128]{1,0:T(8,128)S(1)}, u32[]{:S(2)}, u32[]{:S(2)}) %collective-permute-start.2) | collective-permute-done | bytes 131104 | tf_op jit(solution)/shard_map/ppermute | solution.py:232
  30.9 2.8 %collective-permute-done.1.refs_0_.refs_3_ = f32[256,128]{1,0:T(8,128)S(1)} collective-permute-done((f32[256,128]{1,0:T(8,128)S(1)}, f32[256,128]{1,0:T(8,128)S(1)}, u32[]{:S(2)}, u32[]{:S(2)}) %collective-permute-start.1) | collective-permute-done | bytes 131104 | tf_op jit(solution)/shard_map/ppermute | solution.py:232
  33.8 1.9 %collective-permute-done.13.refs_1_ = f32[1024,128]{1,0:T(8,128)S(1)} collective-permute-done((f32[1024,128]{1,0:T(8,128)S(1)}, f32[1024,128]{1,0:T(8,128)S(1)}, u32[]{:S(2)}, u32[]{:S(2)}) %collective-permute-start.13) | collective-permute-done | bytes 524320 | tf_op jit(solution)/shard_map/ppermute | solution.py:232
  36.9 1.0 %collective-permute-start.15 = (f32[128,128]{1,0:T(8,128)S(1)}, f32[128,128]{1,0:T(8,128)S(1)}, u32[]{:S(2)}, u32[]{:S(2)}) collective-permute-start(f32[128,128]{1,0:T(8,128)S(1)} %get-tuple-element.24), channel_id=1, source_target_pairs={{0,3},{1,2},{2,1},{3,0},{4,17},{5,16},{6,25},{7,24},{8,11},{9,10},... | collective-permute-start | bytes 196616 | tf_op jit(solution)/shard_map/ppermute | solution.py:232
  38.6 2.7 %collective-permute-done.14.refs_0_ = f32[128,128]{1,0:T(8,128)S(1)} collective-permute-done((f32[128,128]{1,0:T(8,128)S(1)}, f32[128,128]{1,0:T(8,128)S(1)}, u32[]{:S(2)}, u32[]{:S(2)}) %collective-permute-start.14) | collective-permute-done | bytes 65568 | tf_op jit(solution)/shard_map/ppermute | solution.py:232
  41.3 1.3 %collective-permute-start.16 = (f32[128,128]{1,0:T(8,128)S(1)}, f32[128,128]{1,0:T(8,128)S(1)}, u32[]{:S(2)}, u32[]{:S(2)}) collective-permute-start(f32[128,128]{1,0:T(8,128)S(1)} %collective-permute-done.14.refs_0_), channel_id=1, source_target_pairs={{0,8},{1,9},{10,2},{11,3},{20,28},{21,29},{30,22},{31,23}} | collective-permute-start | bytes 196616 | tf_op jit(solution)/shard_map/ppermute | solution.py:232
  42.6 1.3 %collective-permute-start.17 = (f32[128,128]{1,0:T(8,128)S(1)}, f32[128,128]{1,0:T(8,128)S(1)}, u32[]{:S(2)}, u32[]{:S(2)}) collective-permute-start(f32[128,128]{1,0:T(8,128)S(1)} %collective-permute-done.15.refs_1_), channel_id=1, source_target_pairs={{0,8},{1,9},{10,2},{11,3},{20,28},{21,29},{30,22},{31,23}} | collective-permute-start | bytes 196616 | tf_op jit(solution)/shard_map/ppermute | solution.py:232
  43.9 3.8 %collective-permute-done.16.refs_2_ = f32[128,128]{1,0:T(8,128)S(1)} collective-permute-done((f32[128,128]{1,0:T(8,128)S(1)}, f32[128,128]{1,0:T(8,128)S(1)}, u32[]{:S(2)}, u32[]{:S(2)}) %collective-permute-start.16) | collective-permute-done | bytes 65568 | tf_op jit(solution)/shard_map/ppermute | solution.py:232
  47.7 1.1 %collective-permute-done.17.refs_3_ = f32[128,128]{1,0:T(8,128)S(1)} collective-permute-done((f32[128,128]{1,0:T(8,128)S(1)}, f32[128,128]{1,0:T(8,128)S(1)}, u32[]{:S(2)}, u32[]{:S(2)}) %collective-permute-start.17) | collective-permute-done | bytes 65568 | tf_op jit(solution)/shard_map/ppermute | solution.py:232
  48.8 1.5 %shard_map.117 = f32[1,8,4096]{2,1,0:T(8,128)} custom-call(s32[1,128]{1,0:T(1,128)S(1)} %get-tuple-element.16.order, f32[264,128]{1,0:T(8,128)S(1)} %get-tuple-element.22.x, f32[128,128]{1,0:T(8,128)S(1)} %collective-permute-done.14.refs_0_, f32[128,128]{1,0:T(8,128)S(1)} %collective-permute-done.15.refs_1_, f32[128,128]{1,0:T(8,128)S(1)} %collective-permute-done.16.refs_2_, ...), custom_call_target="tpu_custom_call" | custom-call | flops 1024 | bytes 1024 | tf_op jit(solution)/shard_map/pallas_call | solution.py:203
  (23 shorter events, 4.5 us)
Async XLA Ops:
  1.8 11.1 %collective-permute-start.3 = (f32[272,128]{1,0:T(8,128)S(1)}, f32[272,128]{1,0:T(8,128)S(1)}, u32[]{:S(2)}, u32[]{:S(2)}) collective-permute-start(f32[272,128]{1,0:T(8,128)S(1)} %get-tuple-element.19), channel_id=1, source_target_pairs={{0,16},{1,17},{2,18},{3,19},{4,20},{5,21},{6,22},{7,23},{8,24},{9,... | collective-permute-start | bytes 417800 | tf_op jit(solution)/shard_map/ppermute | solution.py:232
  4.4 13.6 %collective-permute-start.5 = (f32[272,128]{1,0:T(8,128)S(1)}, f32[272,128]{1,0:T(8,128)S(1)}, u32[]{:S(2)}, u32[]{:S(2)}) collective-permute-start(f32[272,128]{1,0:T(8,128)S(1)} %get-tuple-element.19), channel_id=1, source_target_pairs={{0,8},{1,9},{2,10},{3,11},{4,12},{5,13},{6,14},{7,15},{8,0},{9,1},... | collective-permute-start | bytes 417800 | tf_op jit(solution)/shard_map/ppermute | solution.py:232
  9.3 7.2 %collective-permute-start.6 = (f32[264,128]{1,0:T(8,128)S(1)}, f32[264,128]{1,0:T(8,128)S(1)}, u32[]{:S(2)}, u32[]{:S(2)}) collective-permute-start(f32[264,128]{1,0:T(8,128)S(1)} %get-tuple-element.20.refs_3_), channel_id=1, source_target_pairs={{0,6},{1,7},{2,4},{3,5},{4,2},{5,3},{6,0},{7,1},{8,14},{9,15},{10,... | collective-permute-start | bytes 405512 | tf_op jit(solution)/shard_map/ppermute | solution.py:232
  10.9 7.1 %collective-permute-start.7 = (f32[264,128]{1,0:T(8,128)S(1)}, f32[264,128]{1,0:T(8,128)S(1)}, u32[]{:S(2)}, u32[]{:S(2)}) collective-permute-start(f32[264,128]{1,0:T(8,128)S(1)} %get-tuple-element.20.refs_3_), channel_id=1, source_target_pairs={{0,4},{1,5},{2,6},{3,7},{4,0},{5,1},{6,2},{7,3},{8,12},{9,13},{10,... | collective-permute-start | bytes 405512 | tf_op jit(solution)/shard_map/ppermute | solution.py:232
  11.4 6.7 %collective-permute-start.8 = (f32[264,128]{1,0:T(8,128)S(1)}, f32[264,128]{1,0:T(8,128)S(1)}, u32[]{:S(2)}, u32[]{:S(2)}) collective-permute-start(f32[264,128]{1,0:T(8,128)S(1)} %get-tuple-element.20.refs_3_), channel_id=1, source_target_pairs={{0,2},{1,3},{2,0},{3,1},{4,6},{5,7},{6,4},{7,5},{8,10},{9,11},{10,... | collective-permute-start | bytes 405512 | tf_op jit(solution)/shard_map/ppermute | solution.py:232
  12.9 5.2 %collective-permute-start.4 = (f32[256,128]{1,0:T(8,128)S(1)}, f32[256,128]{1,0:T(8,128)S(1)}, u32[]{:S(2)}, u32[]{:S(2)}) collective-permute-start(f32[256,128]{1,0:T(8,128)S(1)} %shard_map.112), channel_id=1, source_target_pairs={{0,8},{1,9},{2,10},{3,11},{4,12},{5,13},{6,14},{7,15},{8,0},{9,1},... | collective-permute-start | bytes 393224 | tf_op jit(solution)/shard_map/ppermute | solution.py:232
  18.1 2.0 %collective-permute-start.9 = (f32[1024,128]{1,0:T(8,128)S(1)}, f32[1024,128]{1,0:T(8,128)S(1)}, u32[]{:S(2)}, u32[]{:S(2)}) collective-permute-start(f32[1024,128]{1,0:T(8,128)S(1)} %shard_map.113.refs_0_), channel_id=1, source_target_pairs={{0,1},{1,0},{2,3},{3,2},{4,5},{5,4},{6,7},{7,6},{8,9},{9,8},{10,11... | collective-permute-start | bytes 1572872 | tf_op jit(solution)/shard_map/ppermute | solution.py:232
  18.2 10.0 %collective-permute-start = (f32[272,128]{1,0:T(8,128)S(1)}, f32[272,128]{1,0:T(8,128)S(1)}, u32[]{:S(2)}, u32[]{:S(2)}) collective-permute-start(f32[272,128]{1,0:T(8,128)S(1)} %get-tuple-element.17), channel_id=1, source_target_pairs={{0,16},{1,17},{2,18},{3,19},{4,20},{5,21},{6,22},{7,23},{8,24},{9,... | collective-permute-start | bytes 417800 | tf_op jit(solution)/shard_map/ppermute | solution.py:232
  20.7 12.9 %collective-permute-start.10 = (f32[264,128]{1,0:T(8,128)S(1)}, f32[264,128]{1,0:T(8,128)S(1)}, u32[]{:S(2)}, u32[]{:S(2)}) collective-permute-start(f32[264,128]{1,0:T(8,128)S(1)} %shard_map.114.refs_3_), channel_id=1, source_target_pairs={{0,6},{1,7},{2,4},{3,5},{4,2},{5,3},{6,0},{7,1},{8,14},{9,15},{10,... | collective-permute-start | bytes 405512 | tf_op jit(solution)/shard_map/ppermute | solution.py:232
  22.2 11.5 %collective-permute-start.11 = (f32[264,128]{1,0:T(8,128)S(1)}, f32[264,128]{1,0:T(8,128)S(1)}, u32[]{:S(2)}, u32[]{:S(2)}) collective-permute-start(f32[264,128]{1,0:T(8,128)S(1)} %shard_map.114.refs_3_), channel_id=1, source_target_pairs={{0,4},{1,5},{2,6},{3,7},{4,0},{5,1},{6,2},{7,3},{8,12},{9,13},{10,... | collective-permute-start | bytes 405512 | tf_op jit(solution)/shard_map/ppermute | solution.py:232
  22.8 10.9 %collective-permute-start.12 = (f32[264,128]{1,0:T(8,128)S(1)}, f32[264,128]{1,0:T(8,128)S(1)}, u32[]{:S(2)}, u32[]{:S(2)}) collective-permute-start(f32[264,128]{1,0:T(8,128)S(1)} %shard_map.114.refs_3_), channel_id=1, source_target_pairs={{0,2},{1,3},{2,0},{3,1},{4,6},{5,7},{6,4},{7,5},{8,10},{9,11},{10,... | collective-permute-start | bytes 405512 | tf_op jit(solution)/shard_map/ppermute | solution.py:232
  24.3 6.6 %collective-permute-start.2 = (f32[256,128]{1,0:T(8,128)S(1)}, f32[256,128]{1,0:T(8,128)S(1)}, u32[]{:S(2)}, u32[]{:S(2)}) collective-permute-start(f32[256,128]{1,0:T(8,128)S(1)} %get-tuple-element.18.refs_2_), channel_id=1, source_target_pairs={{0,8},{1,9},{2,10},{3,11},{4,12},{5,13},{6,14},{7,15},{8,0},{9,1},... | collective-permute-start | bytes 393224 | tf_op jit(solution)/shard_map/ppermute | solution.py:232
  28.2 5.5 %collective-permute-start.1 = (f32[256,128]{1,0:T(8,128)S(1)}, f32[256,128]{1,0:T(8,128)S(1)}, u32[]{:S(2)}, u32[]{:S(2)}) collective-permute-start(f32[256,128]{1,0:T(8,128)S(1)} %shard_map.111), channel_id=1, source_target_pairs={{0,8},{1,9},{2,10},{3,11},{4,12},{5,13},{6,14},{7,15},{8,0},{9,1},... | collective-permute-start | bytes 393224 | tf_op jit(solution)/shard_map/ppermute | solution.py:232
  33.7 2.0 %collective-permute-start.13 = (f32[1024,128]{1,0:T(8,128)S(1)}, f32[1024,128]{1,0:T(8,128)S(1)}, u32[]{:S(2)}, u32[]{:S(2)}) collective-permute-start(f32[1024,128]{1,0:T(8,128)S(1)} %shard_map.115.refs_0_), channel_id=1, source_target_pairs={{0,1},{1,0},{2,3},{3,2},{4,5},{5,4},{6,7},{7,6},{8,9},{9,8},{10,11... | collective-permute-start | bytes 1572872 | tf_op jit(solution)/shard_map/ppermute | solution.py:232
  36.4 5.0 %collective-permute-start.14 = (f32[128,128]{1,0:T(8,128)S(1)}, f32[128,128]{1,0:T(8,128)S(1)}, u32[]{:S(2)}, u32[]{:S(2)}) collective-permute-start(f32[128,128]{1,0:T(8,128)S(1)} %get-tuple-element.23.refs_4_), channel_id=1, source_target_pairs={{0,2},{1,3},{2,0},{3,1},{4,16},{5,17},{6,24},{7,25},{8,10},{9,11},... | collective-permute-start | bytes 196616 | tf_op jit(solution)/shard_map/ppermute | solution.py:232
  36.9 5.7 %collective-permute-start.15 = (f32[128,128]{1,0:T(8,128)S(1)}, f32[128,128]{1,0:T(8,128)S(1)}, u32[]{:S(2)}, u32[]{:S(2)}) collective-permute-start(f32[128,128]{1,0:T(8,128)S(1)} %get-tuple-element.24), channel_id=1, source_target_pairs={{0,3},{1,2},{2,1},{3,0},{4,17},{5,16},{6,25},{7,24},{8,11},{9,10},... | collective-permute-start | bytes 196616 | tf_op jit(solution)/shard_map/ppermute | solution.py:232
  37.9 6.0 %collective-permute-start.18 = (f32[128,128]{1,0:T(8,128)S(1)}, f32[128,128]{1,0:T(8,128)S(1)}, u32[]{:S(2)}, u32[]{:S(2)}) collective-permute-start(f32[128,128]{1,0:T(8,128)S(1)} %get-tuple-element.24), channel_id=1, source_target_pairs={{0,1},{1,0},{2,3},{3,2},{4,5},{5,4},{6,7},{7,6},{8,9},{9,8},{10,11... | collective-permute-start | bytes 196616 | tf_op jit(solution)/shard_map/ppermute | solution.py:232
  41.3 6.4 %collective-permute-start.16 = (f32[128,128]{1,0:T(8,128)S(1)}, f32[128,128]{1,0:T(8,128)S(1)}, u32[]{:S(2)}, u32[]{:S(2)}) collective-permute-start(f32[128,128]{1,0:T(8,128)S(1)} %collective-permute-done.14.refs_0_), channel_id=1, source_target_pairs={{0,8},{1,9},{10,2},{11,3},{20,28},{21,29},{30,22},{31,23}} | collective-permute-start | bytes 196616 | tf_op jit(solution)/shard_map/ppermute | solution.py:232
  42.6 6.2 %collective-permute-start.17 = (f32[128,128]{1,0:T(8,128)S(1)}, f32[128,128]{1,0:T(8,128)S(1)}, u32[]{:S(2)}, u32[]{:S(2)}) collective-permute-start(f32[128,128]{1,0:T(8,128)S(1)} %collective-permute-done.15.refs_1_), channel_id=1, source_target_pairs={{0,8},{1,9},{10,2},{11,3},{20,28},{21,29},{30,22},{31,23}} | collective-permute-start | bytes 196616 | tf_op jit(solution)/shard_map/ppermute | solution.py:232

commit v4 on v3

--- a/solution.py
+++ b/solution.py
@@ -25,10 +25,11 @@
     return lax.broadcasted_iota(jnp.int32, (rows, LANES), 1) < BS
 
 
-def invert(places, inverse, base):
-    cap = places.shape[1]
-    for slot in range(cap):
-        inverse[base + places[0, slot]] = slot
+def slot_places(places, count, rows=LINES):
+    return [
+        jnp.where(slot < count, jnp.broadcast_to(places[0:1, slot : slot + 1], (rows, LANES)), -1)
+        for slot in range(places.shape[1])
+    ]
 
 
 def fill(ref, rows):
@@ -36,79 +37,61 @@
         ref[rows:, :] = jnp.zeros((ref.shape[0] - rows, LANES), jnp.float32)
 
 
-def assemble(values, places, counts, lines, inverse, ready, tiles):
+def assemble(value, places, count, lines, tiles):
     left = left_lanes(LINES)
-    for which, value in enumerate(values):
-        cap = value.shape[1]
-        ready(which)
-        invert(places[which], inverse, which * cap)
-        count = counts[which][0, 0]
-        for line in range(LINES):
-            lines[which, pl.ds(line, cap, stride=LINES), :] = value[
-                0, :, line * LANES : (line + 1) * LANES
-            ]
-
-        def block(place):
-            slot = inverse[which * cap + place]
-            kept = (slot < count).astype(jnp.float32)
-            start = pl.multiple_of(slot * LINES, LINES)
-            return lines[which, pl.ds(start, LINES), :] * kept
-
-        for pair in range(cap // 2):
-            first, second = block(2 * pair), block(2 * pair + 1)
-            even = jnp.where(left, first, pltpu.roll(second, BS, 1))
-            odd = jnp.where(left, pltpu.roll(first, BS, 1), second)
-            for tile in tiles[which]:
-                tile[pl.ds(pair * BS, LINES, stride=2), :] = even
-                tile[pl.ds(pair * BS + 1, LINES, stride=2), :] = odd
-        for tile in tiles[which]:
-            fill(tile, cap * LINES)
-
-
-def first_kernel(value, places, count, near, far, value_in, places_in, lines, inverse, sems):
+    cap = value.shape[1]
+    for line in range(LINES):
+        lines[pl.ds(line, cap, stride=LINES), :] = value[0, :, line * LANES : (line + 1) * LANES]
+    at = slot_places(places, count)
+
+    def block(place):
+        picked = jnp.zeros((LINES, LANES), jnp.float32)
+        for slot in range(cap):
+            rows = lines[slot * LINES : (slot + 1) * LINES, :]
+            picked = jnp.where(at[slot] == place, rows, picked)
+        return picked
+
+    for pair in range(cap // 2):
+        first, second = block(2 * pair), block(2 * pair + 1)
+        even = jnp.where(left, first, pltpu.roll(second, BS, 1))
+        odd = jnp.where(left, pltpu.roll(first, BS, 1), second)
+        for tile in tiles:
+            tile[pl.ds(pair * BS, LINES, stride=2), :] = even
+            tile[pl.ds(pair * BS + 1, LINES, stride=2), :] = odd
+    for tile in tiles:
+        fill(tile, cap * LINES)
+
+
+def first_kernel(count, *refs):
+    sources, (near, far), fetched = refs[:7], refs[7:9], refs[9:14]
+    value_in, places_in, lines, sems = refs[14:]
     copies = [
-        pltpu.make_async_copy(places, places_in, sems.at[0]),
-        pltpu.make_async_copy(value, value_in, sems.at[1]),
+        pltpu.make_async_copy(source, ref, sems.at[i])
+        for i, (source, ref) in enumerate(zip(sources, (places_in, value_in) + fetched))
     ]
     for copy in copies:
         copy.start()
-
-    def ready(_):
-        for copy in copies:
-            copy.wait()
-
-    assemble([value_in], [places_in], [count], lines, inverse, ready, [(near, far)])
-
-
-def rest_kernel(*refs):
-    sources, counts, (h_tile, s_near, s_far, mask, order) = refs[:5], refs[5:8], refs[9:14]
-    values, places = refs[14:16], refs[16:19]
-    lines, inverse, sems = refs[19:]
-    copies = [
-        pltpu.make_async_copy(source, ref, sems.at[i])
-        for i, (source, ref) in enumerate(zip(sources, refs[14:19]))
-    ]
-    for copy in copies:
-        copy.start()
-    cap = values[0].shape[1]
-
-    def ready(which):
-        copies[which].wait()
-        copies[2 + which].wait()
-
-    assemble(values, places, counts, lines, inverse, ready, [(h_tile,), (s_near, s_far)])
-    copies[4].wait()
-    invert(places[2], inverse, 2 * cap)
-    count = counts[2][0, 0]
-    slots = [inverse[2 * cap + place] for place in range(cap)]
-    lanes = lax.broadcasted_iota(jnp.int32, (1, LANES), 1)
-    row = jnp.where(lanes == cap, count, 0)
-    for place in range(cap):
-        row = jnp.where(lanes == place, slots[place], row)
-    order[...] = row
+    for copy in copies[:2]:
+        copy.wait()
+    assemble(value_in, places_in, count[0, 0], lines, (near, far))
+    for copy in copies[2:]:
+        copy.wait()
+
+
+def rest_kernel(hv, sv, hp, sp, xp, hc, sc, xc, h_tile, s_near, s_far, mask, lines):
+    assemble(hv, hp, hc[0, 0], lines, (h_tile,))
+    assemble(sv, sp, sc[0, 0], lines, (s_near, s_far))
+    cap = xp.shape[1]
+    at = slot_places(xp, xc[0, 0], 1)
+
+    def flag(place):
+        present = jnp.zeros((1, LANES), jnp.float32)
+        for slot in range(cap):
+            present = jnp.where(at[slot] == place, 1.0, present)
+        return present
+
     for pair in range(cap // 2):
-        flags = [(slots[2 * pair + side] < count).astype(jnp.float32) for side in range(2)]
-        mask[pair : pair + 1, :] = jnp.where(left_lanes(1), flags[0], flags[1])
+        mask[pair : pair + 1, :] = jnp.where(left_lanes(1), flag(2 * pair), flag(2 * pair + 1))
 
 
 def stack_kernel(others, count, rows, *refs):
@@ -156,7 +139,7 @@
         ref[...] = out[pl.ds(pl.multiple_of(part * LANES, LANES), LANES), :]
 
 
-def slots_kernel(cap, sends, order, x, *refs):
+def slots_kernel(cap, sends, places, count, x, *refs):
     mirrors, (out, tile, lines) = refs[:-3], refs[-3:]
     row, chip, _ = position()
     tile[...] = x[: tile.shape[0], :]
@@ -173,25 +156,23 @@
     if len(mirrors) == sends:
         straight()
     else:
-        kept, other = mirrors[2 * sends :]
+        relayed, kept, other = (ref[...] for ref in mirrors[sends:])
         far = row ^ chip
-        pl.when(far == 0)(lambda: add([kept[...], other[...]]))
-        pl.when(far == 1)(lambda: add([ref[...] for ref in mirrors[sends : 2 * sends]]))
+        pl.when(far == 0)(lambda: add([kept, other]))
+        pl.when(far == 1)(lambda: add([relayed, mirrors[1][...]]))
         pl.when(far > 1)(straight)
-    count = order[0, cap]
     left = left_lanes(LINES)
+    blocks = []
     for pair in range(cap // 2):
         even = tile[pl.ds(pair * BS, LINES, stride=2), :]
         odd = tile[pl.ds(pair * BS + 1, LINES, stride=2), :]
-        blocks = (
-            jnp.where(left, even, pltpu.roll(odd, BS, 1)),
-            jnp.where(left, pltpu.roll(even, BS, 1), odd),
-        )
-        for side in range(2):
-            slot = order[0, 2 * pair + side]
-            used = (slot < count).astype(jnp.float32)
-            start = pl.multiple_of(slot * LINES, LINES)
-            lines[pl.ds(start, LINES), :] = blocks[side] * used
+        blocks.append(jnp.where(left, even, pltpu.roll(odd, BS, 1)))
+        blocks.append(jnp.where(left, pltpu.roll(even, BS, 1), odd))
+    for slot, at in enumerate(slot_places(places, count[0, 0])):
+        picked = jnp.zeros((LINES, LANES), jnp.float32)
+        for place, block in enumerate(blocks):
+            picked = jnp.where(at == place, block, picked)
+        lines[slot * LINES : (slot + 1) * LINES, :] = picked
     for line in range(LINES):
         out[0, :, line * LANES : (line + 1) * LANES] = lines[
             pl.ds(line, cap, stride=LINES), :
@@ -244,47 +225,33 @@
             *others, *arrays,
         )
 
-    hv, hp, pv, pp, sv, sp, xp = (
-        pltpu.with_memory_space_constraint(x, pltpu.HBM) for x in (hv, hp, pv, pp, sv, sp, xp)
-    )
-    hbm = pl.BlockSpec(memory_space=pltpu.HBM)
-    value_in, places_in = pltpu.VMEM(hv.shape, f32), pltpu.SMEM(hp.shape, jnp.int32)
+    inputs = [
+        pltpu.with_memory_space_constraint(x, pltpu.HBM) for x in (pp, pv, hv, sv, hp, sp, xp)
+    ]
     tile, longer, longest = (
         jax.ShapeDtypeStruct((rows + 8 * extra, LANES), f32) for extra in range(3)
     )
-    p_near, p_far = call(
+    lines = pltpu.VMEM((rows, LANES), f32)
+    p_near, p_far, hv, sv, hp, sp, xp = call(
         first_kernel,
-        [tile, longest],
-        [hbm, hbm, SMEM],
+        [tile, longest] + [jax.ShapeDtypeStruct(x.shape, x.dtype) for x in inputs[2:]],
+        [SMEM] + [pl.BlockSpec(memory_space=pltpu.HBM)] * 7,
         [
-            value_in,
-            places_in,
-            pltpu.VMEM((1, rows, LANES), f32),
-            pltpu.SMEM((cap,), jnp.int32),
-            pltpu.SemaphoreType.DMA((2,)),
+            pltpu.VMEM(pv.shape, f32),
+            pltpu.VMEM(pp.shape, jnp.int32),
+            lines,
+            pltpu.SemaphoreType.DMA((7,)),
         ],
         1 << 10,
-        pv, pp, pc,
-    )
-    h_tile, s_near, s_far, mask, slot_order = call(
+        pc, *inputs,
+    )
+    h_tile, s_near, s_far, mask = call(
         rest_kernel,
-        [
-            longer,
-            tile,
-            longest,
-            jax.ShapeDtypeStruct((max(8, cap // 2), LANES), f32),
-            jax.ShapeDtypeStruct((1, LANES), jnp.int32),
-        ],
-        [hbm] * 5 + [SMEM] * 3 + [pl.BlockSpec(memory_space=pl.ANY)],
-        [value_in] * 2
-        + [places_in] * 3
-        + [
-            pltpu.VMEM((2, rows, LANES), f32),
-            pltpu.SMEM((3 * cap,), jnp.int32),
-            pltpu.SemaphoreType.DMA((5,)),
-        ],
+        [longer, tile, longest, jax.ShapeDtypeStruct((max(8, cap // 2), LANES), f32)],
+        [VMEM] * 5 + [SMEM] * 3,
+        [lines],
         1 << 10,
-        hv, sv, hp, sp, xp, hc, sc, xc, p_near,
+        hv, sv, hp, sp, xp, hc, sc, xc,
     )
     along = list(range(row_count - 1, 0, -1))
     across = list(range(chip_count - 1, 0, -1))
@@ -327,7 +294,7 @@
         def target(r, m, k):
             column = 2 * m + k
             part = (column + turn) % sends
-            if relay and r ^ m < 2:
+            if relay and turn == 0 and r ^ m < 2:
                 return r, m ^ 1, part
             to = r * sends + part
             return column // sends, to // 2, to % 2
@@ -337,20 +304,17 @@
     mirrors = [send(value, mirror(turn)) for turn, value in enumerate(sent)]
     if relay:
         mirrors += [
-            *(
-                send(part, lambda r, m, k: (r ^ 1, m, k) if r == m else None)
-                for part in mirrors
-            ),
+            send(mirrors[0], lambda r, m, k: (r ^ 1, m, k) if r == m else None),
             sent[0],
             to_other(sent[1]),
         ]
     return call(
         functools.partial(slots_kernel, cap, sends),
         jax.ShapeDtypeStruct((1, cap, BS * BS), f32),
-        [SMEM] + [VMEM] * (1 + len(mirrors)),
-        [pltpu.VMEM((rows, LANES), f32)] * 2,
+        [VMEM, SMEM] + [VMEM] * (1 + len(mirrors)),
+        [lines] * 2,
         1 << 20,
-        slot_order, x, *mirrors,
+        xp, xc, x, *mirrors,
     )
 
 

time: 50.5 us -> 48.4 us (0.958)
  Pallas kernels: 5.43 us -> 3.96 us
  waiting for transfers between devices: 23.6 us -> 22.5 us
    pallas_call x9, Pallas kernels: 5.43 us -> 3.96 us  [call(): pl.pallas_call(kernel, out_shape=out_shapes, in_specs=in_specs, out_specs...]
    ppermute x19 -> x18, waiting for transfers between devices: 23.6 us -> 22.5 us  [send(): return lax.ppermute(value, AXES, pairs)]
    ppermute x19 -> x18, starting transfers between devices: 18.6 us -> 18.8 us  [send(): return lax.ppermute(value, AXES, pairs)]
  transfers between devices with their start and end apart: 19 -> 18, of which waited for: 11 -> 9; matrix products, arithmetic and copies ran while one was open for 0% -> 0% of each run, Pallas kernels for 4% -> 2%
where the time goes in v4:
time: 48.4 us; the launch traced here: 48 us
  waiting for transfers between devices  22.5 us (46%)
  starting transfers between devices  18.8 us (39%)
  Pallas kernels  3.96 us (8%)
  between operations  2.7 us (6%)
    ppermute x18, waiting for transfers between devices, send(): return lax.ppermute(value, AXES, pairs)  22.5 us
    ppermute x18, starting transfers between devices, send(): return lax.ppermute(value, AXES, pairs)  18.8 us
    pallas_call x9, Pallas kernels, call(): pl.pallas_call(kernel, out_shape=out_shapes, in_specs=in_specs, out_specs...  3.96 us
  transfers between devices with their start and end apart: 18, of which 9 were waited for; matrix products, arithmetic and copies ran while one was open for 0% of the time, Pallas kernels for 2%

profile of v4, /device:TPU:2, one launch (start us, length us, event | category | flops | bytes accessed | tf_op | source)
XLA Modules:
  0.0 48.0 jit_solution(10402774972953854888)
XLA Ops:
  0.7 1.2 %shard_map.109 = (f32[256,128]{1,0:T(8,128)S(1)}, f32[272,128]{1,0:T(8,128)S(1)}, f32[1,8,4096]{2,1,0:T(8,128)S(1)}, f32[1,8,4096]{2,1,0:T(8,128)S(1)}, s32[1,8]...) custom-call(s32[1,1]{1,0:T(1,128)S(6)} %copy.13.count, s32[1,8]{1,0:T(1,128)} %refs_0_.1, ...), custom_call_target="tpu_custom_call" | custom-call | flops 1024 | bytes 1024 | tf_op jit(solution)/shard_map/pallas_call | solution.py:184
  1.9 2.7 %collective-permute-start.3 = (f32[272,128]{1,0:T(8,128)S(1)}, f32[272,128]{1,0:T(8,128)S(1)}, u32[]{:S(2)}, u32[]{:S(2)}) collective-permute-start(f32[272,128]{1,0:T(8,128)S(1)} %get-tuple-element.26), channel_id=1, source_target_pairs={{0,16},{1,17},{2,18},{3,19},{4,20},{5,21},{6,22},{7,23},{8,24},{9,... | collective-permute-start | bytes 417800 | tf_op jit(solution)/shard_map/ppermute | solution.py:213
  4.5 1.6 %collective-permute-start.5 = (f32[272,128]{1,0:T(8,128)S(1)}, f32[272,128]{1,0:T(8,128)S(1)}, u32[]{:S(2)}, u32[]{:S(2)}) collective-permute-start(f32[272,128]{1,0:T(8,128)S(1)} %get-tuple-element.26), channel_id=1, source_target_pairs={{0,8},{1,9},{2,10},{3,11},{4,12},{5,13},{6,14},{7,15},{8,0},{9,1},... | collective-permute-start | bytes 417800 | tf_op jit(solution)/shard_map/ppermute | solution.py:213
  8.4 1.6 %collective-permute-start.6 = (f32[264,128]{1,0:T(8,128)S(1)}, f32[264,128]{1,0:T(8,128)S(1)}, u32[]{:S(2)}, u32[]{:S(2)}) collective-permute-start(f32[264,128]{1,0:T(8,128)S(1)} %get-tuple-element.27.refs_3_), channel_id=1, source_target_pairs={{0,6},{1,7},{2,4},{3,5},{4,2},{5,3},{6,0},{7,1},{8,14},{9,15},{10,... | collective-permute-start | bytes 405512 | tf_op jit(solution)/shard_map/ppermute | solution.py:213
  10.5 1.5 %collective-permute-start.8 = (f32[264,128]{1,0:T(8,128)S(1)}, f32[264,128]{1,0:T(8,128)S(1)}, u32[]{:S(2)}, u32[]{:S(2)}) collective-permute-start(f32[264,128]{1,0:T(8,128)S(1)} %get-tuple-element.27.refs_3_), channel_id=1, source_target_pairs={{0,2},{1,3},{2,0},{3,1},{4,6},{5,7},{6,4},{7,5},{8,10},{9,11},{10,... | collective-permute-start | bytes 405512 | tf_op jit(solution)/shard_map/ppermute | solution.py:213
  12.5 3.2 %collective-permute-done.6.refs_4_ = f32[264,128]{1,0:T(8,128)S(1)} collective-permute-done((f32[264,128]{1,0:T(8,128)S(1)}, f32[264,128]{1,0:T(8,128)S(1)}, u32[]{:S(2)}, u32[]{:S(2)}) %collective-permute-start.6) | collective-permute-done | bytes 135200 | tf_op jit(solution)/shard_map/ppermute | solution.py:213
  15.6 1.4 %collective-permute-done.7.refs_5_ = f32[264,128]{1,0:T(8,128)S(1)} collective-permute-done((f32[264,128]{1,0:T(8,128)S(1)}, f32[264,128]{1,0:T(8,128)S(1)}, u32[]{:S(2)}, u32[]{:S(2)}) %collective-permute-start.7) | collective-permute-done | bytes 135200 | tf_op jit(solution)/shard_map/ppermute | solution.py:213
  17.2 2.0 %collective-permute-start = (f32[272,128]{1,0:T(8,128)S(1)}, f32[272,128]{1,0:T(8,128)S(1)}, u32[]{:S(2)}, u32[]{:S(2)}) collective-permute-start(f32[272,128]{1,0:T(8,128)S(1)} %get-tuple-element.24), channel_id=1, source_target_pairs={{0,16},{1,17},{2,18},{3,19},{4,20},{5,21},{6,22},{7,23},{8,24},{9,... | collective-permute-start | bytes 417800 | tf_op jit(solution)/shard_map/ppermute | solution.py:213
  19.2 0.7 %shard_map.114.refs_3_ = f32[264,128]{1,0:T(8,128)S(1)} custom-call(f32[1024,128]{1,0:T(8,128)S(1)} %shard_map.113.refs_0_, f32[1024,128]{1,0:T(8,128)S(1)} %collective-permute-done.9.refs_1_, f32[256,128]{1,0:T(8,128)S(1)} %get-tuple-element.28.refs_2_, f32[256,128]{1,0:T(8,128)S(1)} %collective-permute-done.4.refs_0_.refs_3_, ...), custom_call_target="tpu_custom_call" | custom-call | flops 1024 | bytes 1024 | tf_op jit(solution)/shard_map/pallas_call | solution.py:184
  19.9 1.6 %collective-permute-start.10 = (f32[264,128]{1,0:T(8,128)S(1)}, f32[264,128]{1,0:T(8,128)S(1)}, u32[]{:S(2)}, u32[]{:S(2)}) collective-permute-start(f32[264,128]{1,0:T(8,128)S(1)} %shard_map.114.refs_3_), channel_id=1, source_target_pairs={{0,6},{1,7},{2,4},{3,5},{4,2},{5,3},{6,0},{7,1},{8,14},{9,15},{10,... | collective-permute-start | bytes 405512 | tf_op jit(solution)/shard_map/ppermute | solution.py:213
  21.9 1.5 %collective-permute-start.12 = (f32[264,128]{1,0:T(8,128)S(1)}, f32[264,128]{1,0:T(8,128)S(1)}, u32[]{:S(2)}, u32[]{:S(2)}) collective-permute-start(f32[264,128]{1,0:T(8,128)S(1)} %shard_map.114.refs_3_), channel_id=1, source_target_pairs={{0,2},{1,3},{2,0},{3,1},{4,6},{5,7},{6,4},{7,5},{8,10},{9,11},{10,... | collective-permute-start | bytes 405512 | tf_op jit(solution)/shard_map/ppermute | solution.py:213
  23.4 1.7 %collective-permute-start.2 = (f32[256,128]{1,0:T(8,128)S(1)}, f32[256,128]{1,0:T(8,128)S(1)}, u32[]{:S(2)}, u32[]{:S(2)}) collective-permute-start(f32[256,128]{1,0:T(8,128)S(1)} %get-tuple-element.25.refs_2_), channel_id=1, source_target_pairs={{0,8},{1,9},{2,10},{3,11},{4,12},{5,13},{6,14},{7,15},{8,0},{9,1},... | collective-permute-start | bytes 393224 | tf_op jit(solution)/shard_map/ppermute | solution.py:213
  25.2 2.1 %collective-permute-done.refs_0_.refs_1_.refs_4_ = f32[272,128]{1,0:T(8,128)S(1)} collective-permute-done((f32[272,128]{1,0:T(8,128)S(1)}, f32[272,128]{1,0:T(8,128)S(1)}, u32[]{:S(2)}, u32[]{:S(2)}) %collective-permute-start) | collective-permute-done | bytes 139296 | tf_op jit(solution)/shard_map/ppermute | solution.py:213
  27.4 2.7 %collective-permute-done.2.refs_2_.refs_5_ = f32[256,128]{1,0:T(8,128)S(1)} collective-permute-done((f32[256,128]{1,0:T(8,128)S(1)}, f32[256,128]{1,0:T(8,128)S(1)}, u32[]{:S(2)}, u32[]{:S(2)}) %collective-permute-start.2) | collective-permute-done | bytes 131104 | tf_op jit(solution)/shard_map/ppermute | solution.py:213
  30.1 2.7 %collective-permute-done.1.refs_0_.refs_3_ = f32[256,128]{1,0:T(8,128)S(1)} collective-permute-done((f32[256,128]{1,0:T(8,128)S(1)}, f32[256,128]{1,0:T(8,128)S(1)}, u32[]{:S(2)}, u32[]{:S(2)}) %collective-permute-start.1) | collective-permute-done | bytes 131104 | tf_op jit(solution)/shard_map/ppermute | solution.py:213
  33.0 1.9 %collective-permute-done.13.refs_1_ = f32[1024,128]{1,0:T(8,128)S(1)} collective-permute-done((f32[1024,128]{1,0:T(8,128)S(1)}, f32[1024,128]{1,0:T(8,128)S(1)}, u32[]{:S(2)}, u32[]{:S(2)}) %collective-permute-start.13) | collective-permute-done | bytes 524320 | tf_op jit(solution)/shard_map/ppermute | solution.py:213
  34.9 0.7 %shard_map.116 = (f32[264,128]{1,0:T(8,128)S(1)}, f32[128,128]{1,0:T(8,128)S(1)}, f32[128,128]{1,0:T(8,128)S(1)}) custom-call(f32[1024,128]{1,0:T(8,128)S(1)} %shard_map.115.refs_0_, f32[1024,128]{1,0:T(8,128)S(1)} %collective-permute-done.13.refs_1_, f32[256,128]{1,0:T(8,128)S(1)} %get-tuple-element.25.refs_2_, ...), custom_call_target="tpu_custom_call" | custom-call | flops 1024 | bytes 1024 | tf_op jit(solution)/shard_map/pallas_call | solution.py:184
  35.5 0.6 %collective-permute-start.14 = (f32[128,128]{1,0:T(8,128)S(1)}, f32[128,128]{1,0:T(8,128)S(1)}, u32[]{:S(2)}, u32[]{:S(2)}) collective-permute-start(f32[128,128]{1,0:T(8,128)S(1)} %get-tuple-element.31.refs_3_), channel_id=1, source_target_pairs={{0,2},{1,3},{2,0},{3,1},{4,16},{5,17},{6,24},{7,25},{8,10},{9,11},... | collective-permute-start | bytes 196616 | tf_op jit(solution)/shard_map/ppermute | solution.py:213
  36.1 0.6 %collective-permute-start.15 = (f32[128,128]{1,0:T(8,128)S(1)}, f32[128,128]{1,0:T(8,128)S(1)}, u32[]{:S(2)}, u32[]{:S(2)}) collective-permute-start(f32[128,128]{1,0:T(8,128)S(1)} %get-tuple-element.32), channel_id=1, source_target_pairs={{0,1},{1,0},{2,9},{3,8},{4,17},{5,16},{6,25},{7,24},{8,3},{9,2},{1... | collective-permute-start | bytes 196616 | tf_op jit(solution)/shard_map/ppermute | solution.py:213
  36.7 0.7 %collective-permute-start.17 = (f32[128,128]{1,0:T(8,128)S(1)}, f32[128,128]{1,0:T(8,128)S(1)}, u32[]{:S(2)}, u32[]{:S(2)}) collective-permute-start(f32[128,128]{1,0:T(8,128)S(1)} %get-tuple-element.32), channel_id=1, source_target_pairs={{0,1},{1,0},{2,3},{3,2},{4,5},{5,4},{6,7},{7,6},{8,9},{9,8},{10,11... | collective-permute-start | bytes 196616 | tf_op jit(solution)/shard_map/ppermute | solution.py:213
  37.3 2.6 %collective-permute-done.14.refs_0_ = f32[128,128]{1,0:T(8,128)S(1)} collective-permute-done((f32[128,128]{1,0:T(8,128)S(1)}, f32[128,128]{1,0:T(8,128)S(1)}, u32[]{:S(2)}, u32[]{:S(2)}) %collective-permute-start.14) | collective-permute-done | bytes 65568 | tf_op jit(solution)/shard_map/ppermute | solution.py:213
  39.9 1.3 %collective-permute-start.16 = (f32[128,128]{1,0:T(8,128)S(1)}, f32[128,128]{1,0:T(8,128)S(1)}, u32[]{:S(2)}, u32[]{:S(2)}) collective-permute-start(f32[128,128]{1,0:T(8,128)S(1)} %collective-permute-done.14.refs_0_), channel_id=1, source_target_pairs={{0,8},{1,9},{10,2},{11,3},{20,28},{21,29},{30,22},{31,23}} | collective-permute-start | bytes 196616 | tf_op jit(solution)/shard_map/ppermute | solution.py:213
  41.2 5.8 %collective-permute-done.15.refs_1_ = f32[128,128]{1,0:T(8,128)S(1)} collective-permute-done((f32[128,128]{1,0:T(8,128)S(1)}, f32[128,128]{1,0:T(8,128)S(1)}, u32[]{:S(2)}, u32[]{:S(2)}) %collective-permute-start.15) | collective-permute-done | bytes 65568 | tf_op jit(solution)/shard_map/ppermute | solution.py:213
  47.0 1.0 %shard_map.117 = f32[1,8,4096]{2,1,0:T(8,128)} custom-call(s32[1,8]{1,0:T(1,128)S(1)} %get-tuple-element.19.xp.places, s32[1,1]{1,0:T(1,128)S(6)} %copy.15.xc.count, f32[264,128]{1,0:T(8,128)S(1)} %get-tuple-element.30.x, f32[128,128]{1,0:T(8,128)S(1)} %collective-permute-done.14.refs_0_, f32[128,128]{1,0:T(8,128)S(1)} %collective-permute-done.15.refs_1_, ...), custom_call_target="tpu_custom_call" | custom-call | flops 1024 | bytes 1024 | tf_op jit(solution)/shard_map/pallas_call | solution.py:184
  (21 shorter events, 2.3 us)
Async XLA Ops:
  1.9 10.1 %collective-permute-start.3 = (f32[272,128]{1,0:T(8,128)S(1)}, f32[272,128]{1,0:T(8,128)S(1)}, u32[]{:S(2)}, u32[]{:S(2)}) collective-permute-start(f32[272,128]{1,0:T(8,128)S(1)} %get-tuple-element.26), channel_id=1, source_target_pairs={{0,16},{1,17},{2,18},{3,19},{4,20},{5,21},{6,22},{7,23},{8,24},{9,... | collective-permute-start | bytes 417800 | tf_op jit(solution)/shard_map/ppermute | solution.py:213
  4.5 12.6 %collective-permute-start.5 = (f32[272,128]{1,0:T(8,128)S(1)}, f32[272,128]{1,0:T(8,128)S(1)}, u32[]{:S(2)}, u32[]{:S(2)}) collective-permute-start(f32[272,128]{1,0:T(8,128)S(1)} %get-tuple-element.26), channel_id=1, source_target_pairs={{0,8},{1,9},{2,10},{3,11},{4,12},{5,13},{6,14},{7,15},{8,0},{9,1},... | collective-permute-start | bytes 417800 | tf_op jit(solution)/shard_map/ppermute | solution.py:213
  8.4 7.2 %collective-permute-start.6 = (f32[264,128]{1,0:T(8,128)S(1)}, f32[264,128]{1,0:T(8,128)S(1)}, u32[]{:S(2)}, u32[]{:S(2)}) collective-permute-start(f32[264,128]{1,0:T(8,128)S(1)} %get-tuple-element.27.refs_3_), channel_id=1, source_target_pairs={{0,6},{1,7},{2,4},{3,5},{4,2},{5,3},{6,0},{7,1},{8,14},{9,15},{10,... | collective-permute-start | bytes 405512 | tf_op jit(solution)/shard_map/ppermute | solution.py:213
  10.0 7.1 %collective-permute-start.7 = (f32[264,128]{1,0:T(8,128)S(1)}, f32[264,128]{1,0:T(8,128)S(1)}, u32[]{:S(2)}, u32[]{:S(2)}) collective-permute-start(f32[264,128]{1,0:T(8,128)S(1)} %get-tuple-element.27.refs_3_), channel_id=1, source_target_pairs={{0,4},{1,5},{2,6},{3,7},{4,0},{5,1},{6,2},{7,3},{8,12},{9,13},{10,... | collective-permute-start | bytes 405512 | tf_op jit(solution)/shard_map/ppermute | solution.py:213
  10.5 6.7 %collective-permute-start.8 = (f32[264,128]{1,0:T(8,128)S(1)}, f32[264,128]{1,0:T(8,128)S(1)}, u32[]{:S(2)}, u32[]{:S(2)}) collective-permute-start(f32[264,128]{1,0:T(8,128)S(1)} %get-tuple-element.27.refs_3_), channel_id=1, source_target_pairs={{0,2},{1,3},{2,0},{3,1},{4,6},{5,7},{6,4},{7,5},{8,10},{9,11},{10,... | collective-permute-start | bytes 405512 | tf_op jit(solution)/shard_map/ppermute | solution.py:213
  12.0 5.2 %collective-permute-start.4 = (f32[256,128]{1,0:T(8,128)S(1)}, f32[256,128]{1,0:T(8,128)S(1)}, u32[]{:S(2)}, u32[]{:S(2)}) collective-permute-start(f32[256,128]{1,0:T(8,128)S(1)} %shard_map.112), channel_id=1, source_target_pairs={{0,8},{1,9},{2,10},{3,11},{4,12},{5,13},{6,14},{7,15},{8,0},{9,1},... | collective-permute-start | bytes 393224 | tf_op jit(solution)/shard_map/ppermute | solution.py:213
  17.2 2.1 %collective-permute-start.9 = (f32[1024,128]{1,0:T(8,128)S(1)}, f32[1024,128]{1,0:T(8,128)S(1)}, u32[]{:S(2)}, u32[]{:S(2)}) collective-permute-start(f32[1024,128]{1,0:T(8,128)S(1)} %shard_map.113.refs_0_), channel_id=1, source_target_pairs={{0,1},{1,0},{2,3},{3,2},{4,5},{5,4},{6,7},{7,6},{8,9},{9,8},{10,11... | collective-permute-start | bytes 1572872 | tf_op jit(solution)/shard_map/ppermute | solution.py:213
  17.2 10.1 %collective-permute-start = (f32[272,128]{1,0:T(8,128)S(1)}, f32[272,128]{1,0:T(8,128)S(1)}, u32[]{:S(2)}, u32[]{:S(2)}) collective-permute-start(f32[272,128]{1,0:T(8,128)S(1)} %get-tuple-element.24), channel_id=1, source_target_pairs={{0,16},{1,17},{2,18},{3,19},{4,20},{5,21},{6,22},{7,23},{8,24},{9,... | collective-permute-start | bytes 417800 | tf_op jit(solution)/shard_map/ppermute | solution.py:213
  19.9 13.0 %collective-permute-start.10 = (f32[264,128]{1,0:T(8,128)S(1)}, f32[264,128]{1,0:T(8,128)S(1)}, u32[]{:S(2)}, u32[]{:S(2)}) collective-permute-start(f32[264,128]{1,0:T(8,128)S(1)} %shard_map.114.refs_3_), channel_id=1, source_target_pairs={{0,6},{1,7},{2,4},{3,5},{4,2},{5,3},{6,0},{7,1},{8,14},{9,15},{10,... | collective-permute-start | bytes 405512 | tf_op jit(solution)/shard_map/ppermute | solution.py:213
  21.4 11.4 %collective-permute-start.11 = (f32[264,128]{1,0:T(8,128)S(1)}, f32[264,128]{1,0:T(8,128)S(1)}, u32[]{:S(2)}, u32[]{:S(2)}) collective-permute-start(f32[264,128]{1,0:T(8,128)S(1)} %shard_map.114.refs_3_), channel_id=1, source_target_pairs={{0,4},{1,5},{2,6},{3,7},{4,0},{5,1},{6,2},{7,3},{8,12},{9,13},{10,... | collective-permute-start | bytes 405512 | tf_op jit(solution)/shard_map/ppermute | solution.py:213
  21.9 10.9 %collective-permute-start.12 = (f32[264,128]{1,0:T(8,128)S(1)}, f32[264,128]{1,0:T(8,128)S(1)}, u32[]{:S(2)}, u32[]{:S(2)}) collective-permute-start(f32[264,128]{1,0:T(8,128)S(1)} %shard_map.114.refs_3_), channel_id=1, source_target_pairs={{0,2},{1,3},{2,0},{3,1},{4,6},{5,7},{6,4},{7,5},{8,10},{9,11},{10,... | collective-permute-start | bytes 405512 | tf_op jit(solution)/shard_map/ppermute | solution.py:213
  23.4 6.7 %collective-permute-start.2 = (f32[256,128]{1,0:T(8,128)S(1)}, f32[256,128]{1,0:T(8,128)S(1)}, u32[]{:S(2)}, u32[]{:S(2)}) collective-permute-start(f32[256,128]{1,0:T(8,128)S(1)} %get-tuple-element.25.refs_2_), channel_id=1, source_target_pairs={{0,8},{1,9},{2,10},{3,11},{4,12},{5,13},{6,14},{7,15},{8,0},{9,1},... | collective-permute-start | bytes 393224 | tf_op jit(solution)/shard_map/ppermute | solution.py:213
  27.3 5.5 %collective-permute-start.1 = (f32[256,128]{1,0:T(8,128)S(1)}, f32[256,128]{1,0:T(8,128)S(1)}, u32[]{:S(2)}, u32[]{:S(2)}) collective-permute-start(f32[256,128]{1,0:T(8,128)S(1)} %shard_map.111), channel_id=1, source_target_pairs={{0,8},{1,9},{2,10},{3,11},{4,12},{5,13},{6,14},{7,15},{8,0},{9,1},... | collective-permute-start | bytes 393224 | tf_op jit(solution)/shard_map/ppermute | solution.py:213
  32.9 2.0 %collective-permute-start.13 = (f32[1024,128]{1,0:T(8,128)S(1)}, f32[1024,128]{1,0:T(8,128)S(1)}, u32[]{:S(2)}, u32[]{:S(2)}) collective-permute-start(f32[1024,128]{1,0:T(8,128)S(1)} %shard_map.115.refs_0_), channel_id=1, source_target_pairs={{0,1},{1,0},{2,3},{3,2},{4,5},{5,4},{6,7},{7,6},{8,9},{9,8},{10,11... | collective-permute-start | bytes 1572872 | tf_op jit(solution)/shard_map/ppermute | solution.py:213
  35.5 4.3 %collective-permute-start.14 = (f32[128,128]{1,0:T(8,128)S(1)}, f32[128,128]{1,0:T(8,128)S(1)}, u32[]{:S(2)}, u32[]{:S(2)}) collective-permute-start(f32[128,128]{1,0:T(8,128)S(1)} %get-tuple-element.31.refs_3_), channel_id=1, source_target_pairs={{0,2},{1,3},{2,0},{3,1},{4,16},{5,17},{6,24},{7,25},{8,10},{9,11},... | collective-permute-start | bytes 196616 | tf_op jit(solution)/shard_map/ppermute | solution.py:213
  36.1 10.9 %collective-permute-start.15 = (f32[128,128]{1,0:T(8,128)S(1)}, f32[128,128]{1,0:T(8,128)S(1)}, u32[]{:S(2)}, u32[]{:S(2)}) collective-permute-start(f32[128,128]{1,0:T(8,128)S(1)} %get-tuple-element.32), channel_id=1, source_target_pairs={{0,1},{1,0},{2,9},{3,8},{4,17},{5,16},{6,25},{7,24},{8,3},{9,2},{1... | collective-permute-start | bytes 196616 | tf_op jit(solution)/shard_map/ppermute | solution.py:213
  36.7 10.3 %collective-permute-start.17 = (f32[128,128]{1,0:T(8,128)S(1)}, f32[128,128]{1,0:T(8,128)S(1)}, u32[]{:S(2)}, u32[]{:S(2)}) collective-permute-start(f32[128,128]{1,0:T(8,128)S(1)} %get-tuple-element.32), channel_id=1, source_target_pairs={{0,1},{1,0},{2,3},{3,2},{4,5},{5,4},{6,7},{7,6},{8,9},{9,8},{10,11... | collective-permute-start | bytes 196616 | tf_op jit(solution)/shard_map/ppermute | solution.py:213
  39.9 7.1 %collective-permute-start.16 = (f32[128,128]{1,0:T(8,128)S(1)}, f32[128,128]{1,0:T(8,128)S(1)}, u32[]{:S(2)}, u32[]{:S(2)}) collective-permute-start(f32[128,128]{1,0:T(8,128)S(1)} %collective-permute-done.14.refs_0_), channel_id=1, source_target_pairs={{0,8},{1,9},{10,2},{11,3},{20,28},{21,29},{30,22},{31,23}} | collective-permute-start | bytes 196616 | tf_op jit(solution)/shard_map/ppermute | solution.py:213

commit v5 on v4

--- a/solution.py
+++ b/solution.py
@@ -99,43 +99,53 @@
         refs[-1][i * rows : (i + 1) * rows, :] = ref[:rows, :]
 
 
+def parted_kernel(x, *outs):
+    rows = outs[0].shape[0]
+    for i, out in enumerate(outs):
+        out[...] = x[i * rows : (i + 1) * rows, :]
+
+
 def split(x):
     high = x.astype(jnp.bfloat16)
     return high, (x - high.astype(jnp.float32)).astype(jnp.bfloat16)
 
 
-def dot3(a, b_high, b_low):
-    a_high, a_low = split(a)
-    dot = functools.partial(jnp.dot, preferred_element_type=jnp.float32)
-    return dot(a_high, b_high) + (dot(a_high, b_low) + dot(a_low, b_high))
-
-
-def product_kernel(along, across, sends, *refs):
-    got, shared, b_own = refs[:3]
-    b_got = refs[3 : 3 + len(along)]
-    mask, out = refs[3 + len(along) :][:2]
-    sent = refs[5 + len(along) : -2]
-    high, low = refs[-2:]
+def product_kernel(along, across, shares, waits, *refs):
+    got, shared, b_own = refs[0], refs[1 : 1 + shares], refs[1 + shares]
+    refs = refs[2 + shares :]
+    b_got, mask, out = refs[: len(along)], refs[len(along)], refs[len(along) + 1 + waits]
+    sent, both = refs[len(along) + 2 + waits : -1], refs[-1]
     row, chip, core = position()
     rows = b_own.shape[0]
     for offset, ref in zip([0] + along, (b_own,) + b_got):
         at = pl.ds(pl.multiple_of((row ^ offset) * rows, rows), rows)
-        high[at, :], low[at, :] = split(ref[:rows, :])
-    acc = None
-    for i, offset in enumerate([0] + across):
-        for side in range(2):
-            ref = (got, shared)[side]
-            start = i * rows
-            column = 2 * (chip ^ offset) + (core ^ side)
-            at = pl.ds(pl.multiple_of(column * LANES, LANES), LANES)
-            term = dot3(ref[start : start + rows, :], high[at, :], low[at, :])
-            acc = term if acc is None else acc + term
-    for pair in range(rows // BS):
-        at = slice(pair * BS, (pair + 1) * BS)
-        out[at, :] = acc[at, :] * mask[pair : pair + 1, :]
+        both[at, :LANES], both[at, LANES:] = split(ref[:rows, :])
+    dot = functools.partial(jnp.dot, preferred_element_type=jnp.float32)
+
+    def multiply(left, right):
+        wide, narrow = None, None
+
+        def piece(refs, i):
+            per = (1 + len(across)) // len(refs)
+            return refs[i // per][i % per * rows : (i % per + 1) * rows, :]
+
+        for i, offset in enumerate([0] + across):
+            at = pl.ds(pl.multiple_of((chip ^ offset) * 2 * LANES, 2 * LANES), 2 * LANES)
+            a = jnp.concatenate([piece(left, i), piece(right, i)], axis=1)
+            a_high, a_low = split(a)
+            terms = dot(a_high, both[at, :]), dot(a_low, both[at, :LANES])
+            wide = terms[0] if wide is None else wide + terms[0]
+            narrow = terms[1] if narrow is None else narrow + terms[1]
+        acc = wide[:, :LANES] + (wide[:, LANES:] + narrow)
+        for pair in range(rows // BS):
+            at = slice(pair * BS, (pair + 1) * BS)
+            out[at, :] = acc[at, :] * mask[pair : pair + 1, :]
+
+    pl.when(core == 0)(lambda: multiply([got], shared))
+    pl.when(core == 1)(lambda: multiply(shared, [got]))
     fill(out, rows)
     for turn, ref in enumerate(sent):
-        part = lax.rem(2 * chip + core + turn, sends)
+        part = lax.rem(2 * chip + core + turn, len(sent))
         ref[...] = out[pl.ds(pl.multiple_of(part * LANES, LANES), LANES), :]
 
 
@@ -267,26 +277,34 @@
             got[offset] = send(value, lambda r, m, k: (r ^ low, m, k))
         return [got[offset] for offset in along]
 
+    def parted(x, count):
+        return call(
+            parted_kernel, [tile] * count, [VMEM], [], 1 << 10, x
+        )
+
     def in_plane(x):
         return [send(x, lambda r, m, k, o=o: (r, m ^ o, k)) for o in across]
 
-    def product(a_got, b, b_got, parts):
+    def product(a_got, a_shared, b, b_got, parts, *waits):
         part = jax.ShapeDtypeStruct((LANES, LANES), f32)
         return call(
-            functools.partial(product_kernel, along, across, sends),
+            functools.partial(product_kernel, along, across, len(a_shared), len(waits)),
             [longer] + [part] * parts,
-            [VMEM] * (4 + len(b_got)),
-            [pltpu.VMEM((order, LANES), jnp.bfloat16)] * 2,
+            [VMEM] * (3 + len(a_shared) + len(b_got))
+            + [pl.BlockSpec(memory_space=pl.ANY)] * len(waits),
+            [pltpu.VMEM((order, 2 * LANES), jnp.bfloat16)],
             2 * 3 * rows * order * LANES,
-            a_got, to_other(a_got), b, *b_got, mask,
+            a_got, *a_shared, b, *b_got, mask, *waits,
         )
 
-    p_got = along_z(p_far, p_far)
-    h_got = stack([h_tile] + in_plane(h_tile), *p_got)
-    (y,) = product(h_got, p_near, p_got, 0)
-    s_got = along_z(s_near, s_far)
+    p_got = along_z(p_near, p_far)
+    s_got = along_z(s_far, s_far)
+    h_parts = [h_tile] + in_plane(h_tile)
+    h_got = stack(h_parts, *p_got[::-1])
+    h_shared = [to_other(x) for x in parted(h_got, len(h_parts))]
+    (y,) = product(h_got, h_shared, p_near, p_got, 0, s_got[along.index(row_count // 2)])
     y_got = stack([y] + in_plane(y), *s_got)
-    x, *sent = product(y_got, s_near, s_got, sends)
+    x, *sent = product(y_got, [to_other(y_got)], s_near, s_got, sends)
 
     relay = row_count == chip_count == 4
 

time: 48.4 us -> 47.6 us (0.983)
  waiting for transfers between devices: 22.5 us -> 18.7 us
  starting transfers between devices: 18.8 us -> 22 us
    ppermute x18 -> x21, waiting for transfers between devices: 22.5 us -> 18.7 us  [send(): return lax.ppermute(value, AXES, pairs)]
    ppermute x18 -> x21, starting transfers between devices: 18.8 us -> 22 us  [send(): return lax.ppermute(value, AXES, pairs)]
    pallas_call x9 -> x10, Pallas kernels: 3.96 us -> 3.77 us  [call(): pl.pallas_call(kernel, out_shape=out_shapes, in_specs=in_specs, out_specs...]
  transfers between devices with their start and end apart: 18 -> 21, of which waited for: 9 -> 11; matrix products, arithmetic and copies ran while one was open for 0% -> 0% of each run, Pallas kernels for 2% -> 2%
where the time goes in v5:
time: 47.6 us; the launch traced here: 47.1 us
  starting transfers between devices  22 us (46%)
  waiting for transfers between devices  18.7 us (39%)
  Pallas kernels  3.77 us (8%)
  between operations  2.7 us (6%)
    ppermute x21, starting transfers between devices, send(): return lax.ppermute(value, AXES, pairs)  22 us
    ppermute x21, waiting for transfers between devices, send(): return lax.ppermute(value, AXES, pairs)  18.7 us
    pallas_call x10, Pallas kernels, call(): pl.pallas_call(kernel, out_shape=out_shapes, in_specs=in_specs, out_specs...  3.77 us
  transfers between devices with their start and end apart: 21, of which 11 were waited for; matrix products, arithmetic and copies ran while one was open for 0% of the time, Pallas kernels for 2%

profile of v5, /device:TPU:2, one launch (start us, length us, event | category | flops | bytes accessed | tf_op | source)
XLA Modules:
  0.0 47.1 jit_solution(10490334481885975546)
XLA Ops:
  0.7 1.2 %shard_map.109 = (f32[256,128]{1,0:T(8,128)S(1)}, f32[272,128]{1,0:T(8,128)S(1)}, f32[1,8,4096]{2,1,0:T(8,128)S(1)}, f32[1,8,4096]{2,1,0:T(8,128)S(1)}, s32[1,8]...) custom-call(s32[1,1]{1,0:T(1,128)S(6)} %copy.13.count, s32[1,8]{1,0:T(1,128)} %refs_0_.1, ...), custom_call_target="tpu_custom_call" | custom-call | flops 1024 | bytes 1024 | tf_op jit(solution)/shard_map/pallas_call | solution.py:194
  1.9 2.7 %collective-permute-start.4 = (f32[272,128]{1,0:T(8,128)S(1)}, f32[272,128]{1,0:T(8,128)S(1)}, u32[]{:S(2)}, u32[]{:S(2)}) collective-permute-start(f32[272,128]{1,0:T(8,128)S(1)} %get-tuple-element.30), channel_id=1, source_target_pairs={{0,16},{1,17},{2,18},{3,19},{4,20},{5,21},{6,22},{7,23},{8,24},{9,... | collective-permute-start | bytes 417800 | tf_op jit(solution)/shard_map/ppermute | solution.py:223
  4.5 1.6 %collective-permute-start.3 = (f32[256,128]{1,0:T(8,128)S(1)}, f32[256,128]{1,0:T(8,128)S(1)}, u32[]{:S(2)}, u32[]{:S(2)}) collective-permute-start(f32[256,128]{1,0:T(8,128)S(1)} %get-tuple-element.29.refs_5_), channel_id=1, source_target_pairs={{0,8},{1,9},{2,10},{3,11},{4,12},{5,13},{6,14},{7,15},{8,0},{9,1},... | collective-permute-start | bytes 393224 | tf_op jit(solution)/shard_map/ppermute | solution.py:223
  8.4 1.6 %collective-permute-start.6 = (f32[264,128]{1,0:T(8,128)S(1)}, f32[264,128]{1,0:T(8,128)S(1)}, u32[]{:S(2)}, u32[]{:S(2)}) collective-permute-start(f32[264,128]{1,0:T(8,128)S(1)} %get-tuple-element.31.refs_3_), channel_id=1, source_target_pairs={{0,6},{1,7},{2,4},{3,5},{4,2},{5,3},{6,0},{7,1},{8,14},{9,15},{10,... | collective-permute-start | bytes 405512 | tf_op jit(solution)/shard_map/ppermute | solution.py:223
  10.5 1.5 %collective-permute-start.8 = (f32[264,128]{1,0:T(8,128)S(1)}, f32[264,128]{1,0:T(8,128)S(1)}, u32[]{:S(2)}, u32[]{:S(2)}) collective-permute-start(f32[264,128]{1,0:T(8,128)S(1)} %get-tuple-element.31.refs_3_), channel_id=1, source_target_pairs={{0,2},{1,3},{2,0},{3,1},{4,6},{5,7},{6,4},{7,5},{8,10},{9,11},{10,... | collective-permute-start | bytes 405512 | tf_op jit(solution)/shard_map/ppermute | solution.py:223
  12.5 2.9 %collective-permute-start = (f32[272,128]{1,0:T(8,128)S(1)}, f32[272,128]{1,0:T(8,128)S(1)}, u32[]{:S(2)}, u32[]{:S(2)}) collective-permute-start(f32[272,128]{1,0:T(8,128)S(1)} %get-tuple-element.28), channel_id=1, source_target_pairs={{0,16},{1,17},{2,18},{3,19},{4,20},{5,21},{6,22},{7,23},{8,24},{9,... | collective-permute-start | bytes 417800 | tf_op jit(solution)/shard_map/ppermute | solution.py:223
  15.6 1.4 %collective-permute-done.7.refs_5_ = f32[264,128]{1,0:T(8,128)S(1)} collective-permute-done((f32[264,128]{1,0:T(8,128)S(1)}, f32[264,128]{1,0:T(8,128)S(1)}, u32[]{:S(2)}, u32[]{:S(2)}) %collective-permute-start.7) | collective-permute-done | bytes 135200 | tf_op jit(solution)/shard_map/ppermute | solution.py:223
  17.1 2.5 %collective-permute-done.5.refs_2_.refs_6_ = f32[256,128]{1,0:T(8,128)S(1)} collective-permute-done((f32[256,128]{1,0:T(8,128)S(1)}, f32[256,128]{1,0:T(8,128)S(1)}, u32[]{:S(2)}, u32[]{:S(2)}) %collective-permute-start.5) | collective-permute-done | bytes 131104 | tf_op jit(solution)/shard_map/ppermute | solution.py:223
  20.8 1.2 %collective-permute-done.refs_0_.refs_10_.refs_1_.refs_4_ = f32[272,128]{1,0:T(8,128)S(1)} collective-permute-done((f32[272,128]{1,0:T(8,128)S(1)}, f32[272,128]{1,0:T(8,128)S(1)}, u32[]{:S(2)}, u32[]{:S(2)}) %collective-permute-start) | collective-permute-done | bytes 139296 | tf_op jit(solution)/shard_map/ppermute | solution.py:223
  22.1 0.5 %shard_map.115.refs_3_ = f32[264,128]{1,0:T(8,128)S(1)} custom-call(f32[1024,128]{1,0:T(8,128)S(1)} %shard_map.113.x.refs_0_, f32[256,128]{1,0:T(8,128)S(1)} %collective-permute-done.9.refs_1_, f32[256,128]{1,0:T(8,128)S(1)} %collective-permute-done.10.refs_2_, f32[256,128]{1,0:T(8,128)S(1)} %collective-permute-done.11.refs_3_, ...), custom_call_target="tpu_custom_call" | custom-call | flops 1024 | bytes 1024 | tf_op jit(solution)/shard_map/pallas_call | solution.py:194
  22.7 1.6 %collective-permute-start.13 = (f32[264,128]{1,0:T(8,128)S(1)}, f32[264,128]{1,0:T(8,128)S(1)}, u32[]{:S(2)}, u32[]{:S(2)}) collective-permute-start(f32[264,128]{1,0:T(8,128)S(1)} %shard_map.115.refs_3_), channel_id=1, source_target_pairs={{0,6},{1,7},{2,4},{3,5},{4,2},{5,3},{6,0},{7,1},{8,14},{9,15},{10,... | collective-permute-start | bytes 405512 | tf_op jit(solution)/shard_map/ppermute | solution.py:223
  24.8 1.5 %collective-permute-start.15 = (f32[264,128]{1,0:T(8,128)S(1)}, f32[264,128]{1,0:T(8,128)S(1)}, u32[]{:S(2)}, u32[]{:S(2)}) collective-permute-start(f32[264,128]{1,0:T(8,128)S(1)} %shard_map.115.refs_3_), channel_id=1, source_target_pairs={{0,2},{1,3},{2,0},{3,1},{4,6},{5,7},{6,4},{7,5},{8,10},{9,11},{10,... | collective-permute-start | bytes 405512 | tf_op jit(solution)/shard_map/ppermute | solution.py:223
  26.3 1.9 %collective-permute-start.1 = (f32[256,128]{1,0:T(8,128)S(1)}, f32[256,128]{1,0:T(8,128)S(1)}, u32[]{:S(2)}, u32[]{:S(2)}) collective-permute-start(f32[256,128]{1,0:T(8,128)S(1)} %shard_map.111), channel_id=1, source_target_pairs={{0,8},{1,9},{2,10},{3,11},{4,12},{5,13},{6,14},{7,15},{8,0},{9,1},... | collective-permute-start | bytes 393224 | tf_op jit(solution)/shard_map/ppermute | solution.py:223
  28.2 3.1 %collective-permute-done.1.refs_0_.refs_3_ = f32[256,128]{1,0:T(8,128)S(1)} collective-permute-done((f32[256,128]{1,0:T(8,128)S(1)}, f32[256,128]{1,0:T(8,128)S(1)}, u32[]{:S(2)}, u32[]{:S(2)}) %collective-permute-start.1) | collective-permute-done | bytes 131104 | tf_op jit(solution)/shard_map/ppermute | solution.py:223
  31.3 0.7 %collective-permute-done.14.refs_5_ = f32[264,128]{1,0:T(8,128)S(1)} collective-permute-done((f32[264,128]{1,0:T(8,128)S(1)}, f32[264,128]{1,0:T(8,128)S(1)}, u32[]{:S(2)}, u32[]{:S(2)}) %collective-permute-start.14) | collective-permute-done | bytes 135200 | tf_op jit(solution)/shard_map/ppermute | solution.py:223
  32.2 1.9 %collective-permute-done.16.refs_1_ = f32[1024,128]{1,0:T(8,128)S(1)} collective-permute-done((f32[1024,128]{1,0:T(8,128)S(1)}, f32[1024,128]{1,0:T(8,128)S(1)}, u32[]{:S(2)}, u32[]{:S(2)}) %collective-permute-start.16) | collective-permute-done | bytes 524320 | tf_op jit(solution)/shard_map/ppermute | solution.py:223
  34.1 0.6 %shard_map.117 = (f32[264,128]{1,0:T(8,128)S(1)}, f32[128,128]{1,0:T(8,128)S(1)}, f32[128,128]{1,0:T(8,128)S(1)}) custom-call(f32[1024,128]{1,0:T(8,128)S(1)} %shard_map.116.refs_0_, f32[1024,128]{1,0:T(8,128)S(1)} %collective-permute-done.16.refs_1_, f32[256,128]{1,0:T(8,128)S(1)} %get-tuple-element.37.refs_2_, ...), custom_call_target="tpu_custom_call" | custom-call | flops 1024 | bytes 1024 | tf_op jit(solution)/shard_map/pallas_call | solution.py:194
  34.7 0.6 %collective-permute-start.17 = (f32[128,128]{1,0:T(8,128)S(1)}, f32[128,128]{1,0:T(8,128)S(1)}, u32[]{:S(2)}, u32[]{:S(2)}) collective-permute-start(f32[128,128]{1,0:T(8,128)S(1)} %get-tuple-element.39.refs_3_), channel_id=1, source_target_pairs={{0,2},{1,3},{2,0},{3,1},{4,16},{5,17},{6,24},{7,25},{8,10},{9,11},... | collective-permute-start | bytes 196616 | tf_op jit(solution)/shard_map/ppermute | solution.py:223
  35.2 1.5 %collective-permute-start.18 = (f32[128,128]{1,0:T(8,128)S(1)}, f32[128,128]{1,0:T(8,128)S(1)}, u32[]{:S(2)}, u32[]{:S(2)}) collective-permute-start(f32[128,128]{1,0:T(8,128)S(1)} %get-tuple-element.40), channel_id=1, source_target_pairs={{0,1},{1,0},{2,9},{3,8},{4,17},{5,16},{6,25},{7,24},{8,3},{9,2},{1... | collective-permute-start | bytes 196616 | tf_op jit(solution)/shard_map/ppermute | solution.py:223
  36.7 0.7 %collective-permute-start.20 = (f32[128,128]{1,0:T(8,128)S(1)}, f32[128,128]{1,0:T(8,128)S(1)}, u32[]{:S(2)}, u32[]{:S(2)}) collective-permute-start(f32[128,128]{1,0:T(8,128)S(1)} %get-tuple-element.40), channel_id=1, source_target_pairs={{0,1},{1,0},{2,3},{3,2},{4,5},{5,4},{6,7},{7,6},{8,9},{9,8},{10,11... | collective-permute-start | bytes 196616 | tf_op jit(solution)/shard_map/ppermute | solution.py:223
  37.4 1.6 %collective-permute-done.17.refs_0_ = f32[128,128]{1,0:T(8,128)S(1)} collective-permute-done((f32[128,128]{1,0:T(8,128)S(1)}, f32[128,128]{1,0:T(8,128)S(1)}, u32[]{:S(2)}, u32[]{:S(2)}) %collective-permute-start.17) | collective-permute-done | bytes 65568 | tf_op jit(solution)/shard_map/ppermute | solution.py:223
  39.0 1.3 %collective-permute-start.19 = (f32[128,128]{1,0:T(8,128)S(1)}, f32[128,128]{1,0:T(8,128)S(1)}, u32[]{:S(2)}, u32[]{:S(2)}) collective-permute-start(f32[128,128]{1,0:T(8,128)S(1)} %collective-permute-done.17.refs_0_), channel_id=1, source_target_pairs={{0,8},{1,9},{10,2},{11,3},{20,28},{21,29},{30,22},{31,23}} | collective-permute-start | bytes 196616 | tf_op jit(solution)/shard_map/ppermute | solution.py:223
  40.3 5.8 %collective-permute-done.18.refs_1_ = f32[128,128]{1,0:T(8,128)S(1)} collective-permute-done((f32[128,128]{1,0:T(8,128)S(1)}, f32[128,128]{1,0:T(8,128)S(1)}, u32[]{:S(2)}, u32[]{:S(2)}) %collective-permute-start.18) | collective-permute-done | bytes 65568 | tf_op jit(solution)/shard_map/ppermute | solution.py:223
  46.1 1.0 %shard_map.118 = f32[1,8,4096]{2,1,0:T(8,128)} custom-call(s32[1,8]{1,0:T(1,128)S(1)} %get-tuple-element.23.xp.places, s32[1,1]{1,0:T(1,128)S(6)} %copy.15.xc.count, f32[264,128]{1,0:T(8,128)S(1)} %get-tuple-element.38.x, f32[128,128]{1,0:T(8,128)S(1)} %collective-permute-done.17.refs_0_, f32[128,128]{1,0:T(8,128)S(1)} %collective-permute-done.18.refs_1_, ...), custom_call_target="tpu_custom_call" | custom-call | flops 1024 | bytes 1024 | tf_op jit(solution)/shard_map/pallas_call | solution.py:194
  (28 shorter events, 3.8 us)
Async XLA Ops:
  1.9 10.1 %collective-permute-start.4 = (f32[272,128]{1,0:T(8,128)S(1)}, f32[272,128]{1,0:T(8,128)S(1)}, u32[]{:S(2)}, u32[]{:S(2)}) collective-permute-start(f32[272,128]{1,0:T(8,128)S(1)} %get-tuple-element.30), channel_id=1, source_target_pairs={{0,16},{1,17},{2,18},{3,19},{4,20},{5,21},{6,22},{7,23},{8,24},{9,... | collective-permute-start | bytes 417800 | tf_op jit(solution)/shard_map/ppermute | solution.py:223
  4.5 8.0 %collective-permute-start.3 = (f32[256,128]{1,0:T(8,128)S(1)}, f32[256,128]{1,0:T(8,128)S(1)}, u32[]{:S(2)}, u32[]{:S(2)}) collective-permute-start(f32[256,128]{1,0:T(8,128)S(1)} %get-tuple-element.29.refs_5_), channel_id=1, source_target_pairs={{0,8},{1,9},{2,10},{3,11},{4,12},{5,13},{6,14},{7,15},{8,0},{9,1},... | collective-permute-start | bytes 393224 | tf_op jit(solution)/shard_map/ppermute | solution.py:223
  8.4 7.2 %collective-permute-start.6 = (f32[264,128]{1,0:T(8,128)S(1)}, f32[264,128]{1,0:T(8,128)S(1)}, u32[]{:S(2)}, u32[]{:S(2)}) collective-permute-start(f32[264,128]{1,0:T(8,128)S(1)} %get-tuple-element.31.refs_3_), channel_id=1, source_target_pairs={{0,6},{1,7},{2,4},{3,5},{4,2},{5,3},{6,0},{7,1},{8,14},{9,15},{10,... | collective-permute-start | bytes 405512 | tf_op jit(solution)/shard_map/ppermute | solution.py:223
  10.0 7.1 %collective-permute-start.7 = (f32[264,128]{1,0:T(8,128)S(1)}, f32[264,128]{1,0:T(8,128)S(1)}, u32[]{:S(2)}, u32[]{:S(2)}) collective-permute-start(f32[264,128]{1,0:T(8,128)S(1)} %get-tuple-element.31.refs_3_), channel_id=1, source_target_pairs={{0,4},{1,5},{2,6},{3,7},{4,0},{5,1},{6,2},{7,3},{8,12},{9,13},{10,... | collective-permute-start | bytes 405512 | tf_op jit(solution)/shard_map/ppermute | solution.py:223
  10.5 6.7 %collective-permute-start.8 = (f32[264,128]{1,0:T(8,128)S(1)}, f32[264,128]{1,0:T(8,128)S(1)}, u32[]{:S(2)}, u32[]{:S(2)}) collective-permute-start(f32[264,128]{1,0:T(8,128)S(1)} %get-tuple-element.31.refs_3_), channel_id=1, source_target_pairs={{0,2},{1,3},{2,0},{3,1},{4,6},{5,7},{6,4},{7,5},{8,10},{9,11},{10,... | collective-permute-start | bytes 405512 | tf_op jit(solution)/shard_map/ppermute | solution.py:223
  12.0 7.6 %collective-permute-start.5 = (f32[256,128]{1,0:T(8,128)S(1)}, f32[256,128]{1,0:T(8,128)S(1)}, u32[]{:S(2)}, u32[]{:S(2)}) collective-permute-start(f32[256,128]{1,0:T(8,128)S(1)} %shard_map.112), channel_id=1, source_target_pairs={{0,8},{1,9},{2,10},{3,11},{4,12},{5,13},{6,14},{7,15},{8,0},{9,1},... | collective-permute-start | bytes 393224 | tf_op jit(solution)/shard_map/ppermute | solution.py:223
  12.5 9.5 %collective-permute-start = (f32[272,128]{1,0:T(8,128)S(1)}, f32[272,128]{1,0:T(8,128)S(1)}, u32[]{:S(2)}, u32[]{:S(2)}) collective-permute-start(f32[272,128]{1,0:T(8,128)S(1)} %get-tuple-element.28), channel_id=1, source_target_pairs={{0,16},{1,17},{2,18},{3,19},{4,20},{5,21},{6,22},{7,23},{8,24},{9,... | collective-permute-start | bytes 417800 | tf_op jit(solution)/shard_map/ppermute | solution.py:223
  19.7 2.5 %collective-permute-start.10 = (f32[256,128]{1,0:T(8,128)S(1)}, f32[256,128]{1,0:T(8,128)S(1)}, u32[]{:S(2)}, u32[]{:S(2)}) collective-permute-start(f32[256,128]{1,0:T(8,128)S(1)} %get-tuple-element.33), channel_id=1, source_target_pairs={{0,1},{1,0},{2,3},{3,2},{4,5},{5,4},{6,7},{7,6},{8,9},{9,8},{10,11... | collective-permute-start | bytes 393224 | tf_op jit(solution)/shard_map/ppermute | solution.py:223
  19.7 2.4 %collective-permute-start.11 = (f32[256,128]{1,0:T(8,128)S(1)}, f32[256,128]{1,0:T(8,128)S(1)}, u32[]{:S(2)}, u32[]{:S(2)}) collective-permute-start(f32[256,128]{1,0:T(8,128)S(1)} %get-tuple-element.34), channel_id=1, source_target_pairs={{0,1},{1,0},{2,3},{3,2},{4,5},{5,4},{6,7},{7,6},{8,9},{9,8},{10,11... | collective-permute-start | bytes 393224 | tf_op jit(solution)/shard_map/ppermute | solution.py:223
  20.2 1.9 %collective-permute-start.12 = (f32[256,128]{1,0:T(8,128)S(1)}, f32[256,128]{1,0:T(8,128)S(1)}, u32[]{:S(2)}, u32[]{:S(2)}) collective-permute-start(f32[256,128]{1,0:T(8,128)S(1)} %get-tuple-element.35), channel_id=1, source_target_pairs={{0,1},{1,0},{2,3},{3,2},{4,5},{5,4},{6,7},{7,6},{8,9},{9,8},{10,11... | collective-permute-start | bytes 393224 | tf_op jit(solution)/shard_map/ppermute | solution.py:223
  20.3 1.8 %collective-permute-start.9 = (f32[256,128]{1,0:T(8,128)S(1)}, f32[256,128]{1,0:T(8,128)S(1)}, u32[]{:S(2)}, u32[]{:S(2)}) collective-permute-start(f32[256,128]{1,0:T(8,128)S(1)} %get-tuple-element.32), channel_id=1, source_target_pairs={{0,1},{1,0},{2,3},{3,2},{4,5},{5,4},{6,7},{7,6},{8,9},{9,8},{10,11... | collective-permute-start | bytes 393224 | tf_op jit(solution)/shard_map/ppermute | solution.py:223
  22.0 6.2 %collective-permute-start.2 = (f32[272,128]{1,0:T(8,128)S(1)}, f32[272,128]{1,0:T(8,128)S(1)}, u32[]{:S(2)}, u32[]{:S(2)}) collective-permute-start(f32[272,128]{1,0:T(8,128)S(1)} %get-tuple-element.28), channel_id=1, source_target_pairs={{0,8},{1,9},{2,10},{3,11},{4,12},{5,13},{6,14},{7,15},{8,0},{9,1},... | collective-permute-start | bytes 417800 | tf_op jit(solution)/shard_map/ppermute | solution.py:223
  22.7 8.6 %collective-permute-start.13 = (f32[264,128]{1,0:T(8,128)S(1)}, f32[264,128]{1,0:T(8,128)S(1)}, u32[]{:S(2)}, u32[]{:S(2)}) collective-permute-start(f32[264,128]{1,0:T(8,128)S(1)} %shard_map.115.refs_3_), channel_id=1, source_target_pairs={{0,6},{1,7},{2,4},{3,5},{4,2},{5,3},{6,0},{7,1},{8,14},{9,15},{10,... | collective-permute-start | bytes 405512 | tf_op jit(solution)/shard_map/ppermute | solution.py:223
  24.3 7.7 %collective-permute-start.14 = (f32[264,128]{1,0:T(8,128)S(1)}, f32[264,128]{1,0:T(8,128)S(1)}, u32[]{:S(2)}, u32[]{:S(2)}) collective-permute-start(f32[264,128]{1,0:T(8,128)S(1)} %shard_map.115.refs_3_), channel_id=1, source_target_pairs={{0,4},{1,5},{2,6},{3,7},{4,0},{5,1},{6,2},{7,3},{8,12},{9,13},{10,... | collective-permute-start | bytes 405512 | tf_op jit(solution)/shard_map/ppermute | solution.py:223
  24.8 7.3 %collective-permute-start.15 = (f32[264,128]{1,0:T(8,128)S(1)}, f32[264,128]{1,0:T(8,128)S(1)}, u32[]{:S(2)}, u32[]{:S(2)}) collective-permute-start(f32[264,128]{1,0:T(8,128)S(1)} %shard_map.115.refs_3_), channel_id=1, source_target_pairs={{0,2},{1,3},{2,0},{3,1},{4,6},{5,7},{6,4},{7,5},{8,10},{9,11},{10,... | collective-permute-start | bytes 405512 | tf_op jit(solution)/shard_map/ppermute | solution.py:223
  26.3 5.0 %collective-permute-start.1 = (f32[256,128]{1,0:T(8,128)S(1)}, f32[256,128]{1,0:T(8,128)S(1)}, u32[]{:S(2)}, u32[]{:S(2)}) collective-permute-start(f32[256,128]{1,0:T(8,128)S(1)} %shard_map.111), channel_id=1, source_target_pairs={{0,8},{1,9},{2,10},{3,11},{4,12},{5,13},{6,14},{7,15},{8,0},{9,1},... | collective-permute-start | bytes 393224 | tf_op jit(solution)/shard_map/ppermute | solution.py:223
  32.1 2.0 %collective-permute-start.16 = (f32[1024,128]{1,0:T(8,128)S(1)}, f32[1024,128]{1,0:T(8,128)S(1)}, u32[]{:S(2)}, u32[]{:S(2)}) collective-permute-start(f32[1024,128]{1,0:T(8,128)S(1)} %shard_map.116.refs_0_), channel_id=1, source_target_pairs={{0,1},{1,0},{2,3},{3,2},{4,5},{5,4},{6,7},{7,6},{8,9},{9,8},{10,11... | collective-permute-start | bytes 1572872 | tf_op jit(solution)/shard_map/ppermute | solution.py:223
  34.7 4.3 %collective-permute-start.17 = (f32[128,128]{1,0:T(8,128)S(1)}, f32[128,128]{1,0:T(8,128)S(1)}, u32[]{:S(2)}, u32[]{:S(2)}) collective-permute-start(f32[128,128]{1,0:T(8,128)S(1)} %get-tuple-element.39.refs_3_), channel_id=1, source_target_pairs={{0,2},{1,3},{2,0},{3,1},{4,16},{5,17},{6,24},{7,25},{8,10},{9,11},... | collective-permute-start | bytes 196616 | tf_op jit(solution)/shard_map/ppermute | solution.py:223
  35.2 10.9 %collective-permute-start.18 = (f32[128,128]{1,0:T(8,128)S(1)}, f32[128,128]{1,0:T(8,128)S(1)}, u32[]{:S(2)}, u32[]{:S(2)}) collective-permute-start(f32[128,128]{1,0:T(8,128)S(1)} %get-tuple-element.40), channel_id=1, source_target_pairs={{0,1},{1,0},{2,9},{3,8},{4,17},{5,16},{6,25},{7,24},{8,3},{9,2},{1... | collective-permute-start | bytes 196616 | tf_op jit(solution)/shard_map/ppermute | solution.py:223
  36.7 9.4 %collective-permute-start.20 = (f32[128,128]{1,0:T(8,128)S(1)}, f32[128,128]{1,0:T(8,128)S(1)}, u32[]{:S(2)}, u32[]{:S(2)}) collective-permute-start(f32[128,128]{1,0:T(8,128)S(1)} %get-tuple-element.40), channel_id=1, source_target_pairs={{0,1},{1,0},{2,3},{3,2},{4,5},{5,4},{6,7},{7,6},{8,9},{9,8},{10,11... | collective-permute-start | bytes 196616 | tf_op jit(solution)/shard_map/ppermute | solution.py:223
  39.0 7.1 %collective-permute-start.19 = (f32[128,128]{1,0:T(8,128)S(1)}, f32[128,128]{1,0:T(8,128)S(1)}, u32[]{:S(2)}, u32[]{:S(2)}) collective-permute-start(f32[128,128]{1,0:T(8,128)S(1)} %collective-permute-done.17.refs_0_), channel_id=1, source_target_pairs={{0,8},{1,9},{10,2},{11,3},{20,28},{21,29},{30,22},{31,23}} | collective-permute-start | bytes 196616 | tf_op jit(solution)/shard_map/ppermute | solution.py:223

commit v6 on v5

--- a/solution.py
+++ b/solution.py
@@ -99,6 +99,10 @@
         refs[-1][i * rows : (i + 1) * rows, :] = ref[:rows, :]
 
 
+def copy_kernel(x, _, out):
+    out[...] = x[: out.shape[0], :]
+
+
 def parted_kernel(x, *outs):
     rows = outs[0].shape[0]
     for i, out in enumerate(outs):
@@ -116,7 +120,7 @@
     b_got, mask, out = refs[: len(along)], refs[len(along)], refs[len(along) + 1 + waits]
     sent, both = refs[len(along) + 2 + waits : -1], refs[-1]
     row, chip, core = position()
-    rows = b_own.shape[0]
+    rows = out.shape[0] // BS * BS
     for offset, ref in zip([0] + along, (b_own,) + b_got):
         at = pl.ds(pl.multiple_of((row ^ offset) * rows, rows), rows)
         both[at, :LANES], both[at, LANES:] = split(ref[:rows, :])
@@ -238,9 +242,11 @@
     inputs = [
         pltpu.with_memory_space_constraint(x, pltpu.HBM) for x in (pp, pv, hv, sv, hp, sp, xp)
     ]
-    tile, longer, longest = (
-        jax.ShapeDtypeStruct((rows + 8 * extra, LANES), f32) for extra in range(3)
-    )
+
+    def sized(extra):
+        return jax.ShapeDtypeStruct((rows + extra, LANES), f32)
+
+    tile, longer, longest = sized(0), sized(8), sized(16)
     lines = pltpu.VMEM((rows, LANES), f32)
     p_near, p_far, hv, sv, hp, sp, xp = call(
         first_kernel,
@@ -257,7 +263,7 @@
     )
     h_tile, s_near, s_far, mask = call(
         rest_kernel,
-        [longer, tile, longest, jax.ShapeDtypeStruct((max(8, cap // 2), LANES), f32)],
+        [longer, sized(24), sized(56), jax.ShapeDtypeStruct((max(8, cap // 2), LANES), f32)],
         [VMEM] * 5 + [SMEM] * 3,
         [lines],
         1 << 10,
@@ -266,15 +272,24 @@
     along = list(range(row_count - 1, 0, -1))
     across = list(range(chip_count - 1, 0, -1))
 
-    def along_z(near, far):
+    def along_z(near, far, direct=False):
         got = {}
-        for offset in sorted(along, key=lambda s: s.bit_count()):
-            low = offset & -offset
-            if offset != low:
-                value = stack([got[offset ^ low]])
+
+        def hops(offset):
+            taken = []
+            for bit in reversed(range(row_count.bit_length())):
+                if offset >> bit & 1:
+                    taken.append((2 << bit) - 1)
+                    offset ^= taken[-1]
+            return taken
+
+        for offset in sorted(along, key=lambda s: len(hops(s))):
+            hop = hops(offset)[-1]
+            if offset != hop:
+                value = got[offset ^ hop] if direct else stack([got[offset ^ hop]])
             else:
-                value = near if low == 1 else far
-            got[offset] = send(value, lambda r, m, k: (r ^ low, m, k))
+                value = near if hop == 1 else far
+            got[offset] = send(value, lambda r, m, k: (r ^ hop, m, k))
         return [got[offset] for offset in along]
 
     def parted(x, count):
@@ -282,27 +297,30 @@
             parted_kernel, [tile] * count, [VMEM], [], 1 << 10, x
         )
 
-    def in_plane(x):
-        return [send(x, lambda r, m, k, o=o: (r, m ^ o, k)) for o in across]
+    def in_plane(x, last=None):
+        return [
+            send(x if last is None or o > 1 else last, lambda r, m, k, o=o: (r, m ^ o, k))
+            for o in across
+        ]
 
     def product(a_got, a_shared, b, b_got, parts, *waits):
         part = jax.ShapeDtypeStruct((LANES, LANES), f32)
         return call(
             functools.partial(product_kernel, along, across, len(a_shared), len(waits)),
-            [longer] + [part] * parts,
+            [longest] + [part] * parts,
             [VMEM] * (3 + len(a_shared) + len(b_got))
             + [pl.BlockSpec(memory_space=pl.ANY)] * len(waits),
             [pltpu.VMEM((order, 2 * LANES), jnp.bfloat16)],
-            2 * 3 * rows * order * LANES,
+            1 << 10,
             a_got, *a_shared, b, *b_got, mask, *waits,
         )
 
-    p_got = along_z(p_near, p_far)
-    s_got = along_z(s_far, s_far)
+    p_got = along_z(p_far, p_far, direct=True)
+    s_got = along_z(s_near, s_far)
     h_parts = [h_tile] + in_plane(h_tile)
     h_got = stack(h_parts, *p_got[::-1])
     h_shared = [to_other(x) for x in parted(h_got, len(h_parts))]
-    (y,) = product(h_got, h_shared, p_near, p_got, 0, s_got[along.index(row_count // 2)])
+    (y,) = product(h_got, h_shared, p_near, p_got, 0)
     y_got = stack([y] + in_plane(y), *s_got)
     x, *sent = product(y_got, [to_other(y_got)], s_near, s_got, sends)
 

time: 47.6 us -> 47.2 us (level)
  waiting for transfers between devices: 18.7 us -> 18 us
    ppermute x21, waiting for transfers between devices: 18.7 us -> 18 us  [send(): return lax.ppermute(value, AXES, pairs)]
    pallas_call x10 -> x9, Pallas kernels: 3.77 us -> 3.75 us  [call(): pl.pallas_call(kernel, out_shape=out_shapes, in_specs=in_specs, out_specs...]
where the time goes in v6:
time: 47.2 us; the launch traced here: 46.7 us
  starting transfers between devices  22.3 us (47%)
  waiting for transfers between devices  18 us (38%)
  Pallas kernels  3.75 us (8%)
  between operations  2.69 us (6%)
    ppermute x21, starting transfers between devices, send(): return lax.ppermute(value, AXES, pairs)  22.3 us
    ppermute x21, waiting for transfers between devices, send(): return lax.ppermute(value, AXES, pairs)  18 us
    pallas_call x9, Pallas kernels, call(): pl.pallas_call(kernel, out_shape=out_shapes, in_specs=in_specs, out_specs...  3.75 us
  transfers between devices with their start and end apart: 21, of which 11 were waited for; matrix products, arithmetic and copies ran while one was open for 0% of the time, Pallas kernels for 2%

profile of v6, /device:TPU:2, one launch (start us, length us, event | category | flops | bytes accessed | tf_op | source)
XLA Modules:
  0.0 46.7 jit_solution(1902444493202664154)
XLA Ops:
  0.7 1.2 %shard_map.109 = (f32[256,128]{1,0:T(8,128)S(1)}, f32[272,128]{1,0:T(8,128)S(1)}, f32[1,8,4096]{2,1,0:T(8,128)S(1)}, f32[1,8,4096]{2,1,0:T(8,128)S(1)}, s32[1,8]...) custom-call(s32[1,1]{1,0:T(1,128)S(6)} %copy.13.count, s32[1,8]{1,0:T(1,128)} %refs_0_.1, ...), custom_call_target="tpu_custom_call" | custom-call | flops 1024 | bytes 1024 | tf_op jit(solution)/shard_map/pallas_call | solution.py:198
  1.9 3.7 %collective-permute-start.4 = (f32[272,128]{1,0:T(8,128)S(1)}, f32[272,128]{1,0:T(8,128)S(1)}, u32[]{:S(2)}, u32[]{:S(2)}) collective-permute-start(f32[272,128]{1,0:T(8,128)S(1)} %get-tuple-element.30), channel_id=1, source_target_pairs={{0,24},{1,25},{2,26},{3,27},{4,28},{5,29},{6,30},{7,31},{8,16},{9,... | collective-permute-start | bytes 417800 | tf_op jit(solution)/shard_map/ppermute | solution.py:227
  7.8 1.6 %collective-permute-start.6 = (f32[264,128]{1,0:T(8,128)S(1)}, f32[264,128]{1,0:T(8,128)S(1)}, u32[]{:S(2)}, u32[]{:S(2)}) collective-permute-start(f32[264,128]{1,0:T(8,128)S(1)} %get-tuple-element.31.refs_3_), channel_id=1, source_target_pairs={{0,6},{1,7},{2,4},{3,5},{4,2},{5,3},{6,0},{7,1},{8,14},{9,15},{10,... | collective-permute-start | bytes 405512 | tf_op jit(solution)/shard_map/ppermute | solution.py:227
  9.4 2.5 %collective-permute-start.5 = (f32[272,128]{1,0:T(8,128)S(1)}, f32[272,128]{1,0:T(8,128)S(1)}, u32[]{:S(2)}, u32[]{:S(2)}) collective-permute-start(f32[272,128]{1,0:T(8,128)S(1)} %collective-permute-done.4.refs_2_.refs_6_), channel_id=1, source_target_pairs={{0,8},{1,9},{2,10},{3,11},{4,12},{5,13},{6,14},{7,15},{8,0},{9,1},... | collective-permute-start | bytes 417800 | tf_op jit(solution)/shard_map/ppermute | solution.py:227
  11.9 1.5 %collective-permute-start.7 = (f32[264,128]{1,0:T(8,128)S(1)}, f32[264,128]{1,0:T(8,128)S(1)}, u32[]{:S(2)}, u32[]{:S(2)}) collective-permute-start(f32[264,128]{1,0:T(8,128)S(1)} %get-tuple-element.31.refs_3_), channel_id=1, source_target_pairs={{0,4},{1,5},{2,6},{3,7},{4,0},{5,1},{6,2},{7,3},{8,12},{9,13},{10,... | collective-permute-start | bytes 405512 | tf_op jit(solution)/shard_map/ppermute | solution.py:227
  13.4 0.5 %collective-permute-start.8 = (f32[264,128]{1,0:T(8,128)S(1)}, f32[264,128]{1,0:T(8,128)S(1)}, u32[]{:S(2)}, u32[]{:S(2)}) collective-permute-start(f32[264,128]{1,0:T(8,128)S(1)} %get-tuple-element.31.refs_3_), channel_id=1, source_target_pairs={{0,2},{1,3},{2,0},{3,1},{4,6},{5,7},{6,4},{7,5},{8,10},{9,11},{10,... | collective-permute-start | bytes 405512 | tf_op jit(solution)/shard_map/ppermute | solution.py:227
  14.0 2.5 %collective-permute-start = (f32[312,128]{1,0:T(8,128)S(1)}, f32[312,128]{1,0:T(8,128)S(1)}, u32[]{:S(2)}, u32[]{:S(2)}) collective-permute-start(f32[312,128]{1,0:T(8,128)S(1)} %get-tuple-element.28), channel_id=1, source_target_pairs={{0,24},{1,25},{2,26},{3,27},{4,28},{5,29},{6,30},{7,31},{8,16},{9,... | collective-permute-start | bytes 479240 | tf_op jit(solution)/shard_map/ppermute | solution.py:227
  16.9 1.5 %collective-permute-done.8.refs_6_ = f32[264,128]{1,0:T(8,128)S(1)} collective-permute-done((f32[264,128]{1,0:T(8,128)S(1)}, f32[264,128]{1,0:T(8,128)S(1)}, u32[]{:S(2)}, u32[]{:S(2)}) %collective-permute-start.8) | collective-permute-done | bytes 135200 | tf_op jit(solution)/shard_map/ppermute | solution.py:227
  18.6 0.5 %collective-permute-start.11 = (f32[256,128]{1,0:T(8,128)S(1)}, f32[256,128]{1,0:T(8,128)S(1)}, u32[]{:S(2)}, u32[]{:S(2)}) collective-permute-start(f32[256,128]{1,0:T(8,128)S(1)} %get-tuple-element.34), channel_id=1, source_target_pairs={{0,1},{1,0},{2,3},{3,2},{4,5},{5,4},{6,7},{7,6},{8,9},{9,8},{10,11... | collective-permute-start | bytes 393224 | tf_op jit(solution)/shard_map/ppermute | solution.py:227
  20.6 0.5 %shard_map.114.refs_3_ = f32[272,128]{1,0:T(8,128)S(1)} custom-call(f32[1024,128]{1,0:T(8,128)S(1)} %shard_map.112.x.refs_0_, f32[256,128]{1,0:T(8,128)S(1)} %collective-permute-done.9.refs_1_, f32[256,128]{1,0:T(8,128)S(1)} %collective-permute-done.10.refs_2_, f32[256,128]{1,0:T(8,128)S(1)} %collective-permute-done.11.refs_3_, ...), custom_call_target="tpu_custom_call" | custom-call | flops 1024 | bytes 1024 | tf_op jit(solution)/shard_map/pallas_call | solution.py:198
  21.2 1.0 %collective-permute-start.13 = (f32[272,128]{1,0:T(8,128)S(1)}, f32[272,128]{1,0:T(8,128)S(1)}, u32[]{:S(2)}, u32[]{:S(2)}) collective-permute-start(f32[272,128]{1,0:T(8,128)S(1)} %shard_map.114.refs_3_), channel_id=1, source_target_pairs={{0,6},{1,7},{2,4},{3,5},{4,2},{5,3},{6,0},{7,1},{8,14},{9,15},{10,... | collective-permute-start | bytes 417800 | tf_op jit(solution)/shard_map/ppermute | solution.py:227
  22.2 2.5 %collective-permute-start.14 = (f32[272,128]{1,0:T(8,128)S(1)}, f32[272,128]{1,0:T(8,128)S(1)}, u32[]{:S(2)}, u32[]{:S(2)}) collective-permute-start(f32[272,128]{1,0:T(8,128)S(1)} %shard_map.114.refs_3_), channel_id=1, source_target_pairs={{0,4},{1,5},{2,6},{3,7},{4,0},{5,1},{6,2},{7,3},{8,12},{9,13},{10,... | collective-permute-start | bytes 417800 | tf_op jit(solution)/shard_map/ppermute | solution.py:227
  24.8 1.4 %collective-permute-start.1 = (f32[256,128]{1,0:T(8,128)S(1)}, f32[256,128]{1,0:T(8,128)S(1)}, u32[]{:S(2)}, u32[]{:S(2)}) collective-permute-start(f32[256,128]{1,0:T(8,128)S(1)} %shard_map.111), channel_id=1, source_target_pairs={{0,8},{1,9},{2,10},{3,11},{4,12},{5,13},{6,14},{7,15},{8,0},{9,1},... | collective-permute-start | bytes 393224 | tf_op jit(solution)/shard_map/ppermute | solution.py:227
  26.2 3.8 %collective-permute-done.1.refs_1_.refs_4_ = f32[256,128]{1,0:T(8,128)S(1)} collective-permute-done((f32[256,128]{1,0:T(8,128)S(1)}, f32[256,128]{1,0:T(8,128)S(1)}, u32[]{:S(2)}, u32[]{:S(2)}) %collective-permute-start.1) | collective-permute-done | bytes 131104 | tf_op jit(solution)/shard_map/ppermute | solution.py:227
  30.0 1.1 %collective-permute-done.14.refs_5_ = f32[272,128]{1,0:T(8,128)S(1)} collective-permute-done((f32[272,128]{1,0:T(8,128)S(1)}, f32[272,128]{1,0:T(8,128)S(1)}, u32[]{:S(2)}, u32[]{:S(2)}) %collective-permute-start.14) | collective-permute-done | bytes 139296 | tf_op jit(solution)/shard_map/ppermute | solution.py:227
  31.2 1.9 %collective-permute-done.16.refs_1_ = f32[1024,128]{1,0:T(8,128)S(1)} collective-permute-done((f32[1024,128]{1,0:T(8,128)S(1)}, f32[1024,128]{1,0:T(8,128)S(1)}, u32[]{:S(2)}, u32[]{:S(2)}) %collective-permute-start.16) | collective-permute-done | bytes 524320 | tf_op jit(solution)/shard_map/ppermute | solution.py:227
  33.1 0.5 %shard_map.116 = (f32[272,128]{1,0:T(8,128)S(1)}, f32[128,128]{1,0:T(8,128)S(1)}, f32[128,128]{1,0:T(8,128)S(1)}) custom-call(f32[1024,128]{1,0:T(8,128)S(1)} %shard_map.115.refs_0_, f32[1024,128]{1,0:T(8,128)S(1)} %collective-permute-done.16.refs_1_, f32[280,128]{1,0:T(8,128)S(1)} %get-tuple-element.29.refs_2_, ...), custom_call_target="tpu_custom_call" | custom-call | flops 1024 | bytes 1024 | tf_op jit(solution)/shard_map/pallas_call | solution.py:198
  33.6 1.2 %collective-permute-start.17 = (f32[128,128]{1,0:T(8,128)S(1)}, f32[128,128]{1,0:T(8,128)S(1)}, u32[]{:S(2)}, u32[]{:S(2)}) collective-permute-start(f32[128,128]{1,0:T(8,128)S(1)} %get-tuple-element.39.refs_3_), channel_id=1, source_target_pairs={{0,2},{1,3},{2,0},{3,1},{4,16},{5,17},{6,24},{7,25},{8,10},{9,11},... | collective-permute-start | bytes 196616 | tf_op jit(solution)/shard_map/ppermute | solution.py:227
  34.8 0.7 %collective-permute-start.18 = (f32[128,128]{1,0:T(8,128)S(1)}, f32[128,128]{1,0:T(8,128)S(1)}, u32[]{:S(2)}, u32[]{:S(2)}) collective-permute-start(f32[128,128]{1,0:T(8,128)S(1)} %get-tuple-element.40), channel_id=1, source_target_pairs={{0,1},{1,0},{2,9},{3,8},{4,17},{5,16},{6,25},{7,24},{8,3},{9,2},{1... | collective-permute-start | bytes 196616 | tf_op jit(solution)/shard_map/ppermute | solution.py:227
  35.5 0.7 %collective-permute-start.20 = (f32[128,128]{1,0:T(8,128)S(1)}, f32[128,128]{1,0:T(8,128)S(1)}, u32[]{:S(2)}, u32[]{:S(2)}) collective-permute-start(f32[128,128]{1,0:T(8,128)S(1)} %get-tuple-element.40), channel_id=1, source_target_pairs={{0,1},{1,0},{2,3},{3,2},{4,5},{5,4},{6,7},{7,6},{8,9},{9,8},{10,11... | collective-permute-start | bytes 196616 | tf_op jit(solution)/shard_map/ppermute | solution.py:227
  36.1 1.8 %collective-permute-done.17.refs_0_ = f32[128,128]{1,0:T(8,128)S(1)} collective-permute-done((f32[128,128]{1,0:T(8,128)S(1)}, f32[128,128]{1,0:T(8,128)S(1)}, u32[]{:S(2)}, u32[]{:S(2)}) %collective-permute-start.17) | collective-permute-done | bytes 65568 | tf_op jit(solution)/shard_map/ppermute | solution.py:227
  37.9 1.3 %collective-permute-start.19 = (f32[128,128]{1,0:T(8,128)S(1)}, f32[128,128]{1,0:T(8,128)S(1)}, u32[]{:S(2)}, u32[]{:S(2)}) collective-permute-start(f32[128,128]{1,0:T(8,128)S(1)} %collective-permute-done.17.refs_0_), channel_id=1, source_target_pairs={{0,8},{1,9},{10,2},{11,3},{20,28},{21,29},{30,22},{31,23}} | collective-permute-start | bytes 196616 | tf_op jit(solution)/shard_map/ppermute | solution.py:227
  39.2 6.5 %collective-permute-done.18.refs_1_ = f32[128,128]{1,0:T(8,128)S(1)} collective-permute-done((f32[128,128]{1,0:T(8,128)S(1)}, f32[128,128]{1,0:T(8,128)S(1)}, u32[]{:S(2)}, u32[]{:S(2)}) %collective-permute-start.18) | collective-permute-done | bytes 65568 | tf_op jit(solution)/shard_map/ppermute | solution.py:227
  45.7 1.0 %shard_map.117 = f32[1,8,4096]{2,1,0:T(8,128)} custom-call(s32[1,8]{1,0:T(1,128)S(1)} %get-tuple-element.23.xp.places, s32[1,1]{1,0:T(1,128)S(6)} %copy.15.xc.count, f32[272,128]{1,0:T(8,128)S(1)} %get-tuple-element.38.x, f32[128,128]{1,0:T(8,128)S(1)} %collective-permute-done.17.refs_0_, f32[128,128]{1,0:T(8,128)S(1)} %collective-permute-done.18.refs_1_, ...), custom_call_target="tpu_custom_call" | custom-call | flops 1024 | bytes 1024 | tf_op jit(solution)/shard_map/pallas_call | solution.py:198
  (27 shorter events, 2.7 us)
Async XLA Ops:
  1.9 7.5 %collective-permute-start.4 = (f32[272,128]{1,0:T(8,128)S(1)}, f32[272,128]{1,0:T(8,128)S(1)}, u32[]{:S(2)}, u32[]{:S(2)}) collective-permute-start(f32[272,128]{1,0:T(8,128)S(1)} %get-tuple-element.30), channel_id=1, source_target_pairs={{0,24},{1,25},{2,26},{3,27},{4,28},{5,29},{6,30},{7,31},{8,16},{9,... | collective-permute-start | bytes 417800 | tf_op jit(solution)/shard_map/ppermute | solution.py:227
  7.8 6.1 %collective-permute-start.6 = (f32[264,128]{1,0:T(8,128)S(1)}, f32[264,128]{1,0:T(8,128)S(1)}, u32[]{:S(2)}, u32[]{:S(2)}) collective-permute-start(f32[264,128]{1,0:T(8,128)S(1)} %get-tuple-element.31.refs_3_), channel_id=1, source_target_pairs={{0,6},{1,7},{2,4},{3,5},{4,2},{5,3},{6,0},{7,1},{8,14},{9,15},{10,... | collective-permute-start | bytes 405512 | tf_op jit(solution)/shard_map/ppermute | solution.py:227
  9.4 9.1 %collective-permute-start.3 = (f32[272,128]{1,0:T(8,128)S(1)}, f32[272,128]{1,0:T(8,128)S(1)}, u32[]{:S(2)}, u32[]{:S(2)}) collective-permute-start(f32[272,128]{1,0:T(8,128)S(1)} %get-tuple-element.30), channel_id=1, source_target_pairs={{0,8},{1,9},{2,10},{3,11},{4,12},{5,13},{6,14},{7,15},{8,0},{9,1},... | collective-permute-start | bytes 417800 | tf_op jit(solution)/shard_map/ppermute | solution.py:227
  9.4 9.0 %collective-permute-start.5 = (f32[272,128]{1,0:T(8,128)S(1)}, f32[272,128]{1,0:T(8,128)S(1)}, u32[]{:S(2)}, u32[]{:S(2)}) collective-permute-start(f32[272,128]{1,0:T(8,128)S(1)} %collective-permute-done.4.refs_2_.refs_6_), channel_id=1, source_target_pairs={{0,8},{1,9},{2,10},{3,11},{4,12},{5,13},{6,14},{7,15},{8,0},{9,1},... | collective-permute-start | bytes 417800 | tf_op jit(solution)/shard_map/ppermute | solution.py:227
  11.9 5.0 %collective-permute-start.7 = (f32[264,128]{1,0:T(8,128)S(1)}, f32[264,128]{1,0:T(8,128)S(1)}, u32[]{:S(2)}, u32[]{:S(2)}) collective-permute-start(f32[264,128]{1,0:T(8,128)S(1)} %get-tuple-element.31.refs_3_), channel_id=1, source_target_pairs={{0,4},{1,5},{2,6},{3,7},{4,0},{5,1},{6,2},{7,3},{8,12},{9,13},{10,... | collective-permute-start | bytes 405512 | tf_op jit(solution)/shard_map/ppermute | solution.py:227
  13.4 5.0 %collective-permute-start.8 = (f32[264,128]{1,0:T(8,128)S(1)}, f32[264,128]{1,0:T(8,128)S(1)}, u32[]{:S(2)}, u32[]{:S(2)}) collective-permute-start(f32[264,128]{1,0:T(8,128)S(1)} %get-tuple-element.31.refs_3_), channel_id=1, source_target_pairs={{0,2},{1,3},{2,0},{3,1},{4,6},{5,7},{6,4},{7,5},{8,10},{9,11},{10,... | collective-permute-start | bytes 405512 | tf_op jit(solution)/shard_map/ppermute | solution.py:227
  14.0 10.8 %collective-permute-start = (f32[312,128]{1,0:T(8,128)S(1)}, f32[312,128]{1,0:T(8,128)S(1)}, u32[]{:S(2)}, u32[]{:S(2)}) collective-permute-start(f32[312,128]{1,0:T(8,128)S(1)} %get-tuple-element.28), channel_id=1, source_target_pairs={{0,24},{1,25},{2,26},{3,27},{4,28},{5,29},{6,30},{7,31},{8,16},{9,... | collective-permute-start | bytes 479240 | tf_op jit(solution)/shard_map/ppermute | solution.py:227
  18.5 1.4 %collective-permute-start.10 = (f32[256,128]{1,0:T(8,128)S(1)}, f32[256,128]{1,0:T(8,128)S(1)}, u32[]{:S(2)}, u32[]{:S(2)}) collective-permute-start(f32[256,128]{1,0:T(8,128)S(1)} %get-tuple-element.33), channel_id=1, source_target_pairs={{0,1},{1,0},{2,3},{3,2},{4,5},{5,4},{6,7},{7,6},{8,9},{9,8},{10,11... | collective-permute-start | bytes 393224 | tf_op jit(solution)/shard_map/ppermute | solution.py:227
  18.6 1.5 %collective-permute-start.11 = (f32[256,128]{1,0:T(8,128)S(1)}, f32[256,128]{1,0:T(8,128)S(1)}, u32[]{:S(2)}, u32[]{:S(2)}) collective-permute-start(f32[256,128]{1,0:T(8,128)S(1)} %get-tuple-element.34), channel_id=1, source_target_pairs={{0,1},{1,0},{2,3},{3,2},{4,5},{5,4},{6,7},{7,6},{8,9},{9,8},{10,11... | collective-permute-start | bytes 393224 | tf_op jit(solution)/shard_map/ppermute | solution.py:227
  19.1 1.3 %collective-permute-start.12 = (f32[256,128]{1,0:T(8,128)S(1)}, f32[256,128]{1,0:T(8,128)S(1)}, u32[]{:S(2)}, u32[]{:S(2)}) collective-permute-start(f32[256,128]{1,0:T(8,128)S(1)} %get-tuple-element.35), channel_id=1, source_target_pairs={{0,1},{1,0},{2,3},{3,2},{4,5},{5,4},{6,7},{7,6},{8,9},{9,8},{10,11... | collective-permute-start | bytes 393224 | tf_op jit(solution)/shard_map/ppermute | solution.py:227
  19.2 1.5 %collective-permute-start.9 = (f32[256,128]{1,0:T(8,128)S(1)}, f32[256,128]{1,0:T(8,128)S(1)}, u32[]{:S(2)}, u32[]{:S(2)}) collective-permute-start(f32[256,128]{1,0:T(8,128)S(1)} %get-tuple-element.32), channel_id=1, source_target_pairs={{0,1},{1,0},{2,3},{3,2},{4,5},{5,4},{6,7},{7,6},{8,9},{9,8},{10,11... | collective-permute-start | bytes 393224 | tf_op jit(solution)/shard_map/ppermute | solution.py:227
  19.9 6.2 %collective-permute-start.2 = (f32[280,128]{1,0:T(8,128)S(1)}, f32[280,128]{1,0:T(8,128)S(1)}, u32[]{:S(2)}, u32[]{:S(2)}) collective-permute-start(f32[280,128]{1,0:T(8,128)S(1)} %get-tuple-element.29.refs_2_), channel_id=1, source_target_pairs={{0,8},{1,9},{2,10},{3,11},{4,12},{5,13},{6,14},{7,15},{8,0},{9,1},... | collective-permute-start | bytes 430088 | tf_op jit(solution)/shard_map/ppermute | solution.py:227
  21.2 8.8 %collective-permute-start.13 = (f32[272,128]{1,0:T(8,128)S(1)}, f32[272,128]{1,0:T(8,128)S(1)}, u32[]{:S(2)}, u32[]{:S(2)}) collective-permute-start(f32[272,128]{1,0:T(8,128)S(1)} %shard_map.114.refs_3_), channel_id=1, source_target_pairs={{0,6},{1,7},{2,4},{3,5},{4,2},{5,3},{6,0},{7,1},{8,14},{9,15},{10,... | collective-permute-start | bytes 417800 | tf_op jit(solution)/shard_map/ppermute | solution.py:227
  22.2 8.8 %collective-permute-start.14 = (f32[272,128]{1,0:T(8,128)S(1)}, f32[272,128]{1,0:T(8,128)S(1)}, u32[]{:S(2)}, u32[]{:S(2)}) collective-permute-start(f32[272,128]{1,0:T(8,128)S(1)} %shard_map.114.refs_3_), channel_id=1, source_target_pairs={{0,4},{1,5},{2,6},{3,7},{4,0},{5,1},{6,2},{7,3},{8,12},{9,13},{10,... | collective-permute-start | bytes 417800 | tf_op jit(solution)/shard_map/ppermute | solution.py:227
  24.7 6.3 %collective-permute-start.15 = (f32[272,128]{1,0:T(8,128)S(1)}, f32[272,128]{1,0:T(8,128)S(1)}, u32[]{:S(2)}, u32[]{:S(2)}) collective-permute-start(f32[272,128]{1,0:T(8,128)S(1)} %shard_map.114.refs_3_), channel_id=1, source_target_pairs={{0,2},{1,3},{2,0},{3,1},{4,6},{5,7},{6,4},{7,5},{8,10},{9,11},{10,... | collective-permute-start | bytes 417800 | tf_op jit(solution)/shard_map/ppermute | solution.py:227
  24.8 5.2 %collective-permute-start.1 = (f32[256,128]{1,0:T(8,128)S(1)}, f32[256,128]{1,0:T(8,128)S(1)}, u32[]{:S(2)}, u32[]{:S(2)}) collective-permute-start(f32[256,128]{1,0:T(8,128)S(1)} %shard_map.111), channel_id=1, source_target_pairs={{0,8},{1,9},{2,10},{3,11},{4,12},{5,13},{6,14},{7,15},{8,0},{9,1},... | collective-permute-start | bytes 393224 | tf_op jit(solution)/shard_map/ppermute | solution.py:227
  31.1 2.0 %collective-permute-start.16 = (f32[1024,128]{1,0:T(8,128)S(1)}, f32[1024,128]{1,0:T(8,128)S(1)}, u32[]{:S(2)}, u32[]{:S(2)}) collective-permute-start(f32[1024,128]{1,0:T(8,128)S(1)} %shard_map.115.refs_0_), channel_id=1, source_target_pairs={{0,1},{1,0},{2,3},{3,2},{4,5},{5,4},{6,7},{7,6},{8,9},{9,8},{10,11... | collective-permute-start | bytes 1572872 | tf_op jit(solution)/shard_map/ppermute | solution.py:227
  33.6 4.3 %collective-permute-start.17 = (f32[128,128]{1,0:T(8,128)S(1)}, f32[128,128]{1,0:T(8,128)S(1)}, u32[]{:S(2)}, u32[]{:S(2)}) collective-permute-start(f32[128,128]{1,0:T(8,128)S(1)} %get-tuple-element.39.refs_3_), channel_id=1, source_target_pairs={{0,2},{1,3},{2,0},{3,1},{4,16},{5,17},{6,24},{7,25},{8,10},{9,11},... | collective-permute-start | bytes 196616 | tf_op jit(solution)/shard_map/ppermute | solution.py:227
  34.8 10.9 %collective-permute-start.18 = (f32[128,128]{1,0:T(8,128)S(1)}, f32[128,128]{1,0:T(8,128)S(1)}, u32[]{:S(2)}, u32[]{:S(2)}) collective-permute-start(f32[128,128]{1,0:T(8,128)S(1)} %get-tuple-element.40), channel_id=1, source_target_pairs={{0,1},{1,0},{2,9},{3,8},{4,17},{5,16},{6,25},{7,24},{8,3},{9,2},{1... | collective-permute-start | bytes 196616 | tf_op jit(solution)/shard_map/ppermute | solution.py:227
  35.5 10.2 %collective-permute-start.20 = (f32[128,128]{1,0:T(8,128)S(1)}, f32[128,128]{1,0:T(8,128)S(1)}, u32[]{:S(2)}, u32[]{:S(2)}) collective-permute-start(f32[128,128]{1,0:T(8,128)S(1)} %get-tuple-element.40), channel_id=1, source_target_pairs={{0,1},{1,0},{2,3},{3,2},{4,5},{5,4},{6,7},{7,6},{8,9},{9,8},{10,11... | collective-permute-start | bytes 196616 | tf_op jit(solution)/shard_map/ppermute | solution.py:227
  37.9 7.8 %collective-permute-start.19 = (f32[128,128]{1,0:T(8,128)S(1)}, f32[128,128]{1,0:T(8,128)S(1)}, u32[]{:S(2)}, u32[]{:S(2)}) collective-permute-start(f32[128,128]{1,0:T(8,128)S(1)} %collective-permute-done.17.refs_0_), channel_id=1, source_target_pairs={{0,8},{1,9},{10,2},{11,3},{20,28},{21,29},{30,22},{31,23}} | collective-permute-start | bytes 196616 | tf_op jit(solution)/shard_map/ppermute | solution.py:227

commit v7 on v6

--- a/solution.py
+++ b/solution.py
@@ -78,8 +78,10 @@
         copy.wait()
 
 
-def rest_kernel(hv, sv, hp, sp, xp, hc, sc, xc, h_tile, s_near, s_far, mask, lines):
-    assemble(hv, hp, hc[0, 0], lines, (h_tile,))
+def rest_kernel(
+    hv, sv, hp, sp, xp, hc, sc, xc, h_far, h_near, s_near, s_far, mask, lines
+):
+    assemble(hv, hp, hc[0, 0], lines, (h_far, h_near))
     assemble(sv, sp, sc[0, 0], lines, (s_near, s_far))
     cap = xp.shape[1]
     at = slot_places(xp, xc[0, 0], 1)
@@ -261,9 +263,9 @@
         1 << 10,
         pc, *inputs,
     )
-    h_tile, s_near, s_far, mask = call(
+    h_far, h_near, s_near, s_far, mask = call(
         rest_kernel,
-        [longer, sized(24), sized(56), jax.ShapeDtypeStruct((max(8, cap // 2), LANES), f32)],
+        [tile, sized(24), sized(24), sized(40), jax.ShapeDtypeStruct((max(8, cap // 2), LANES), f32)],
         [VMEM] * 5 + [SMEM] * 3,
         [lines],
         1 << 10,
@@ -297,17 +299,16 @@
             parted_kernel, [tile] * count, [VMEM], [], 1 << 10, x
         )
 
-    def in_plane(x, last=None):
+    def in_plane(x, other, others):
         return [
-            send(x if last is None or o > 1 else last, lambda r, m, k, o=o: (r, m ^ o, k))
-            for o in across
+            send(other if o in others else x, lambda r, m, k, o=o: (r, m ^ o, k)) for o in across
         ]
 
     def product(a_got, a_shared, b, b_got, parts, *waits):
         part = jax.ShapeDtypeStruct((LANES, LANES), f32)
         return call(
             functools.partial(product_kernel, along, across, len(a_shared), len(waits)),
-            [longest] + [part] * parts,
+            [longer] + [part] * parts,
             [VMEM] * (3 + len(a_shared) + len(b_got))
             + [pl.BlockSpec(memory_space=pl.ANY)] * len(waits),
             [pltpu.VMEM((order, 2 * LANES), jnp.bfloat16)],
@@ -315,13 +316,13 @@
             a_got, *a_shared, b, *b_got, mask, *waits,
         )
 
-    p_got = along_z(p_far, p_far, direct=True)
+    p_got = along_z(p_far, p_far)
     s_got = along_z(s_near, s_far)
-    h_parts = [h_tile] + in_plane(h_tile)
+    h_parts = [h_far] + in_plane(h_far, h_near, (1, 2))
     h_got = stack(h_parts, *p_got[::-1])
     h_shared = [to_other(x) for x in parted(h_got, len(h_parts))]
     (y,) = product(h_got, h_shared, p_near, p_got, 0)
-    y_got = stack([y] + in_plane(y), *s_got)
+    y_got = stack([y] + in_plane(y, y, ()), *s_got)
     x, *sent = product(y_got, [to_other(y_got)], s_near, s_got, sends)
 
     relay = row_count == chip_count == 4

time: 47.2 us -> 45.8 us (0.970)
  starting transfers between devices: 22.3 us -> 20 us
  waiting for transfers between devices: 18 us -> 18.8 us
    ppermute x21, starting transfers between devices: 22.3 us -> 20 us  [send(): return lax.ppermute(value, AXES, pairs)]
    ppermute x21, waiting for transfers between devices: 18 us -> 18.8 us  [send(): return lax.ppermute(value, AXES, pairs)]
    pallas_call x9 -> x10, Pallas kernels: 3.75 us -> 3.77 us  [call(): pl.pallas_call(kernel, out_shape=out_shapes, in_specs=in_specs, out_specs...]
  transfers between devices with their start and end apart: 21 -> 21, of which waited for: 11 -> 10; matrix products, arithmetic and copies ran while one was open for 0% -> 0% of each run, Pallas kernels for 2% -> 2%
where the time goes in v7:
time: 45.8 us; the launch traced here: 45.3 us
  starting transfers between devices  20 us (44%)
  waiting for transfers between devices  18.8 us (41%)
  Pallas kernels  3.77 us (8%)
  between operations  2.71 us (6%)
    ppermute x21, starting transfers between devices, send(): return lax.ppermute(value, AXES, pairs)  20 us
    ppermute x21, waiting for transfers between devices, send(): return lax.ppermute(value, AXES, pairs)  18.8 us
    pallas_call x10, Pallas kernels, call(): pl.pallas_call(kernel, out_shape=out_shapes, in_specs=in_specs, out_specs...  3.77 us
  transfers between devices with their start and end apart: 21, of which 10 were waited for; matrix products, arithmetic and copies ran while one was open for 0% of the time, Pallas kernels for 2%

profile of v7, /device:TPU:2, one launch (start us, length us, event | category | flops | bytes accessed | tf_op | source)
XLA Modules:
  0.0 45.3 jit_solution(9053816526550418128)
XLA Ops:
  0.7 1.2 %shard_map.109 = (f32[256,128]{1,0:T(8,128)S(1)}, f32[272,128]{1,0:T(8,128)S(1)}, f32[1,8,4096]{2,1,0:T(8,128)S(1)}, f32[1,8,4096]{2,1,0:T(8,128)S(1)}, s32[1,8]...) custom-call(s32[1,1]{1,0:T(1,128)S(6)} %copy.13.count, s32[1,8]{1,0:T(1,128)} %refs_0_.1, ...), custom_call_target="tpu_custom_call" | custom-call | flops 1024 | bytes 1024 | tf_op jit(solution)/shard_map/pallas_call | solution.py:200
  1.9 3.7 %collective-permute-start.4 = (f32[272,128]{1,0:T(8,128)S(1)}, f32[272,128]{1,0:T(8,128)S(1)}, u32[]{:S(2)}, u32[]{:S(2)}) collective-permute-start(f32[272,128]{1,0:T(8,128)S(1)} %get-tuple-element.31), channel_id=1, source_target_pairs={{0,24},{1,25},{2,26},{3,27},{4,28},{5,29},{6,30},{7,31},{8,16},{9,... | collective-permute-start | bytes 417800 | tf_op jit(solution)/shard_map/ppermute | solution.py:229
  7.8 1.6 %collective-permute-start.7 = (f32[280,128]{1,0:T(8,128)S(1)}, f32[280,128]{1,0:T(8,128)S(1)}, u32[]{:S(2)}, u32[]{:S(2)}) collective-permute-start(f32[280,128]{1,0:T(8,128)S(1)} %get-tuple-element.33), channel_id=1, source_target_pairs={{0,4},{1,5},{2,6},{3,7},{4,0},{5,1},{6,2},{7,3},{8,12},{9,13},{10,... | collective-permute-start | bytes 430088 | tf_op jit(solution)/shard_map/ppermute | solution.py:229
  9.4 0.5 %collective-permute-start.8 = (f32[280,128]{1,0:T(8,128)S(1)}, f32[280,128]{1,0:T(8,128)S(1)}, u32[]{:S(2)}, u32[]{:S(2)}) collective-permute-start(f32[280,128]{1,0:T(8,128)S(1)} %get-tuple-element.33), channel_id=1, source_target_pairs={{0,2},{1,3},{2,0},{3,1},{4,6},{5,7},{6,4},{7,5},{8,10},{9,11},{10,... | collective-permute-start | bytes 430088 | tf_op jit(solution)/shard_map/ppermute | solution.py:229
  10.0 1.4 %collective-permute-start.6 = (f32[256,128]{1,0:T(8,128)S(1)}, f32[256,128]{1,0:T(8,128)S(1)}, u32[]{:S(2)}, u32[]{:S(2)}) collective-permute-start(f32[256,128]{1,0:T(8,128)S(1)} %get-tuple-element.32.refs_3_), channel_id=1, source_target_pairs={{0,6},{1,7},{2,4},{3,5},{4,2},{5,3},{6,0},{7,1},{8,14},{9,15},{10,... | collective-permute-start | bytes 393224 | tf_op jit(solution)/shard_map/ppermute | solution.py:229
  11.4 2.1 %collective-permute-start.5 = (f32[256,128]{1,0:T(8,128)S(1)}, f32[256,128]{1,0:T(8,128)S(1)}, u32[]{:S(2)}, u32[]{:S(2)}) collective-permute-start(f32[256,128]{1,0:T(8,128)S(1)} %shard_map.112), channel_id=1, source_target_pairs={{0,8},{1,9},{2,10},{3,11},{4,12},{5,13},{6,14},{7,15},{8,0},{9,1},... | collective-permute-start | bytes 393224 | tf_op jit(solution)/shard_map/ppermute | solution.py:229
  13.5 3.6 %collective-permute-done.6.refs_4_ = f32[256,128]{1,0:T(8,128)S(1)} collective-permute-done((f32[256,128]{1,0:T(8,128)S(1)}, f32[256,128]{1,0:T(8,128)S(1)}, u32[]{:S(2)}, u32[]{:S(2)}) %collective-permute-start.6) | collective-permute-done | bytes 131104 | tf_op jit(solution)/shard_map/ppermute | solution.py:229
  17.6 0.5 %collective-permute-start.11 = (f32[256,128]{1,0:T(8,128)S(1)}, f32[256,128]{1,0:T(8,128)S(1)}, u32[]{:S(2)}, u32[]{:S(2)}) collective-permute-start(f32[256,128]{1,0:T(8,128)S(1)} %get-tuple-element.36), channel_id=1, source_target_pairs={{0,1},{1,0},{2,3},{3,2},{4,5},{5,4},{6,7},{7,6},{8,9},{9,8},{10,11... | collective-permute-start | bytes 393224 | tf_op jit(solution)/shard_map/ppermute | solution.py:229
  18.9 1.3 %collective-permute-start.2 = (f32[280,128]{1,0:T(8,128)S(1)}, f32[280,128]{1,0:T(8,128)S(1)}, u32[]{:S(2)}, u32[]{:S(2)}) collective-permute-start(f32[280,128]{1,0:T(8,128)S(1)} %get-tuple-element.30.refs_2_), channel_id=1, source_target_pairs={{0,8},{1,9},{2,10},{3,11},{4,12},{5,13},{6,14},{7,15},{8,0},{9,1},... | collective-permute-start | bytes 430088 | tf_op jit(solution)/shard_map/ppermute | solution.py:229
  20.2 0.5 %shard_map.115.refs_3_ = f32[264,128]{1,0:T(8,128)S(1)} custom-call(f32[1024,128]{1,0:T(8,128)S(1)} %shard_map.113.x.refs_0_, f32[256,128]{1,0:T(8,128)S(1)} %collective-permute-done.9.refs_1_, f32[256,128]{1,0:T(8,128)S(1)} %collective-permute-done.10.refs_2_, f32[256,128]{1,0:T(8,128)S(1)} %collective-permute-done.11.refs_3_, ...), custom_call_target="tpu_custom_call" | custom-call | flops 1024 | bytes 1024 | tf_op jit(solution)/shard_map/pallas_call | solution.py:200
  20.8 1.6 %collective-permute-start.13 = (f32[264,128]{1,0:T(8,128)S(1)}, f32[264,128]{1,0:T(8,128)S(1)}, u32[]{:S(2)}, u32[]{:S(2)}) collective-permute-start(f32[264,128]{1,0:T(8,128)S(1)} %shard_map.115.refs_3_), channel_id=1, source_target_pairs={{0,6},{1,7},{2,4},{3,5},{4,2},{5,3},{6,0},{7,1},{8,14},{9,15},{10,... | collective-permute-start | bytes 405512 | tf_op jit(solution)/shard_map/ppermute | solution.py:229
  22.4 0.7 %collective-permute-start.14 = (f32[264,128]{1,0:T(8,128)S(1)}, f32[264,128]{1,0:T(8,128)S(1)}, u32[]{:S(2)}, u32[]{:S(2)}) collective-permute-start(f32[264,128]{1,0:T(8,128)S(1)} %shard_map.115.refs_3_), channel_id=1, source_target_pairs={{0,4},{1,5},{2,6},{3,7},{4,0},{5,1},{6,2},{7,3},{8,12},{9,13},{10,... | collective-permute-start | bytes 405512 | tf_op jit(solution)/shard_map/ppermute | solution.py:229
  23.1 1.2 %collective-permute-start.15 = (f32[264,128]{1,0:T(8,128)S(1)}, f32[264,128]{1,0:T(8,128)S(1)}, u32[]{:S(2)}, u32[]{:S(2)}) collective-permute-start(f32[264,128]{1,0:T(8,128)S(1)} %shard_map.115.refs_3_), channel_id=1, source_target_pairs={{0,2},{1,3},{2,0},{3,1},{4,6},{5,7},{6,4},{7,5},{8,10},{9,11},{10,... | collective-permute-start | bytes 405512 | tf_op jit(solution)/shard_map/ppermute | solution.py:229
  25.2 1.5 %collective-permute-done.2.refs_2_.refs_5_ = f32[280,128]{1,0:T(8,128)S(1)} collective-permute-done((f32[280,128]{1,0:T(8,128)S(1)}, f32[280,128]{1,0:T(8,128)S(1)}, u32[]{:S(2)}, u32[]{:S(2)}) %collective-permute-start.2) | collective-permute-done | bytes 143392 | tf_op jit(solution)/shard_map/ppermute | solution.py:229
  26.6 3.2 %collective-permute-done.1.refs_1_.refs_4_ = f32[256,128]{1,0:T(8,128)S(1)} collective-permute-done((f32[256,128]{1,0:T(8,128)S(1)}, f32[256,128]{1,0:T(8,128)S(1)}, u32[]{:S(2)}, u32[]{:S(2)}) %collective-permute-start.1) | collective-permute-done | bytes 131104 | tf_op jit(solution)/shard_map/ppermute | solution.py:229
  30.3 1.9 %collective-permute-done.16.refs_1_ = f32[1024,128]{1,0:T(8,128)S(1)} collective-permute-done((f32[1024,128]{1,0:T(8,128)S(1)}, f32[1024,128]{1,0:T(8,128)S(1)}, u32[]{:S(2)}, u32[]{:S(2)}) %collective-permute-start.16) | collective-permute-done | bytes 524320 | tf_op jit(solution)/shard_map/ppermute | solution.py:229
  32.2 0.5 %shard_map.117 = (f32[264,128]{1,0:T(8,128)S(1)}, f32[128,128]{1,0:T(8,128)S(1)}, f32[128,128]{1,0:T(8,128)S(1)}) custom-call(f32[1024,128]{1,0:T(8,128)S(1)} %shard_map.116.refs_0_, f32[1024,128]{1,0:T(8,128)S(1)} %collective-permute-done.16.refs_1_, f32[280,128]{1,0:T(8,128)S(1)} %get-tuple-element.30.refs_2_, ...), custom_call_target="tpu_custom_call" | custom-call | flops 1024 | bytes 1024 | tf_op jit(solution)/shard_map/pallas_call | solution.py:200
  32.8 1.1 %collective-permute-start.17 = (f32[128,128]{1,0:T(8,128)S(1)}, f32[128,128]{1,0:T(8,128)S(1)}, u32[]{:S(2)}, u32[]{:S(2)}) collective-permute-start(f32[128,128]{1,0:T(8,128)S(1)} %get-tuple-element.41.refs_3_), channel_id=1, source_target_pairs={{0,2},{1,3},{2,0},{3,1},{4,16},{5,17},{6,24},{7,25},{8,10},{9,11},... | collective-permute-start | bytes 196616 | tf_op jit(solution)/shard_map/ppermute | solution.py:229
  33.9 1.0 %collective-permute-start.18 = (f32[128,128]{1,0:T(8,128)S(1)}, f32[128,128]{1,0:T(8,128)S(1)}, u32[]{:S(2)}, u32[]{:S(2)}) collective-permute-start(f32[128,128]{1,0:T(8,128)S(1)} %get-tuple-element.42), channel_id=1, source_target_pairs={{0,1},{1,0},{2,9},{3,8},{4,17},{5,16},{6,25},{7,24},{8,3},{9,2},{1... | collective-permute-start | bytes 196616 | tf_op jit(solution)/shard_map/ppermute | solution.py:229
  34.9 0.7 %collective-permute-start.20 = (f32[128,128]{1,0:T(8,128)S(1)}, f32[128,128]{1,0:T(8,128)S(1)}, u32[]{:S(2)}, u32[]{:S(2)}) collective-permute-start(f32[128,128]{1,0:T(8,128)S(1)} %get-tuple-element.42), channel_id=1, source_target_pairs={{0,1},{1,0},{2,3},{3,2},{4,5},{5,4},{6,7},{7,6},{8,9},{9,8},{10,11... | collective-permute-start | bytes 196616 | tf_op jit(solution)/shard_map/ppermute | solution.py:229
  35.5 1.6 %collective-permute-done.17.refs_0_ = f32[128,128]{1,0:T(8,128)S(1)} collective-permute-done((f32[128,128]{1,0:T(8,128)S(1)}, f32[128,128]{1,0:T(8,128)S(1)}, u32[]{:S(2)}, u32[]{:S(2)}) %collective-permute-start.17) | collective-permute-done | bytes 65568 | tf_op jit(solution)/shard_map/ppermute | solution.py:229
  37.1 1.3 %collective-permute-start.19 = (f32[128,128]{1,0:T(8,128)S(1)}, f32[128,128]{1,0:T(8,128)S(1)}, u32[]{:S(2)}, u32[]{:S(2)}) collective-permute-start(f32[128,128]{1,0:T(8,128)S(1)} %collective-permute-done.17.refs_0_), channel_id=1, source_target_pairs={{0,8},{1,9},{10,2},{11,3},{20,28},{21,29},{30,22},{31,23}} | collective-permute-start | bytes 196616 | tf_op jit(solution)/shard_map/ppermute | solution.py:229
  38.4 5.9 %collective-permute-done.18.refs_1_ = f32[128,128]{1,0:T(8,128)S(1)} collective-permute-done((f32[128,128]{1,0:T(8,128)S(1)}, f32[128,128]{1,0:T(8,128)S(1)}, u32[]{:S(2)}, u32[]{:S(2)}) %collective-permute-start.18) | collective-permute-done | bytes 65568 | tf_op jit(solution)/shard_map/ppermute | solution.py:229
  44.3 1.0 %shard_map.118 = f32[1,8,4096]{2,1,0:T(8,128)} custom-call(s32[1,8]{1,0:T(1,128)S(1)} %get-tuple-element.24.xp.places, s32[1,1]{1,0:T(1,128)S(6)} %copy.15.xc.count, f32[264,128]{1,0:T(8,128)S(1)} %get-tuple-element.40.x, f32[128,128]{1,0:T(8,128)S(1)} %collective-permute-done.17.refs_0_, f32[128,128]{1,0:T(8,128)S(1)} %collective-permute-done.18.refs_1_, ...), custom_call_target="tpu_custom_call" | custom-call | flops 1024 | bytes 1024 | tf_op jit(solution)/shard_map/pallas_call | solution.py:200
  (28 shorter events, 2.9 us)
Async XLA Ops:
  1.9 9.5 %collective-permute-start.4 = (f32[272,128]{1,0:T(8,128)S(1)}, f32[272,128]{1,0:T(8,128)S(1)}, u32[]{:S(2)}, u32[]{:S(2)}) collective-permute-start(f32[272,128]{1,0:T(8,128)S(1)} %get-tuple-element.31), channel_id=1, source_target_pairs={{0,24},{1,25},{2,26},{3,27},{4,28},{5,29},{6,30},{7,31},{8,16},{9,... | collective-permute-start | bytes 417800 | tf_op jit(solution)/shard_map/ppermute | solution.py:229
  7.8 9.6 %collective-permute-start.7 = (f32[280,128]{1,0:T(8,128)S(1)}, f32[280,128]{1,0:T(8,128)S(1)}, u32[]{:S(2)}, u32[]{:S(2)}) collective-permute-start(f32[280,128]{1,0:T(8,128)S(1)} %get-tuple-element.33), channel_id=1, source_target_pairs={{0,4},{1,5},{2,6},{3,7},{4,0},{5,1},{6,2},{7,3},{8,12},{9,13},{10,... | collective-permute-start | bytes 430088 | tf_op jit(solution)/shard_map/ppermute | solution.py:229
  9.4 8.0 %collective-permute-start.8 = (f32[280,128]{1,0:T(8,128)S(1)}, f32[280,128]{1,0:T(8,128)S(1)}, u32[]{:S(2)}, u32[]{:S(2)}) collective-permute-start(f32[280,128]{1,0:T(8,128)S(1)} %get-tuple-element.33), channel_id=1, source_target_pairs={{0,2},{1,3},{2,0},{3,1},{4,6},{5,7},{6,4},{7,5},{8,10},{9,11},{10,... | collective-permute-start | bytes 430088 | tf_op jit(solution)/shard_map/ppermute | solution.py:229
  10.0 7.5 %collective-permute-start.3 = (f32[272,128]{1,0:T(8,128)S(1)}, f32[272,128]{1,0:T(8,128)S(1)}, u32[]{:S(2)}, u32[]{:S(2)}) collective-permute-start(f32[272,128]{1,0:T(8,128)S(1)} %get-tuple-element.31), channel_id=1, source_target_pairs={{0,8},{1,9},{2,10},{3,11},{4,12},{5,13},{6,14},{7,15},{8,0},{9,1},... | collective-permute-start | bytes 417800 | tf_op jit(solution)/shard_map/ppermute | solution.py:229
  10.0 7.2 %collective-permute-start.6 = (f32[256,128]{1,0:T(8,128)S(1)}, f32[256,128]{1,0:T(8,128)S(1)}, u32[]{:S(2)}, u32[]{:S(2)}) collective-permute-start(f32[256,128]{1,0:T(8,128)S(1)} %get-tuple-element.32.refs_3_), channel_id=1, source_target_pairs={{0,6},{1,7},{2,4},{3,5},{4,2},{5,3},{6,0},{7,1},{8,14},{9,15},{10,... | collective-permute-start | bytes 393224 | tf_op jit(solution)/shard_map/ppermute | solution.py:229
  11.4 6.0 %collective-permute-start.5 = (f32[256,128]{1,0:T(8,128)S(1)}, f32[256,128]{1,0:T(8,128)S(1)}, u32[]{:S(2)}, u32[]{:S(2)}) collective-permute-start(f32[256,128]{1,0:T(8,128)S(1)} %shard_map.112), channel_id=1, source_target_pairs={{0,8},{1,9},{2,10},{3,11},{4,12},{5,13},{6,14},{7,15},{8,0},{9,1},... | collective-permute-start | bytes 393224 | tf_op jit(solution)/shard_map/ppermute | solution.py:229
  17.1 7.7 %collective-permute-start = (f32[296,128]{1,0:T(8,128)S(1)}, f32[296,128]{1,0:T(8,128)S(1)}, u32[]{:S(2)}, u32[]{:S(2)}) collective-permute-start(f32[296,128]{1,0:T(8,128)S(1)} %get-tuple-element.29), channel_id=1, source_target_pairs={{0,24},{1,25},{2,26},{3,27},{4,28},{5,29},{6,30},{7,31},{8,16},{9,... | collective-permute-start | bytes 454664 | tf_op jit(solution)/shard_map/ppermute | solution.py:229
  17.5 1.4 %collective-permute-start.10 = (f32[256,128]{1,0:T(8,128)S(1)}, f32[256,128]{1,0:T(8,128)S(1)}, u32[]{:S(2)}, u32[]{:S(2)}) collective-permute-start(f32[256,128]{1,0:T(8,128)S(1)} %get-tuple-element.35), channel_id=1, source_target_pairs={{0,1},{1,0},{2,3},{3,2},{4,5},{5,4},{6,7},{7,6},{8,9},{9,8},{10,11... | collective-permute-start | bytes 393224 | tf_op jit(solution)/shard_map/ppermute | solution.py:229
  17.6 2.6 %collective-permute-start.11 = (f32[256,128]{1,0:T(8,128)S(1)}, f32[256,128]{1,0:T(8,128)S(1)}, u32[]{:S(2)}, u32[]{:S(2)}) collective-permute-start(f32[256,128]{1,0:T(8,128)S(1)} %get-tuple-element.36), channel_id=1, source_target_pairs={{0,1},{1,0},{2,3},{3,2},{4,5},{5,4},{6,7},{7,6},{8,9},{9,8},{10,11... | collective-permute-start | bytes 393224 | tf_op jit(solution)/shard_map/ppermute | solution.py:229
  18.1 2.1 %collective-permute-start.12 = (f32[256,128]{1,0:T(8,128)S(1)}, f32[256,128]{1,0:T(8,128)S(1)}, u32[]{:S(2)}, u32[]{:S(2)}) collective-permute-start(f32[256,128]{1,0:T(8,128)S(1)} %get-tuple-element.37), channel_id=1, source_target_pairs={{0,1},{1,0},{2,3},{3,2},{4,5},{5,4},{6,7},{7,6},{8,9},{9,8},{10,11... | collective-permute-start | bytes 393224 | tf_op jit(solution)/shard_map/ppermute | solution.py:229
  18.2 2.0 %collective-permute-start.9 = (f32[256,128]{1,0:T(8,128)S(1)}, f32[256,128]{1,0:T(8,128)S(1)}, u32[]{:S(2)}, u32[]{:S(2)}) collective-permute-start(f32[256,128]{1,0:T(8,128)S(1)} %get-tuple-element.34), channel_id=1, source_target_pairs={{0,1},{1,0},{2,3},{3,2},{4,5},{5,4},{6,7},{7,6},{8,9},{9,8},{10,11... | collective-permute-start | bytes 393224 | tf_op jit(solution)/shard_map/ppermute | solution.py:229
  18.9 7.7 %collective-permute-start.2 = (f32[280,128]{1,0:T(8,128)S(1)}, f32[280,128]{1,0:T(8,128)S(1)}, u32[]{:S(2)}, u32[]{:S(2)}) collective-permute-start(f32[280,128]{1,0:T(8,128)S(1)} %get-tuple-element.30.refs_2_), channel_id=1, source_target_pairs={{0,8},{1,9},{2,10},{3,11},{4,12},{5,13},{6,14},{7,15},{8,0},{9,1},... | collective-permute-start | bytes 430088 | tf_op jit(solution)/shard_map/ppermute | solution.py:229
  20.8 9.1 %collective-permute-start.13 = (f32[264,128]{1,0:T(8,128)S(1)}, f32[264,128]{1,0:T(8,128)S(1)}, u32[]{:S(2)}, u32[]{:S(2)}) collective-permute-start(f32[264,128]{1,0:T(8,128)S(1)} %shard_map.115.refs_3_), channel_id=1, source_target_pairs={{0,6},{1,7},{2,4},{3,5},{4,2},{5,3},{6,0},{7,1},{8,14},{9,15},{10,... | collective-permute-start | bytes 405512 | tf_op jit(solution)/shard_map/ppermute | solution.py:229
  22.4 7.6 %collective-permute-start.14 = (f32[264,128]{1,0:T(8,128)S(1)}, f32[264,128]{1,0:T(8,128)S(1)}, u32[]{:S(2)}, u32[]{:S(2)}) collective-permute-start(f32[264,128]{1,0:T(8,128)S(1)} %shard_map.115.refs_3_), channel_id=1, source_target_pairs={{0,4},{1,5},{2,6},{3,7},{4,0},{5,1},{6,2},{7,3},{8,12},{9,13},{10,... | collective-permute-start | bytes 405512 | tf_op jit(solution)/shard_map/ppermute | solution.py:229
  23.1 7.1 %collective-permute-start.15 = (f32[264,128]{1,0:T(8,128)S(1)}, f32[264,128]{1,0:T(8,128)S(1)}, u32[]{:S(2)}, u32[]{:S(2)}) collective-permute-start(f32[264,128]{1,0:T(8,128)S(1)} %shard_map.115.refs_3_), channel_id=1, source_target_pairs={{0,2},{1,3},{2,0},{3,1},{4,6},{5,7},{6,4},{7,5},{8,10},{9,11},{10,... | collective-permute-start | bytes 405512 | tf_op jit(solution)/shard_map/ppermute | solution.py:229
  24.8 5.0 %collective-permute-start.1 = (f32[256,128]{1,0:T(8,128)S(1)}, f32[256,128]{1,0:T(8,128)S(1)}, u32[]{:S(2)}, u32[]{:S(2)}) collective-permute-start(f32[256,128]{1,0:T(8,128)S(1)} %shard_map.111), channel_id=1, source_target_pairs={{0,8},{1,9},{2,10},{3,11},{4,12},{5,13},{6,14},{7,15},{8,0},{9,1},... | collective-permute-start | bytes 393224 | tf_op jit(solution)/shard_map/ppermute | solution.py:229
  30.2 2.0 %collective-permute-start.16 = (f32[1024,128]{1,0:T(8,128)S(1)}, f32[1024,128]{1,0:T(8,128)S(1)}, u32[]{:S(2)}, u32[]{:S(2)}) collective-permute-start(f32[1024,128]{1,0:T(8,128)S(1)} %shard_map.116.refs_0_), channel_id=1, source_target_pairs={{0,1},{1,0},{2,3},{3,2},{4,5},{5,4},{6,7},{7,6},{8,9},{9,8},{10,11... | collective-permute-start | bytes 1572872 | tf_op jit(solution)/shard_map/ppermute | solution.py:229
  32.8 4.3 %collective-permute-start.17 = (f32[128,128]{1,0:T(8,128)S(1)}, f32[128,128]{1,0:T(8,128)S(1)}, u32[]{:S(2)}, u32[]{:S(2)}) collective-permute-start(f32[128,128]{1,0:T(8,128)S(1)} %get-tuple-element.41.refs_3_), channel_id=1, source_target_pairs={{0,2},{1,3},{2,0},{3,1},{4,16},{5,17},{6,24},{7,25},{8,10},{9,11},... | collective-permute-start | bytes 196616 | tf_op jit(solution)/shard_map/ppermute | solution.py:229
  33.9 10.4 %collective-permute-start.18 = (f32[128,128]{1,0:T(8,128)S(1)}, f32[128,128]{1,0:T(8,128)S(1)}, u32[]{:S(2)}, u32[]{:S(2)}) collective-permute-start(f32[128,128]{1,0:T(8,128)S(1)} %get-tuple-element.42), channel_id=1, source_target_pairs={{0,1},{1,0},{2,9},{3,8},{4,17},{5,16},{6,25},{7,24},{8,3},{9,2},{1... | collective-permute-start | bytes 196616 | tf_op jit(solution)/shard_map/ppermute | solution.py:229
  34.9 9.4 %collective-permute-start.20 = (f32[128,128]{1,0:T(8,128)S(1)}, f32[128,128]{1,0:T(8,128)S(1)}, u32[]{:S(2)}, u32[]{:S(2)}) collective-permute-start(f32[128,128]{1,0:T(8,128)S(1)} %get-tuple-element.42), channel_id=1, source_target_pairs={{0,1},{1,0},{2,3},{3,2},{4,5},{5,4},{6,7},{7,6},{8,9},{9,8},{10,11... | collective-permute-start | bytes 196616 | tf_op jit(solution)/shard_map/ppermute | solution.py:229
  37.1 7.2 %collective-permute-start.19 = (f32[128,128]{1,0:T(8,128)S(1)}, f32[128,128]{1,0:T(8,128)S(1)}, u32[]{:S(2)}, u32[]{:S(2)}) collective-permute-start(f32[128,128]{1,0:T(8,128)S(1)} %collective-permute-done.17.refs_0_), channel_id=1, source_target_pairs={{0,8},{1,9},{10,2},{11,3},{20,28},{21,29},{30,22},{31,23}} | collective-permute-start | bytes 196616 | tf_op jit(solution)/shard_map/ppermute | solution.py:229

commit v8 on v7

--- a/solution.py
+++ b/solution.py
@@ -265,7 +265,7 @@
     )
     h_far, h_near, s_near, s_far, mask = call(
         rest_kernel,
-        [tile, sized(24), sized(24), sized(40), jax.ShapeDtypeStruct((max(8, cap // 2), LANES), f32)],
+        [tile, sized(32), sized(24), sized(40), jax.ShapeDtypeStruct((max(8, cap // 2), LANES), f32)],
         [VMEM] * 5 + [SMEM] * 3,
         [lines],
         1 << 10,
@@ -343,7 +343,7 @@
         mirrors += [
             send(mirrors[0], lambda r, m, k: (r ^ 1, m, k) if r == m else None),
             sent[0],
-            to_other(sent[1]),
+            send(sent[1], lambda r, m, k: (r, m, 1 - k) if r == m else None),
         ]
     return call(
         functools.partial(slots_kernel, cap, sends),

time: 45.8 us -> 45.6 us (level)
  the two profiles are of different devices: /device:TPU:2 before, /device:TPU:0 now
where the time goes in v8:
time: 45.6 us; the launch traced here: 45.4 us
  starting transfers between devices  24.7 us (54%)
  waiting for transfers between devices  14.2 us (31%)
  Pallas kernels  3.76 us (8%)
  between operations  2.71 us (6%)
    ppermute x21, starting transfers between devices, send(): return lax.ppermute(value, AXES, pairs)  24.7 us
    ppermute x21, waiting for transfers between devices, send(): return lax.ppermute(value, AXES, pairs)  14.2 us
    pallas_call x10, Pallas kernels, call(): pl.pallas_call(kernel, out_shape=out_shapes, in_specs=in_specs, out_specs...  3.76 us
  transfers between devices with their start and end apart: 21, of which 10 were waited for; matrix products, arithmetic and copies ran while one was open for 0% of the time, Pallas kernels for 2%

profile of v8, /device:TPU:0, one launch (start us, length us, event | category | flops | bytes accessed | tf_op | source)
XLA Modules:
  0.0 45.4 jit_solution(3480330134477583773)
XLA Ops:
  0.7 1.2 %shard_map.109 = (f32[256,128]{1,0:T(8,128)S(1)}, f32[272,128]{1,0:T(8,128)S(1)}, f32[1,8,4096]{2,1,0:T(8,128)S(1)}, f32[1,8,4096]{2,1,0:T(8,128)S(1)}, s32[1,8]...) custom-call(s32[1,1]{1,0:T(1,128)S(6)} %copy.13.count, s32[1,8]{1,0:T(1,128)} %refs_0_.1, ...), custom_call_target="tpu_custom_call" | custom-call | flops 1024 | bytes 1024 | tf_op jit(solution)/shard_map/pallas_call | solution.py:200
  1.9 5.1 %collective-permute-start.4 = (f32[272,128]{1,0:T(8,128)S(1)}, f32[272,128]{1,0:T(8,128)S(1)}, u32[]{:S(2)}, u32[]{:S(2)}) collective-permute-start(f32[272,128]{1,0:T(8,128)S(1)} %get-tuple-element.31), channel_id=1, source_target_pairs={{0,24},{1,25},{2,26},{3,27},{4,28},{5,29},{6,30},{7,31},{8,16},{9,... | collective-permute-start | bytes 417800 | tf_op jit(solution)/shard_map/ppermute | solution.py:229
  9.3 1.6 %collective-permute-start.7 = (f32[288,128]{1,0:T(8,128)S(1)}, f32[288,128]{1,0:T(8,128)S(1)}, u32[]{:S(2)}, u32[]{:S(2)}) collective-permute-start(f32[288,128]{1,0:T(8,128)S(1)} %get-tuple-element.33), channel_id=1, source_target_pairs={{0,4},{1,5},{2,6},{3,7},{4,0},{5,1},{6,2},{7,3},{8,12},{9,13},{10,... | collective-permute-start | bytes 442376 | tf_op jit(solution)/shard_map/ppermute | solution.py:229
  10.9 1.5 %collective-permute-start.8 = (f32[288,128]{1,0:T(8,128)S(1)}, f32[288,128]{1,0:T(8,128)S(1)}, u32[]{:S(2)}, u32[]{:S(2)}) collective-permute-start(f32[288,128]{1,0:T(8,128)S(1)} %get-tuple-element.33), channel_id=1, source_target_pairs={{0,2},{1,3},{2,0},{3,1},{4,6},{5,7},{6,4},{7,5},{8,10},{9,11},{10,... | collective-permute-start | bytes 442376 | tf_op jit(solution)/shard_map/ppermute | solution.py:229
  12.9 2.1 %collective-permute-start.5 = (f32[256,128]{1,0:T(8,128)S(1)}, f32[256,128]{1,0:T(8,128)S(1)}, u32[]{:S(2)}, u32[]{:S(2)}) collective-permute-start(f32[256,128]{1,0:T(8,128)S(1)} %shard_map.112), channel_id=1, source_target_pairs={{0,8},{1,9},{2,10},{3,11},{4,12},{5,13},{6,14},{7,15},{8,0},{9,1},... | collective-permute-start | bytes 393224 | tf_op jit(solution)/shard_map/ppermute | solution.py:229
  14.9 3.8 %collective-permute-done.6.refs_4_ = f32[256,128]{1,0:T(8,128)S(1)} collective-permute-done((f32[256,128]{1,0:T(8,128)S(1)}, f32[256,128]{1,0:T(8,128)S(1)}, u32[]{:S(2)}, u32[]{:S(2)}) %collective-permute-start.6) | collective-permute-done | bytes 131104 | tf_op jit(solution)/shard_map/ppermute | solution.py:229
  19.1 0.6 %collective-permute-done.5.refs_1_.refs_7_ = f32[256,128]{1,0:T(8,128)S(1)} collective-permute-done((f32[256,128]{1,0:T(8,128)S(1)}, f32[256,128]{1,0:T(8,128)S(1)}, u32[]{:S(2)}, u32[]{:S(2)}) %collective-permute-start.5) | collective-permute-done | bytes 131104 | tf_op jit(solution)/shard_map/ppermute | solution.py:229
  21.2 0.6 %collective-permute-start.2 = (f32[280,128]{1,0:T(8,128)S(1)}, f32[280,128]{1,0:T(8,128)S(1)}, u32[]{:S(2)}, u32[]{:S(2)}) collective-permute-start(f32[280,128]{1,0:T(8,128)S(1)} %get-tuple-element.30.refs_2_), channel_id=1, source_target_pairs={{0,8},{1,9},{2,10},{3,11},{4,12},{5,13},{6,14},{7,15},{8,0},{9,1},... | collective-permute-start | bytes 430088 | tf_op jit(solution)/shard_map/ppermute | solution.py:229
  21.9 0.5 %shard_map.115.refs_3_ = f32[264,128]{1,0:T(8,128)S(1)} custom-call(f32[1024,128]{1,0:T(8,128)S(1)} %shard_map.113.x.refs_0_, f32[256,128]{1,0:T(8,128)S(1)} %collective-permute-done.9.refs_1_, f32[256,128]{1,0:T(8,128)S(1)} %collective-permute-done.10.refs_2_, f32[256,128]{1,0:T(8,128)S(1)} %collective-permute-done.11.refs_3_, ...), custom_call_target="tpu_custom_call" | custom-call | flops 1024 | bytes 1024 | tf_op jit(solution)/shard_map/pallas_call | solution.py:200
  22.5 2.2 %collective-permute-start.13 = (f32[264,128]{1,0:T(8,128)S(1)}, f32[264,128]{1,0:T(8,128)S(1)}, u32[]{:S(2)}, u32[]{:S(2)}) collective-permute-start(f32[264,128]{1,0:T(8,128)S(1)} %shard_map.115.refs_3_), channel_id=1, source_target_pairs={{0,6},{1,7},{2,4},{3,5},{4,2},{5,3},{6,0},{7,1},{8,14},{9,15},{10,... | collective-permute-start | bytes 405512 | tf_op jit(solution)/shard_map/ppermute | solution.py:229
  24.7 0.5 %collective-permute-start.14 = (f32[264,128]{1,0:T(8,128)S(1)}, f32[264,128]{1,0:T(8,128)S(1)}, u32[]{:S(2)}, u32[]{:S(2)}) collective-permute-start(f32[264,128]{1,0:T(8,128)S(1)} %shard_map.115.refs_3_), channel_id=1, source_target_pairs={{0,4},{1,5},{2,6},{3,7},{4,0},{5,1},{6,2},{7,3},{8,12},{9,13},{10,... | collective-permute-start | bytes 405512 | tf_op jit(solution)/shard_map/ppermute | solution.py:229
  25.2 0.8 %collective-permute-start.15 = (f32[264,128]{1,0:T(8,128)S(1)}, f32[264,128]{1,0:T(8,128)S(1)}, u32[]{:S(2)}, u32[]{:S(2)}) collective-permute-start(f32[264,128]{1,0:T(8,128)S(1)} %shard_map.115.refs_3_), channel_id=1, source_target_pairs={{0,2},{1,3},{2,0},{3,1},{4,6},{5,7},{6,4},{7,5},{8,10},{9,11},{10,... | collective-permute-start | bytes 405512 | tf_op jit(solution)/shard_map/ppermute | solution.py:229
  26.1 1.5 %collective-permute-start.1 = (f32[256,128]{1,0:T(8,128)S(1)}, f32[256,128]{1,0:T(8,128)S(1)}, u32[]{:S(2)}, u32[]{:S(2)}) collective-permute-start(f32[256,128]{1,0:T(8,128)S(1)} %shard_map.111), channel_id=1, source_target_pairs={{0,8},{1,9},{2,10},{3,11},{4,12},{5,13},{6,14},{7,15},{8,0},{9,1},... | collective-permute-start | bytes 393224 | tf_op jit(solution)/shard_map/ppermute | solution.py:229
  27.6 1.3 %collective-permute-done.2.refs_2_.refs_5_ = f32[280,128]{1,0:T(8,128)S(1)} collective-permute-done((f32[280,128]{1,0:T(8,128)S(1)}, f32[280,128]{1,0:T(8,128)S(1)}, u32[]{:S(2)}, u32[]{:S(2)}) %collective-permute-start.2) | collective-permute-done | bytes 143392 | tf_op jit(solution)/shard_map/ppermute | solution.py:229
  28.9 2.6 %collective-permute-done.1.refs_1_.refs_4_ = f32[256,128]{1,0:T(8,128)S(1)} collective-permute-done((f32[256,128]{1,0:T(8,128)S(1)}, f32[256,128]{1,0:T(8,128)S(1)}, u32[]{:S(2)}, u32[]{:S(2)}) %collective-permute-start.1) | collective-permute-done | bytes 131104 | tf_op jit(solution)/shard_map/ppermute | solution.py:229
  31.5 0.7 %collective-permute-done.14.refs_5_ = f32[264,128]{1,0:T(8,128)S(1)} collective-permute-done((f32[264,128]{1,0:T(8,128)S(1)}, f32[264,128]{1,0:T(8,128)S(1)}, u32[]{:S(2)}, u32[]{:S(2)}) %collective-permute-start.14) | collective-permute-done | bytes 135200 | tf_op jit(solution)/shard_map/ppermute | solution.py:229
  32.3 1.9 %collective-permute-done.16.refs_1_ = f32[1024,128]{1,0:T(8,128)S(1)} collective-permute-done((f32[1024,128]{1,0:T(8,128)S(1)}, f32[1024,128]{1,0:T(8,128)S(1)}, u32[]{:S(2)}, u32[]{:S(2)}) %collective-permute-start.16) | collective-permute-done | bytes 524320 | tf_op jit(solution)/shard_map/ppermute | solution.py:229
  34.2 0.5 %shard_map.117 = (f32[264,128]{1,0:T(8,128)S(1)}, f32[128,128]{1,0:T(8,128)S(1)}, f32[128,128]{1,0:T(8,128)S(1)}) custom-call(f32[1024,128]{1,0:T(8,128)S(1)} %shard_map.116.refs_0_, f32[1024,128]{1,0:T(8,128)S(1)} %collective-permute-done.16.refs_1_, f32[280,128]{1,0:T(8,128)S(1)} %get-tuple-element.30.refs_2_, ...), custom_call_target="tpu_custom_call" | custom-call | flops 1024 | bytes 1024 | tf_op jit(solution)/shard_map/pallas_call | solution.py:200
  34.7 0.9 %collective-permute-start.17 = (f32[128,128]{1,0:T(8,128)S(1)}, f32[128,128]{1,0:T(8,128)S(1)}, u32[]{:S(2)}, u32[]{:S(2)}) collective-permute-start(f32[128,128]{1,0:T(8,128)S(1)} %get-tuple-element.41.refs_3_), channel_id=1, source_target_pairs={{0,2},{1,3},{2,0},{3,1},{4,16},{5,17},{6,24},{7,25},{8,10},{9,11},... | collective-permute-start | bytes 196616 | tf_op jit(solution)/shard_map/ppermute | solution.py:229
  35.7 2.4 %collective-permute-start.20 = (f32[128,128]{1,0:T(8,128)S(1)}, f32[128,128]{1,0:T(8,128)S(1)}, u32[]{:S(2)}, u32[]{:S(2)}) collective-permute-start(f32[128,128]{1,0:T(8,128)S(1)} %get-tuple-element.42), channel_id=1, source_target_pairs={{0,1},{1,0},{10,11},{11,10},{20,21},{21,20},{30,31},{31,30}} | collective-permute-start | bytes 196616 | tf_op jit(solution)/shard_map/ppermute | solution.py:229
  38.1 1.0 %collective-permute-done.17.refs_0_ = f32[128,128]{1,0:T(8,128)S(1)} collective-permute-done((f32[128,128]{1,0:T(8,128)S(1)}, f32[128,128]{1,0:T(8,128)S(1)}, u32[]{:S(2)}, u32[]{:S(2)}) %collective-permute-start.17) | collective-permute-done | bytes 65568 | tf_op jit(solution)/shard_map/ppermute | solution.py:229
  39.1 3.5 %collective-permute-start.19 = (f32[128,128]{1,0:T(8,128)S(1)}, f32[128,128]{1,0:T(8,128)S(1)}, u32[]{:S(2)}, u32[]{:S(2)}) collective-permute-start(f32[128,128]{1,0:T(8,128)S(1)} %collective-permute-done.17.refs_0_), channel_id=1, source_target_pairs={{0,8},{1,9},{10,2},{11,3},{20,28},{21,29},{30,22},{31,23}} | collective-permute-start | bytes 196616 | tf_op jit(solution)/shard_map/ppermute | solution.py:229
  42.6 1.9 %collective-permute-done.19.refs_2_ = f32[128,128]{1,0:T(8,128)S(1)} collective-permute-done((f32[128,128]{1,0:T(8,128)S(1)}, f32[128,128]{1,0:T(8,128)S(1)}, u32[]{:S(2)}, u32[]{:S(2)}) %collective-permute-start.19) | collective-permute-done | bytes 65568 | tf_op jit(solution)/shard_map/ppermute | solution.py:229
  44.4 1.0 %shard_map.118 = f32[1,8,4096]{2,1,0:T(8,128)} custom-call(s32[1,8]{1,0:T(1,128)S(1)} %get-tuple-element.24.xp.places, s32[1,1]{1,0:T(1,128)S(6)} %copy.15.xc.count, f32[264,128]{1,0:T(8,128)S(1)} %get-tuple-element.40.x, f32[128,128]{1,0:T(8,128)S(1)} %collective-permute-done.17.refs_0_, f32[128,128]{1,0:T(8,128)S(1)} %collective-permute-done.18.refs_1_, ...), custom_call_target="tpu_custom_call" | custom-call | flops 1024 | bytes 1024 | tf_op jit(solution)/shard_map/pallas_call | solution.py:200
  (28 shorter events, 3.0 us)
Async XLA Ops:
  1.9 11.0 %collective-permute-start.4 = (f32[272,128]{1,0:T(8,128)S(1)}, f32[272,128]{1,0:T(8,128)S(1)}, u32[]{:S(2)}, u32[]{:S(2)}) collective-permute-start(f32[272,128]{1,0:T(8,128)S(1)} %get-tuple-element.31), channel_id=1, source_target_pairs={{0,24},{1,25},{2,26},{3,27},{4,28},{5,29},{6,30},{7,31},{8,16},{9,... | collective-permute-start | bytes 417800 | tf_op jit(solution)/shard_map/ppermute | solution.py:229
  9.3 9.8 %collective-permute-start.7 = (f32[288,128]{1,0:T(8,128)S(1)}, f32[288,128]{1,0:T(8,128)S(1)}, u32[]{:S(2)}, u32[]{:S(2)}) collective-permute-start(f32[288,128]{1,0:T(8,128)S(1)} %get-tuple-element.33), channel_id=1, source_target_pairs={{0,4},{1,5},{2,6},{3,7},{4,0},{5,1},{6,2},{7,3},{8,12},{9,13},{10,... | collective-permute-start | bytes 442376 | tf_op jit(solution)/shard_map/ppermute | solution.py:229
  10.9 8.3 %collective-permute-start.8 = (f32[288,128]{1,0:T(8,128)S(1)}, f32[288,128]{1,0:T(8,128)S(1)}, u32[]{:S(2)}, u32[]{:S(2)}) collective-permute-start(f32[288,128]{1,0:T(8,128)S(1)} %get-tuple-element.33), channel_id=1, source_target_pairs={{0,2},{1,3},{2,0},{3,1},{4,6},{5,7},{6,4},{7,5},{8,10},{9,11},{10,... | collective-permute-start | bytes 442376 | tf_op jit(solution)/shard_map/ppermute | solution.py:229
  12.4 6.8 %collective-permute-start.3 = (f32[272,128]{1,0:T(8,128)S(1)}, f32[272,128]{1,0:T(8,128)S(1)}, u32[]{:S(2)}, u32[]{:S(2)}) collective-permute-start(f32[272,128]{1,0:T(8,128)S(1)} %get-tuple-element.31), channel_id=1, source_target_pairs={{0,8},{1,9},{2,10},{3,11},{4,12},{5,13},{6,14},{7,15},{8,0},{9,1},... | collective-permute-start | bytes 417800 | tf_op jit(solution)/shard_map/ppermute | solution.py:229
  12.4 6.4 %collective-permute-start.6 = (f32[256,128]{1,0:T(8,128)S(1)}, f32[256,128]{1,0:T(8,128)S(1)}, u32[]{:S(2)}, u32[]{:S(2)}) collective-permute-start(f32[256,128]{1,0:T(8,128)S(1)} %get-tuple-element.32.refs_3_), channel_id=1, source_target_pairs={{0,6},{1,7},{2,4},{3,5},{4,2},{5,3},{6,0},{7,1},{8,14},{9,15},{10,... | collective-permute-start | bytes 393224 | tf_op jit(solution)/shard_map/ppermute | solution.py:229
  12.9 6.9 %collective-permute-start.5 = (f32[256,128]{1,0:T(8,128)S(1)}, f32[256,128]{1,0:T(8,128)S(1)}, u32[]{:S(2)}, u32[]{:S(2)}) collective-permute-start(f32[256,128]{1,0:T(8,128)S(1)} %shard_map.112), channel_id=1, source_target_pairs={{0,8},{1,9},{2,10},{3,11},{4,12},{5,13},{6,14},{7,15},{8,0},{9,1},... | collective-permute-start | bytes 393224 | tf_op jit(solution)/shard_map/ppermute | solution.py:229
  18.8 7.3 %collective-permute-start = (f32[296,128]{1,0:T(8,128)S(1)}, f32[296,128]{1,0:T(8,128)S(1)}, u32[]{:S(2)}, u32[]{:S(2)}) collective-permute-start(f32[296,128]{1,0:T(8,128)S(1)} %get-tuple-element.29), channel_id=1, source_target_pairs={{0,24},{1,25},{2,26},{3,27},{4,28},{5,29},{6,30},{7,31},{8,16},{9,... | collective-permute-start | bytes 454664 | tf_op jit(solution)/shard_map/ppermute | solution.py:229
  19.8 1.4 %collective-permute-start.10 = (f32[256,128]{1,0:T(8,128)S(1)}, f32[256,128]{1,0:T(8,128)S(1)}, u32[]{:S(2)}, u32[]{:S(2)}) collective-permute-start(f32[256,128]{1,0:T(8,128)S(1)} %get-tuple-element.35), channel_id=1, source_target_pairs={{0,1},{1,0},{2,3},{3,2},{4,5},{5,4},{6,7},{7,6},{8,9},{9,8},{10,11... | collective-permute-start | bytes 393224 | tf_op jit(solution)/shard_map/ppermute | solution.py:229
  19.9 1.9 %collective-permute-start.11 = (f32[256,128]{1,0:T(8,128)S(1)}, f32[256,128]{1,0:T(8,128)S(1)}, u32[]{:S(2)}, u32[]{:S(2)}) collective-permute-start(f32[256,128]{1,0:T(8,128)S(1)} %get-tuple-element.36), channel_id=1, source_target_pairs={{0,1},{1,0},{2,3},{3,2},{4,5},{5,4},{6,7},{7,6},{8,9},{9,8},{10,11... | collective-permute-start | bytes 393224 | tf_op jit(solution)/shard_map/ppermute | solution.py:229
  20.4 1.4 %collective-permute-start.12 = (f32[256,128]{1,0:T(8,128)S(1)}, f32[256,128]{1,0:T(8,128)S(1)}, u32[]{:S(2)}, u32[]{:S(2)}) collective-permute-start(f32[256,128]{1,0:T(8,128)S(1)} %get-tuple-element.37), channel_id=1, source_target_pairs={{0,1},{1,0},{2,3},{3,2},{4,5},{5,4},{6,7},{7,6},{8,9},{9,8},{10,11... | collective-permute-start | bytes 393224 | tf_op jit(solution)/shard_map/ppermute | solution.py:229
  20.5 1.5 %collective-permute-start.9 = (f32[256,128]{1,0:T(8,128)S(1)}, f32[256,128]{1,0:T(8,128)S(1)}, u32[]{:S(2)}, u32[]{:S(2)}) collective-permute-start(f32[256,128]{1,0:T(8,128)S(1)} %get-tuple-element.34), channel_id=1, source_target_pairs={{0,1},{1,0},{2,3},{3,2},{4,5},{5,4},{6,7},{7,6},{8,9},{9,8},{10,11... | collective-permute-start | bytes 393224 | tf_op jit(solution)/shard_map/ppermute | solution.py:229
  21.2 7.7 %collective-permute-start.2 = (f32[280,128]{1,0:T(8,128)S(1)}, f32[280,128]{1,0:T(8,128)S(1)}, u32[]{:S(2)}, u32[]{:S(2)}) collective-permute-start(f32[280,128]{1,0:T(8,128)S(1)} %get-tuple-element.30.refs_2_), channel_id=1, source_target_pairs={{0,8},{1,9},{2,10},{3,11},{4,12},{5,13},{6,14},{7,15},{8,0},{9,1},... | collective-permute-start | bytes 430088 | tf_op jit(solution)/shard_map/ppermute | solution.py:229
  22.5 9.0 %collective-permute-start.13 = (f32[264,128]{1,0:T(8,128)S(1)}, f32[264,128]{1,0:T(8,128)S(1)}, u32[]{:S(2)}, u32[]{:S(2)}) collective-permute-start(f32[264,128]{1,0:T(8,128)S(1)} %shard_map.115.refs_3_), channel_id=1, source_target_pairs={{0,6},{1,7},{2,4},{3,5},{4,2},{5,3},{6,0},{7,1},{8,14},{9,15},{10,... | collective-permute-start | bytes 405512 | tf_op jit(solution)/shard_map/ppermute | solution.py:229
  24.7 7.4 %collective-permute-start.14 = (f32[264,128]{1,0:T(8,128)S(1)}, f32[264,128]{1,0:T(8,128)S(1)}, u32[]{:S(2)}, u32[]{:S(2)}) collective-permute-start(f32[264,128]{1,0:T(8,128)S(1)} %shard_map.115.refs_3_), channel_id=1, source_target_pairs={{0,4},{1,5},{2,6},{3,7},{4,0},{5,1},{6,2},{7,3},{8,12},{9,13},{10,... | collective-permute-start | bytes 405512 | tf_op jit(solution)/shard_map/ppermute | solution.py:229
  25.2 6.9 %collective-permute-start.15 = (f32[264,128]{1,0:T(8,128)S(1)}, f32[264,128]{1,0:T(8,128)S(1)}, u32[]{:S(2)}, u32[]{:S(2)}) collective-permute-start(f32[264,128]{1,0:T(8,128)S(1)} %shard_map.115.refs_3_), channel_id=1, source_target_pairs={{0,2},{1,3},{2,0},{3,1},{4,6},{5,7},{6,4},{7,5},{8,10},{9,11},{10,... | collective-permute-start | bytes 405512 | tf_op jit(solution)/shard_map/ppermute | solution.py:229
  26.1 5.4 %collective-permute-start.1 = (f32[256,128]{1,0:T(8,128)S(1)}, f32[256,128]{1,0:T(8,128)S(1)}, u32[]{:S(2)}, u32[]{:S(2)}) collective-permute-start(f32[256,128]{1,0:T(8,128)S(1)} %shard_map.111), channel_id=1, source_target_pairs={{0,8},{1,9},{2,10},{3,11},{4,12},{5,13},{6,14},{7,15},{8,0},{9,1},... | collective-permute-start | bytes 393224 | tf_op jit(solution)/shard_map/ppermute | solution.py:229
  32.2 2.0 %collective-permute-start.16 = (f32[1024,128]{1,0:T(8,128)S(1)}, f32[1024,128]{1,0:T(8,128)S(1)}, u32[]{:S(2)}, u32[]{:S(2)}) collective-permute-start(f32[1024,128]{1,0:T(8,128)S(1)} %shard_map.116.refs_0_), channel_id=1, source_target_pairs={{0,1},{1,0},{2,3},{3,2},{4,5},{5,4},{6,7},{7,6},{8,9},{9,8},{10,11... | collective-permute-start | bytes 1572872 | tf_op jit(solution)/shard_map/ppermute | solution.py:229
  34.7 4.3 %collective-permute-start.17 = (f32[128,128]{1,0:T(8,128)S(1)}, f32[128,128]{1,0:T(8,128)S(1)}, u32[]{:S(2)}, u32[]{:S(2)}) collective-permute-start(f32[128,128]{1,0:T(8,128)S(1)} %get-tuple-element.41.refs_3_), channel_id=1, source_target_pairs={{0,2},{1,3},{2,0},{3,1},{4,16},{5,17},{6,24},{7,25},{8,10},{9,11},... | collective-permute-start | bytes 196616 | tf_op jit(solution)/shard_map/ppermute | solution.py:229
  35.6 6.9 %collective-permute-start.18 = (f32[128,128]{1,0:T(8,128)S(1)}, f32[128,128]{1,0:T(8,128)S(1)}, u32[]{:S(2)}, u32[]{:S(2)}) collective-permute-start(f32[128,128]{1,0:T(8,128)S(1)} %get-tuple-element.42), channel_id=1, source_target_pairs={{0,1},{1,0},{2,9},{3,8},{4,17},{5,16},{6,25},{7,24},{8,3},{9,2},{1... | collective-permute-start | bytes 196616 | tf_op jit(solution)/shard_map/ppermute | solution.py:229
  35.7 6.9 %collective-permute-start.20 = (f32[128,128]{1,0:T(8,128)S(1)}, f32[128,128]{1,0:T(8,128)S(1)}, u32[]{:S(2)}, u32[]{:S(2)}) collective-permute-start(f32[128,128]{1,0:T(8,128)S(1)} %get-tuple-element.42), channel_id=1, source_target_pairs={{0,1},{1,0},{10,11},{11,10},{20,21},{21,20},{30,31},{31,30}} | collective-permute-start | bytes 196616 | tf_op jit(solution)/shard_map/ppermute | solution.py:229
  39.1 5.4 %collective-permute-start.19 = (f32[128,128]{1,0:T(8,128)S(1)}, f32[128,128]{1,0:T(8,128)S(1)}, u32[]{:S(2)}, u32[]{:S(2)}) collective-permute-start(f32[128,128]{1,0:T(8,128)S(1)} %collective-permute-done.17.refs_0_), channel_id=1, source_target_pairs={{0,8},{1,9},{10,2},{11,3},{20,28},{21,29},{30,22},{31,23}} | collective-permute-start | bytes 196616 | tf_op jit(solution)/shard_map/ppermute | solution.py:229
